TPU v7x, 256 devices: a whole 4x4x8 slice. The times are simulated.
256 devices in a mesh: qrow: 16 (over z, x_lo), kcol: 8 (over x_hi, y), head: 2 (over core).
Axes of the slice: x: 4 (x_hi: 2, x_lo: 2; x = x_hi * 2 + x_lo), y: 4, z: 8, core: 2. Of those that a mesh axis runs over, the one named last changes fastest.
Arguments:
- query: bfloat16 [16384, 1024], P(('qrow', 'kcol'), 'head'), parts along dimension 1, may hold values from -5 to 5, as said below
- key: bfloat16 [16384, 256], P(('kcol', 'qrow'), 'head'), parts along dimension 1, may hold values from -5 to 5, as said below
- value: bfloat16 [16384, 256], P(('kcol', 'qrow'), 'head'), parts along dimension 1, may hold values from -0.5 to 2.5
- dout: bfloat16 [16384, 1024], P(('qrow', 'kcol'), 'head'), parts along dimension 1, may hold values from -6 to 6
- document: int32 [16384], replicated, may hold values from 0 to 7, never falling along the last dimension, each value on 1 to 8192 neighbouring positions
Outputs:
- attended: bfloat16 [16384, 1024], P(('qrow', 'kcol'), 'head'), parts along dimension 1
- grad_query: bfloat16 [16384, 1024], P(('qrow', 'kcol'), 'head'), parts along dimension 1
- grad_key: bfloat16 [16384, 256], P(('kcol', 'qrow'), 'head'), parts along dimension 1
- grad_value: bfloat16 [16384, 256], P(('kcol', 'qrow'), 'head'), parts along dimension 1
There are 2 independent parts, one for each index of `head`. A program takes and returns all parts, laid end to end along the dimension named above; an argument that names none is the same for every part. Nothing has to cross between parts.
Inputs may be any that keep to these rules, and one draw needn't show every extreme that they name: `query`: entries of order one. `key`: entries of order one. Document numbers never fall along the sequence; each document is a run of 1 to 8192 positions, and one has exactly 8192.
All inputs are finite; a program needn't handle non-finite values.
Results may differ from a plain program's by a relative error of at most 0.035.
Values may be sent and summed in bfloat16 or wider, within the bound.
No kernel may reach another device: no remote copies, remote signals or barrier semaphores. Data moves between devices by JAX's collectives and lax.ppermute only.
A program may use at most 128 MiB of HBM per device.

v0:
```python
import functools
import math

import jax
import jax.numpy as jnp
from jax import lax
from jax.experimental import pallas as pl
from jax.experimental.pallas import tpu as pltpu
from jax.sharding import PartitionSpec as P

AXES = ("qrow", "kcol")
DEVICES = 128
CHUNK = 128
SLOTS = 4
TILES = 2
ROWS = SLOTS * CHUNK
PAIR = 2 * CHUNK
PIECES = 4
PLANE = 16 * CHUNK
DOCS = 8
NEG = -1e30
FLOOR = -1e29
LOG2E = math.log2(math.e)
F32 = jnp.float32
BF16 = jnp.bfloat16


def flip(mask):
    return [(d, d ^ mask) for d in range(DEVICES)]


Y = [flip(s) for s in range(SLOTS)]
X = [flip(m) for m in (0, 8, 4, 12)]
NEXT = flip(16)
NEAR = flip(32)
REST = [(d, (d + (32 if d // 32 % 2 else -32)) % DEVICES) for d in range(DEVICES)]


def dot(a, b):
    return lax.dot_general(a, b, (((1,), (0,)), ((), ())), preferred_element_type=F32)


def dot_t(a, b):
    return lax.dot_general(a, b, (((1,), (1,)), ((), ())), preferred_element_type=F32)


def fill(rows, keys, q_s, do_s, k_s, v_s, kt_s, vt_s, group, width):
    for t in range(TILES):
        for s in range(SLOTS):
            ref, to = rows[t * SLOTS + s], pl.ds(s * CHUNK, CHUNK)
            for h in range(group):
                q_s[t, h, to, :] = ref[:, h * width : (h + 1) * width]
                do_s[t, h, to, :] = ref[:, (group + h) * width : (group + h + 1) * width]
    for piece in range(PIECES):
        for m, ref in enumerate(keys):
            part = ref[pl.ds(piece * CHUNK, CHUNK), :]
            block, at = 2 * piece + m // 2, pl.ds(m % 2 * CHUNK, CHUNK)
            k_s[block, at, :] = part[:, :width]
            v_s[block, at, :] = part[:, width:]
            kt_s[block, :, at] = jnp.transpose(part[:, :width])
            vt_s[block, :, at] = jnp.transpose(part[:, width:])


def start_of(sc, row):
    start = 0
    for n in range(DOCS):
        one = sc[4 + n]
        start = jnp.maximum(start, jnp.where(one <= row, one, 0))
    return start


def place(sc, block, t):
    z, x_lo, x_hi, y = (sc[n] for n in range(4))
    base = (4 * (x_hi ^ (block & 1)) + y) * PLANE + sc[4 + DOCS + block // 2] * PAIR
    row = ((z * 4 + x_lo * 2 + x_hi) ^ (4 * t)) * ROWS
    needed = (base <= row + ROWS - 1) & (base + PAIR - 1 >= start_of(sc, row))
    whole = (base + PAIR - 1 <= row) & (base >= start_of(sc, row + ROWS - 1))
    return base, row, needed, whole


def allowed_of(sc, base, row):
    key_at = base + (lax.broadcasted_iota(jnp.int32, (PAIR, 1), 0) ^ (sc[1] * CHUNK))
    row_at = row + (lax.broadcasted_iota(jnp.int32, (1, ROWS), 1) ^ (sc[3] * CHUNK))
    return (key_at >= start_of(sc, row_at)) & (key_at <= row_at)


def pack(query, key, value, dout, rows, keys):
    width = query.shape[1]
    rows[:, :width] = query[...]
    rows[:, width:] = dout[...]
    width = key.shape[1]
    keys[:, :width] = key[...]
    keys[:, width:] = value[...]


def forward(group, width, sc, *refs):
    rows, keys, refs = refs[: TILES * SLOTS], refs[TILES * SLOTS :][:4], refs[TILES * SLOTS + 4 :]
    values, stat, q_s, do_s, k_s, v_s, kt_s, t_s, acc, high, total, mixed = refs
    unit = LOG2E / math.sqrt(width)
    heads = range(group)
    fill(rows, keys, q_s, do_s, k_s, v_s, kt_s, t_s, group, width)
    acc[...] = jnp.zeros_like(acc)
    high[...] = jnp.full_like(high, FLOOR)
    total[...] = jnp.zeros_like(total)
    mixed[...] = jnp.zeros_like(mixed)

    def block(b, t, base, row, masked):
        scores = [dot_t(k_s[b], q_s[t, h]) for h in heads]
        dprobs = [dot_t(v_s[b], do_s[t, h]) for h in heads]
        if masked:
            allowed = allowed_of(sc, base, row)
            scores = [jnp.where(allowed, s, NEG) for s in scores]
        olds = [high[t, h] for h in heads]
        news = [jnp.maximum(o, jnp.max(s, axis=0, keepdims=True)) for o, s in zip(olds, scores)]
        shrinks = [jnp.exp2((o - n) * unit) for o, n in zip(olds, news)]
        es = [jnp.exp2(s * unit - n * unit) for s, n in zip(scores, news)]
        totals = [total[t, h] * shrinks[h] + jnp.sum(es[h], axis=0, keepdims=True) for h in heads]
        mixeds = [
            mixed[t, h] * shrinks[h] + jnp.sum(es[h] * dprobs[h], axis=0, keepdims=True)
            for h in heads
        ]
        accs = [acc[t, h] * shrinks[h] + dot(t_s[b], es[h].astype(BF16)) for h in heads]
        for h in heads:
            high[t, h] = news[h]
            total[t, h] = totals[h]
            mixed[t, h] = mixeds[h]
            acc[t, h] = accs[h]

    def step(n, carry):
        b, t = n // 2, n & 1
        base, row, needed, whole = place(sc, b, t)

        @pl.when(needed & whole)
        def _():
            block(b, t, base, row, False)

        @pl.when(needed & jnp.logical_not(whole))
        def _():
            block(b, t, base, row, True)

        return carry

    lax.fori_loop(0, 4 * PIECES, step, 0)
    for t in range(TILES):
        for h in heads:
            values[t, h] = (acc[t, h] * (1.0 / jnp.maximum(total[t, h], 1e-30))).astype(BF16)
            stat[t, h : h + 1, :] = high[t, h]
            stat[t, group + h : group + h + 1, :] = total[t, h]
            stat[t, 2 * group + h : 2 * group + h + 1, :] = mixed[t, h]


def backward(group, width, span, begins, ends, sc, q_s, do_s, k_s, v_s, t_s, *refs):
    scale = 1.0 / math.sqrt(width)
    unit = LOG2E * scale
    heads = range(group)
    if begins:
        stats, own, values, refs = refs[:SLOTS], refs[SLOTS], refs[SLOTS + 1], refs[SLOTS + 2 :]
    else:
        acc_in, lse_in, delta_in, refs = *refs[:3], refs[3:]
    dkv, refs = refs[0], refs[1:]
    if begins:
        mixed, refs = refs[:SLOTS], refs[SLOTS:]
    if ends:
        dq, refs = refs[:SLOTS], refs[SLOTS:]
    acc, lse, delta, grads = refs
    if begins:
        acc[...] = jnp.zeros_like(acc)
        for t in range(TILES):
            for u in range(SLOTS):
                at = pl.ds(u * CHUNK, CHUNK)
                parts = [stats[s][t, :, pl.ds((u ^ s) * CHUNK, CHUNK)] for s in range(SLOTS)]
                top = functools.reduce(jnp.maximum, [p[:group] for p in parts])
                weights = [jnp.exp2((p[:group] - top) * unit) for p in parts]
                total = sum(w * p[group : 2 * group] for w, p in zip(weights, parts))
                product = sum(w * p[2 * group :] for w, p in zip(weights, parts))
                low, small = top * unit + jnp.log2(total), product / total
                part = own[t, group : 2 * group, at] * jnp.exp2(own[t, :group, at] * unit - low)
                for h in heads:
                    lse[t, h, :, at] = low[h : h + 1]
                    delta[t, h, :, at] = small[h : h + 1]
                    mixed[u][t, h * width : (h + 1) * width, :] = (
                        values[t, h, :, at].astype(F32) * part[h : h + 1]
                    ).astype(BF16)
    else:
        acc[...] = acc_in[...]
        lse[...] = lse_in[...]
        delta[...] = delta_in[...]

    def block(b, t, base, row, masked):
        scores = [dot_t(k_s[b], q_s[t, h]) for h in heads]
        dprobs = [dot_t(v_s[b], do_s[t, h]) for h in heads]
        if masked:
            allowed = allowed_of(sc, base, row)
            scores = [jnp.where(allowed, s, NEG) for s in scores]
        probs = [jnp.exp2(scores[h] * unit - lse[t, h]) for h in heads]
        dscores = [(probs[h] * (dprobs[h] - delta[t, h])).astype(BF16) for h in heads]
        lows = [p.astype(BF16) for p in probs]
        dk = sum(dot(dscores[h], q_s[t, h]) for h in heads)
        dv = sum(dot(lows[h], do_s[t, h]) for h in heads)
        accs = [acc[t, h] + dot(t_s[b], dscores[h]) for h in heads]
        for h in heads:
            acc[t, h] = accs[h]
        grads[:, :width] = grads[:, :width] + dk * scale
        grads[:, width:] = grads[:, width:] + dv

    def step(b, carry):
        grads[...] = jnp.zeros_like(grads)

        def tile(t, carry):
            base, row, needed, whole = place(sc, b, t)

            @pl.when(needed & whole)
            def _():
                block(b, t, base, row, False)

            @pl.when(needed & jnp.logical_not(whole))
            def _():
                block(b, t, base, row, True)

            return carry

        lax.fori_loop(0, TILES, tile, 0)
        dkv[b - 2 * span[0]] = grads[...].astype(BF16)
        return carry

    lax.fori_loop(2 * span[0], 2 * span[1], step, 0)
    if ends:
        for t in range(TILES):
            for h in heads:
                value = (acc[t, h] * scale).astype(BF16)
                for s in range(SLOTS):
                    dq[s][t, h * width : (h + 1) * width, :] = value[
                        :, s * CHUNK : (s + 1) * CHUNK
                    ]


def combine(group, width, *refs):
    for one, two, out in zip(refs[:2], refs[2:4], refs[4:]):
        for h in range(group):
            at = pl.ds(h * width, width)
            whole = one[at, :].astype(F32) + two[at, :].astype(F32)
            out[:, at] = jnp.transpose(whole).astype(BF16)


SMEM = pl.BlockSpec(memory_space=pltpu.SMEM)
VMEM = pl.BlockSpec(memory_space=pltpu.VMEM)
PARAMS = pltpu.CompilerParams(vmem_limit_bytes=20 * 1024 * 1024)


def cost(group, width, dots, pieces):
    work = TILES * ROWS * group * pieces * 2 * PAIR * width * 2
    return pl.CostEstimate(flops=2 * dots * work, bytes_accessed=1 << 23, transcendentals=0)


def state_shapes(group, width):
    acc = jax.ShapeDtypeStruct((TILES, group, width, ROWS), F32)
    line = jax.ShapeDtypeStruct((TILES, group, 1, ROWS), F32)
    return [acc, line, line]


def run_forward(group, width, sc, rows, keys):
    acc, line, _ = state_shapes(group, width)
    row = jax.ShapeDtypeStruct((TILES, group, ROWS, width), BF16)
    key = jax.ShapeDtypeStruct((2 * PIECES, PAIR, width), BF16)
    turned = jax.ShapeDtypeStruct((2 * PIECES, width, PAIR), BF16)
    stat = jax.ShapeDtypeStruct((TILES, 3 * group, ROWS), F32)
    return pl.pallas_call(
        functools.partial(forward, group, width),
        out_shape=[jax.ShapeDtypeStruct(acc.shape, BF16), stat, row, row, key, key, turned],
        in_specs=[SMEM] + [VMEM] * (TILES * SLOTS + 4),
        out_specs=[VMEM] * 7,
        scratch_shapes=[pltpu.VMEM(turned.shape, BF16), pltpu.VMEM(acc.shape, F32)]
        + [pltpu.VMEM(line.shape, F32)] * 3,
        compiler_params=PARAMS,
        cost_estimate=cost(group, width, 3, PIECES),
        name="forward",
    )(sc, *rows, *keys)


def run_backward(group, width, span, begins, ends, sc, held, *more):
    pieces = span[1] - span[0]
    carried = state_shapes(group, width)
    piece = jax.ShapeDtypeStruct((TILES, group * width, CHUNK), BF16)
    shapes = [jax.ShapeDtypeStruct((2 * pieces, PAIR, 2 * width), BF16)]
    shapes = shapes + [piece] * (SLOTS * (begins + ends))
    spaces = [pltpu.VMEM((PAIR, 2 * width), F32)]
    if not ends:
        shapes = shapes + carried
    else:
        spaces = [pltpu.VMEM(s.shape, F32) for s in carried] + spaces
    return pl.pallas_call(
        functools.partial(backward, group, width, span, begins, ends),
        out_shape=shapes,
        in_specs=[SMEM] + [VMEM] * (len(held) + len(more)),
        out_specs=[VMEM] * len(shapes),
        scratch_shapes=spaces,
        compiler_params=PARAMS,
        cost_estimate=cost(group, width, 5, pieces),
        name="backward_begin" if begins else "backward_end" if ends else "backward_middle",
    )(sc, *held, *more)


def add(*parts):
    return sum(part.astype(F32) for part in parts).astype(BF16)


def local(query, key, value, dout, document):
    width = key.shape[1]
    group = query.shape[1] // width
    send = functools.partial(lax.ppermute, axis_name=AXES)
    qrow, kcol = lax.axis_index("qrow"), lax.axis_index("kcol")
    z, x_lo, x_hi, y = qrow // 2, qrow % 2, kcol // 4, kcol % 4

    row_home, key_home = pl.pallas_call(
        pack,
        out_shape=[
            jax.ShapeDtypeStruct((CHUNK, 2 * group * width), BF16),
            jax.ShapeDtypeStruct((CHUNK, 2 * width), BF16),
        ],
        name="pack",
    )(query, key, value, dout)
    row_other = send(row_home, perm=NEXT)
    near, last = send(row_home, perm=Y[1]), send(row_home, perm=Y[3])
    a, b = send(key_home, perm=NEAR), send(key_home, perm=REST)
    row_other, near, last, a, b = lax.optimization_barrier((row_other, near, last, a, b))
    near_other, last_other = send(row_other, perm=Y[1]), send(row_other, perm=Y[3])
    held = jnp.concatenate([key_home, a, b, send(b, perm=NEAR)], axis=0)
    keys = [held] + [send(held, perm=X[n]) for n in range(1, 4)]
    far, far_other = send(last, perm=Y[1]), send(near_other, perm=Y[3])
    rows = [row_home, near, far, last, row_other, near_other, far_other, last_other]

    numbers = jnp.arange(DOCS, dtype=jnp.int32)
    starts = jnp.sum((document[None, :] < numbers[:, None]).astype(jnp.int32), axis=1)
    side = 2 - 4 * (z // 2 % 2)
    sources = jnp.stack([z, z + side, z - side, z + 4]) & 7
    sc = jnp.concatenate([jnp.stack([z, x_lo, x_hi, y]), starts, sources]).astype(jnp.int32)

    values, stat, *held = run_forward(group, width, sc, rows, keys)
    unit = LOG2E / math.sqrt(width)
    other = send(stat, perm=NEXT)[::-1]
    top = jnp.maximum(stat[:, :group], other[:, :group])
    mine, theirs = (jnp.exp2((s[:, :group] - top) * unit) for s in (stat, other))
    merged = jnp.concatenate(
        [top]
        + [
            stat[:, n * group : (n + 1) * group] * mine
            + other[:, n * group : (n + 1) * group] * theirs
            for n in (1, 2)
        ],
        axis=1,
    )
    stats = [merged] + [send(merged, perm=Y[s]) for s in range(1, SLOTS)]

    back = functools.partial(run_backward, group, width)
    out = back((3, 4), True, False, sc, held, *stats, stat, values)
    far, mixed, carried = out[0], out[1 : 1 + SLOTS], out[1 + SLOTS :]
    one, two = send(far[0], perm=NEAR), send(far[1], perm=REST)
    mixed = add(mixed[0], *[send(mixed[s], perm=Y[s]) for s in range(1, SLOTS)])
    near_by, *carried = back((1, 3), False, False, sc, held, *carried)
    ga = jnp.concatenate([near_by[0], add(near_by[1], two)], axis=0)
    gb = jnp.concatenate([add(near_by[2], one), near_by[3]], axis=0)
    ga, gb, mixed, carried = lax.optimization_barrier((ga, gb, mixed, carried))
    ga, gb = send(ga, perm=NEAR), send(gb, perm=REST)
    close, *dq = back((0, 1), False, True, sc, held, *carried)
    dq = [dq[0]] + [send(dq[s], perm=Y[s]) for s in range(1, SLOTS)]
    grad = add(close.reshape(2 * PAIR, 2 * width), ga, gb)
    _, mixed, dq = lax.optimization_barrier((grad, mixed, dq))
    mixed = [mixed[0], send(mixed[1], perm=NEXT)]
    grad = grad.reshape(4, CHUNK, 2 * width)
    grad = add(grad[0], *[send(grad[n], perm=X[n]) for n in range(1, 4)])
    dq = add(*dq)
    dq = [dq[0], send(dq[1], perm=NEXT)]
    out_shape = jax.ShapeDtypeStruct((CHUNK, group * width), BF16)
    attended, grad_query = pl.pallas_call(
        functools.partial(combine, group, width),
        out_shape=[out_shape, out_shape],
        in_specs=[VMEM] * 4,
        out_specs=[VMEM] * 2,
        compiler_params=PARAMS,
        name="combine",
    )(mixed[0], dq[0], mixed[1], dq[1])
    return attended, grad_query, grad[:, :width], grad[:, width:]


def solution(mesh):
    by_row = P(("qrow", "kcol"), "head")
    by_key = P(("kcol", "qrow"), "head")
    return jax.shard_map(
        local,
        mesh=mesh,
        in_specs=(by_row, by_key, by_key, by_row, P()),
        out_specs=(by_row, by_row, by_key, by_key),
        check_vma=False,
    )
```

profile of v0, /device:TPU:128, one launch (start us, length us, event | category | flops | bytes accessed | tf_op | source)
XLA Modules:
  0.0 118.4 jit_solution(9019604188007468923)
XLA Ops:
  2.4 3.0 %collective-permute-start.2 = (bf16[128,1024]{1,0:T(8,128)(2,1)}, bf16[128,1024]{1,0:T(8,128)(2,1)S(1)}, u32[]{:S(2)}, u32[]{:S(2)}) collective-permute-start(bf16[128,1024]{1,0:T(8,128)(2,1)} %get-tuple-element.48.refs_0_), channel_id=1, source_target_pairs={{0,6},{2,4},{4,2},{6,0},{8,14},{10,12},{12,10},{14,8},{16,22},{18,... | collective-permute-start | bytes 786440 | tf_op jit(solution)/shard_map/ppermute | solution.py:323
  8.9 6.7 %collective-permute-done.4 = bf16[128,256]{1,0:T(8,128)(2,1)S(1)} collective-permute-done((bf16[128,256]{1,0:T(8,128)(2,1)}, bf16[128,256]{1,0:T(8,128)(2,1)S(1)}, u32[]{:S(2)}, u32[]{:S(2)}) %collective-permute-start.4) | collective-permute-done | bytes 65568 | tf_op jit(solution)/shard_map/ppermute | solution.py:324
  17.5 2.5 %collective-permute-start.9 = (bf16[128,256]{1,0:T(8,128)(2,1)S(1)}, bf16[128,256]{1,0:T(8,128)(2,1)S(1)}, u32[]{:S(2)}, u32[]{:S(2)}) collective-permute-start(bf16[128,256]{1,0:T(8,128)(2,1)S(1)} %collective-permute-done.4), channel_id=1, source_target_pairs={{0,64},{2,66},{4,68},{6,70},{8,72},{10,74},{12,76},{14,78},{16,80}... | collective-permute-start | bytes 196616 | tf_op jit(solution)/shard_map/ppermute | solution.py:327
  22.7 2.8 %collective-permute-start.12 = (bf16[512,256]{1,0:T(8,128)(2,1)S(1)}, bf16[512,256]{1,0:T(8,128)(2,1)S(1)}, u32[]{:S(2)}, u32[]{:S(2)}) collective-permute-start(bf16[512,256]{1,0:T(8,128)(2,1)S(1)} %constant_dynamic-update-slice_fusion.refs_8_), channel_id=1, source_target_pairs={{0,24},{2,26},{4,28},{6,30},{8,16},{10,18},{12,20},{14,22},{16,8},... | collective-permute-start | bytes 786440 | tf_op jit(solution)/shard_map/ppermute | solution.py:328
  26.3 2.3 %collective-permute-done.5.refs_2_ = bf16[128,1024]{1,0:T(8,128)(2,1)S(1)} collective-permute-done((bf16[128,1024]{1,0:T(8,128)(2,1)S(1)}, bf16[128,1024]{1,0:T(8,128)(2,1)S(1)}, u32[]{:S(2)}, u32[]{:S(2)}) %collective-permute-start.5) | collective-permute-done | bytes 262176 | tf_op jit(solution)/shard_map/ppermute | solution.py:329
  30.1 2.3 %collective-permute-start.7 = (bf16[128,1024]{1,0:T(8,128)(2,1)S(1)}, bf16[128,1024]{1,0:T(8,128)(2,1)S(1)}, u32[]{:S(2)}, u32[]{:S(2)}) collective-permute-start(bf16[128,1024]{1,0:T(8,128)(2,1)S(1)} %collective-permute-done.6.refs_5_), channel_id=1, source_target_pairs={{0,6},{2,4},{4,2},{6,0},{8,14},{10,12},{12,10},{14,8},{16,22},{18,... | collective-permute-start | bytes 786440 | tf_op jit(solution)/shard_map/ppermute | solution.py:329
  33.6 2.5 %collective-permute-done.11.refs_10_ = bf16[512,256]{1,0:T(8,128)(2,1)S(1)} collective-permute-done((bf16[512,256]{1,0:T(8,128)(2,1)S(1)}, bf16[512,256]{1,0:T(8,128)(2,1)S(1)}, u32[]{:S(2)}, u32[]{:S(2)}) %collective-permute-start.11) | collective-permute-done | bytes 262176 | tf_op jit(solution)/shard_map/ppermute | solution.py:328
  38.6 8.9 %forward.1 = (bf16[2,4,128,512]{3,2,1,0:T(8,128)(2,1)S(1)}, f32[2,12,512]{2,1,0:T(8,128)S(1)}, bf16[2,4,512,128]{3,2,1,0:T(8,128)(2,1)S(1)}, bf16[2,4,512,128]{3...) custom-call(s32[16]{0:T(128)S(1)} %concatenate.15.sc, ...), custom_call_target="tpu_custom_call" | custom-call | flops 12884901888 | bytes 8388608 | tf_op jit(solution)/shard_map/forward/pallas_call | solution.py:267
  49.4 2.5 %collective-permute-done.13 = f32[2,12,512]{2,1,0:T(8,128)S(1)} collective-permute-done((f32[2,12,512]{2,1,0:T(8,128)S(1)}, f32[2,12,512]{2,1,0:T(8,128)S(1)}, u32[]{:S(2)}, u32[]{:S(2)}) %collective-permute-start.13) | collective-permute-done | bytes 49184 | tf_op jit(solution)/shard_map/ppermute | solution.py:340
  52.0 6.3 %collective-permute-start.16 = (f32[2,12,512]{2,1,0:T(8,128)S(1)}, f32[2,12,512]{2,1,0:T(8,128)S(1)}, u32[]{:S(2)}, u32[]{:S(2)}) collective-permute-start(f32[2,12,512]{2,1,0:T(8,128)S(1)} %pad_maximum_fusion.2.refs_0_), channel_id=1, source_target_pairs={{0,6},{2,4},{4,2},{6,0},{8,14},{10,12},{12,10},{14,8},{16,22},{18,... | collective-permute-start | bytes 147464 | tf_op jit(solution)/shard_map/ppermute | solution.py:352
  60.8 3.3 %collective-permute-done.15.refs_2_ = f32[2,12,512]{2,1,0:T(8,128)S(1)} collective-permute-done((f32[2,12,512]{2,1,0:T(8,128)S(1)}, f32[2,12,512]{2,1,0:T(8,128)S(1)}, u32[]{:S(2)}, u32[]{:S(2)}) %collective-permute-start.15) | collective-permute-done | bytes 49184 | tf_op jit(solution)/shard_map/ppermute | solution.py:352
  64.0 4.3 %backward_begin.1 = (bf16[2,256,256]{2,1,0:T(8,128)(2,1)S(1)}, bf16[2,512,128]{2,1,0:T(8,128)(2,1)S(1)}, bf16[2,512,128]{2,1,0:T(8,128)(2,1)S(1)}, bf16[2,512,12...) custom-call(s32[16]{0:T(128)S(1)} %concatenate.15.sc, ...), custom_call_target="tpu_custom_call" | custom-call | flops 5368709120 | bytes 8388608 | tf_op jit(solution)/shard_map/backward_begin/pallas_call | solution.py:291
  68.7 2.6 %collective-permute-start.20 = (bf16[2,512,128]{2,1,0:T(8,128)(2,1)S(1)}, bf16[2,512,128]{2,1,0:T(8,128)(2,1)S(1)}, u32[]{:S(2)}, u32[]{:S(2)}) collective-permute-start(bf16[2,512,128]{2,1,0:T(8,128)(2,1)S(1)} %get-tuple-element.69), channel_id=1, source_target_pairs={{0,4},{2,6},{4,0},{6,2},{8,12},{10,14},{12,8},{14,10},{16,20},{18,... | collective-permute-start | bytes 786440 | tf_op jit(solution)/shard_map/ppermute | solution.py:358
  71.2 2.1 %collective-permute-start.21 = (bf16[2,512,128]{2,1,0:T(8,128)(2,1)S(1)}, bf16[2,512,128]{2,1,0:T(8,128)(2,1)S(1)}, u32[]{:S(2)}, u32[]{:S(2)}) collective-permute-start(bf16[2,512,128]{2,1,0:T(8,128)(2,1)S(1)} %get-tuple-element.70), channel_id=1, source_target_pairs={{0,6},{2,4},{4,2},{6,0},{8,14},{10,12},{12,10},{14,8},{16,22},{18,... | collective-permute-start | bytes 786440 | tf_op jit(solution)/shard_map/ppermute | solution.py:358
  73.4 4.2 %backward_middle.1 = (bf16[4,256,256]{2,1,0:T(8,128)(2,1)S(1)}, f32[2,4,128,512]{3,2,1,0:T(8,128)S(1)}, f32[2,4,1,512]{3,2,1,0:T(1,128)S(1)}, f32[2,4,1,512]{3,2,1,0:T(1,128)S(1)}) custom-call(s32[16]{0:T(128)S(1)} %concatenate.15.sc, bf16[2,4,512,128]{3,2,1,0:T(8,128)(2,1)S(1)} %get-tuple-element.55.q_s, ...), custom_call_target="tpu_custom_call" | custom-call | flops 10737418240 | bytes 8388608 | tf_op jit(solution)/shard_map/backward_middle/pallas_call | solution.py:291
  78.5 2.7 %collective-permute-done.21 = bf16[2,512,128]{2,1,0:T(8,128)(2,1)S(1)} collective-permute-done((bf16[2,512,128]{2,1,0:T(8,128)(2,1)S(1)}, bf16[2,512,128]{2,1,0:T(8,128)(2,1)S(1)}, u32[]{:S(2)}, u32[]{:S(2)}) %collective-permute-start.21) | collective-permute-done | bytes 262176 | tf_op jit(solution)/shard_map/ppermute | solution.py:358
  81.4 2.8 %collective-permute-start.22 = (bf16[512,256]{1,0:T(8,128)(2,1)S(1)}, bf16[512,256]{1,0:T(8,128)(2,1)S(1)}, u32[]{:S(2)}, u32[]{:S(2)}) collective-permute-start(bf16[512,256]{1,0:T(8,128)(2,1)S(1)} %get-tuple-element.78), channel_id=1, source_target_pairs={{0,64},{2,66},{4,68},{6,70},{8,72},{10,74},{12,76},{14,78},{16,80}... | collective-permute-start | bytes 786440 | tf_op jit(solution)/shard_map/ppermute | solution.py:363
  84.2 4.1 %collective-permute-start.23 = (bf16[512,256]{1,0:T(8,128)(2,1)S(1)}, bf16[512,256]{1,0:T(8,128)(2,1)S(1)}, u32[]{:S(2)}, u32[]{:S(2)}) collective-permute-start(bf16[512,256]{1,0:T(8,128)(2,1)S(1)} %get-tuple-element.79), channel_id=1, source_target_pairs={{0,192},{2,194},{4,196},{6,198},{8,200},{10,202},{12,204},{14,206}... | collective-permute-start | bytes 786440 | tf_op jit(solution)/shard_map/ppermute | solution.py:363
  88.3 2.6 %backward_end.1 = (bf16[2,256,256]{2,1,0:T(8,128)(2,1)S(1)}, bf16[2,512,128]{2,1,0:T(8,128)(2,1)S(1)}, bf16[2,512,128]{2,1,0:T(8,128)(2,1)S(1)}, bf16[2,512,128]...) custom-call(s32[16]{0:T(128)S(1)} %concatenate.15.sc, bf16[2,4,512,128]{3,2,1,0:T(8,128)(2,1)S(1)} %get-tuple-element.55.q_s, ...), custom_call_target="tpu_custom_call" | custom-call | flops 5368709120 | bytes 8388608 | tf_op jit(solution)/shard_map/backward_end/pallas_call | solution.py:291
  91.0 5.0 %collective-permute-start.25 = (bf16[2,512,128]{2,1,0:T(8,128)(2,1)S(1)}, bf16[2,512,128]{2,1,0:T(8,128)(2,1)S(1)}, u32[]{:S(2)}, u32[]{:S(2)}) collective-permute-start(bf16[2,512,128]{2,1,0:T(8,128)(2,1)S(1)} %get-tuple-element.83), channel_id=1, source_target_pairs={{0,4},{2,6},{4,0},{6,2},{8,12},{10,14},{12,8},{14,10},{16,20},{18,... | collective-permute-start | bytes 786440 | tf_op jit(solution)/shard_map/ppermute | solution.py:365
  97.3 5.9 %collective-permute-done.25 = bf16[2,512,128]{2,1,0:T(8,128)(2,1)S(1)} collective-permute-done((bf16[2,512,128]{2,1,0:T(8,128)(2,1)S(1)}, bf16[2,512,128]{2,1,0:T(8,128)(2,1)S(1)}, u32[]{:S(2)}, u32[]{:S(2)}) %collective-permute-start.25) | collective-permute-done | bytes 262176 | tf_op jit(solution)/shard_map/ppermute | solution.py:365
  103.3 2.7 %collective-permute-done.26 = bf16[2,512,128]{2,1,0:T(8,128)(2,1)S(1)} collective-permute-done((bf16[2,512,128]{2,1,0:T(8,128)(2,1)S(1)}, bf16[2,512,128]{2,1,0:T(8,128)(2,1)S(1)}, u32[]{:S(2)}, u32[]{:S(2)}) %collective-permute-start.26) | collective-permute-done | bytes 262176 | tf_op jit(solution)/shard_map/ppermute | solution.py:365
  108.4 2.8 %collective-permute-start.31 = (bf16[128,256]{1,0:T(8,128)(2,1)S(1)}, bf16[128,256]{1,0:T(8,128)(2,1)S(1)}, u32[]{:S(2)}, u32[]{:S(2)}) collective-permute-start(bf16[128,256]{1,0:T(8,128)(2,1)S(1)} %get-tuple-element.97), channel_id=1, source_target_pairs={{0,24},{2,26},{4,28},{6,30},{8,16},{10,18},{12,20},{14,22},{16,8},... | collective-permute-start | bytes 196616 | tf_op jit(solution)/shard_map/ppermute | solution.py:370
  113.9 3.1 %collective-permute-done.30 = bf16[128,256]{1,0:T(8,128)(2,1)S(1)} collective-permute-done((bf16[128,256]{1,0:T(8,128)(2,1)S(1)}, bf16[128,256]{1,0:T(8,128)(2,1)S(1)}, u32[]{:S(2)}, u32[]{:S(2)}) %collective-permute-start.30) | collective-permute-done | bytes 65568 | tf_op jit(solution)/shard_map/ppermute | solution.py:370
  (70 shorter events, 29.7 us)
Async XLA Ops:
  2.4 13.2 %collective-permute-start.2 = (bf16[128,1024]{1,0:T(8,128)(2,1)}, bf16[128,1024]{1,0:T(8,128)(2,1)S(1)}, u32[]{:S(2)}, u32[]{:S(2)}) collective-permute-start(bf16[128,1024]{1,0:T(8,128)(2,1)} %get-tuple-element.48.refs_0_), channel_id=1, source_target_pairs={{0,6},{2,4},{4,2},{6,0},{8,14},{10,12},{12,10},{14,8},{16,22},{18,... | collective-permute-start | bytes 786440 | tf_op jit(solution)/shard_map/ppermute | solution.py:323
  5.4 10.2 %collective-permute-start.1 = (bf16[128,1024]{1,0:T(8,128)(2,1)}, bf16[128,1024]{1,0:T(8,128)(2,1)S(1)}, u32[]{:S(2)}, u32[]{:S(2)}) collective-permute-start(bf16[128,1024]{1,0:T(8,128)(2,1)} %get-tuple-element.48.refs_0_), channel_id=1, source_target_pairs={{0,2},{2,0},{4,6},{6,4},{8,10},{10,8},{12,14},{14,12},{16,18},{18,... | collective-permute-start | bytes 786440 | tf_op jit(solution)/shard_map/ppermute | solution.py:323
  5.5 10.1 %collective-permute-start = (bf16[128,1024]{1,0:T(8,128)(2,1)}, bf16[128,1024]{1,0:T(8,128)(2,1)S(1)}, u32[]{:S(2)}, u32[]{:S(2)}) collective-permute-start(bf16[128,1024]{1,0:T(8,128)(2,1)} %get-tuple-element.48.refs_0_), channel_id=1, source_target_pairs={{0,32},{2,34},{4,36},{6,38},{8,40},{10,42},{12,44},{14,46},{16,48}... | collective-permute-start | bytes 786440 | tf_op jit(solution)/shard_map/ppermute | solution.py:322
  6.6 9.0 %collective-permute-start.4 = (bf16[128,256]{1,0:T(8,128)(2,1)}, bf16[128,256]{1,0:T(8,128)(2,1)S(1)}, u32[]{:S(2)}, u32[]{:S(2)}) collective-permute-start(bf16[128,256]{1,0:T(8,128)(2,1)} %get-tuple-element.49), channel_id=1, source_target_pairs={{0,192},{2,194},{4,196},{6,198},{8,200},{10,202},{12,204},{14,206}... | collective-permute-start | bytes 196616 | tf_op jit(solution)/shard_map/ppermute | solution.py:324
  7.1 8.5 %collective-permute-start.3 = (bf16[128,256]{1,0:T(8,128)(2,1)}, bf16[128,256]{1,0:T(8,128)(2,1)S(1)}, u32[]{:S(2)}, u32[]{:S(2)}) collective-permute-start(bf16[128,256]{1,0:T(8,128)(2,1)} %get-tuple-element.49), channel_id=1, source_target_pairs={{0,64},{2,66},{4,68},{6,70},{8,72},{10,74},{12,76},{14,78},{16,80}... | collective-permute-start | bytes 196616 | tf_op jit(solution)/shard_map/ppermute | solution.py:324
  15.6 18.0 %collective-permute-start.8 = (bf16[128,1024]{1,0:T(8,128)(2,1)S(1)}, bf16[128,1024]{1,0:T(8,128)(2,1)S(1)}, u32[]{:S(2)}, u32[]{:S(2)}) collective-permute-start(bf16[128,1024]{1,0:T(8,128)(2,1)S(1)} %collective-permute-done.refs_4_), channel_id=1, source_target_pairs={{0,6},{2,4},{4,2},{6,0},{8,14},{10,12},{12,10},{14,8},{16,22},{18,... | collective-permute-start | bytes 786440 | tf_op jit(solution)/shard_map/ppermute | solution.py:326
  16.6 13.5 %collective-permute-start.6 = (bf16[128,1024]{1,0:T(8,128)(2,1)S(1)}, bf16[128,1024]{1,0:T(8,128)(2,1)S(1)}, u32[]{:S(2)}, u32[]{:S(2)}) collective-permute-start(bf16[128,1024]{1,0:T(8,128)(2,1)S(1)} %collective-permute-done.refs_4_), channel_id=1, source_target_pairs={{0,2},{2,0},{4,6},{6,4},{8,10},{10,8},{12,14},{14,12},{16,18},{18,... | collective-permute-start | bytes 786440 | tf_op jit(solution)/shard_map/ppermute | solution.py:326
  20.1 8.5 %collective-permute-start.5 = (bf16[128,1024]{1,0:T(8,128)(2,1)S(1)}, bf16[128,1024]{1,0:T(8,128)(2,1)S(1)}, u32[]{:S(2)}, u32[]{:S(2)}) collective-permute-start(bf16[128,1024]{1,0:T(8,128)(2,1)S(1)} %collective-permute-done.2.refs_3_), channel_id=1, source_target_pairs={{0,2},{2,0},{4,6},{6,4},{8,10},{10,8},{12,14},{14,12},{16,18},{18,... | collective-permute-start | bytes 786440 | tf_op jit(solution)/shard_map/ppermute | solution.py:329
  22.7 10.9 %collective-permute-start.12 = (bf16[512,256]{1,0:T(8,128)(2,1)S(1)}, bf16[512,256]{1,0:T(8,128)(2,1)S(1)}, u32[]{:S(2)}, u32[]{:S(2)}) collective-permute-start(bf16[512,256]{1,0:T(8,128)(2,1)S(1)} %constant_dynamic-update-slice_fusion.refs_8_), channel_id=1, source_target_pairs={{0,24},{2,26},{4,28},{6,30},{8,16},{10,18},{12,20},{14,22},{16,8},... | collective-permute-start | bytes 786440 | tf_op jit(solution)/shard_map/ppermute | solution.py:328
  25.5 10.6 %collective-permute-start.11 = (bf16[512,256]{1,0:T(8,128)(2,1)S(1)}, bf16[512,256]{1,0:T(8,128)(2,1)S(1)}, u32[]{:S(2)}, u32[]{:S(2)}) collective-permute-start(bf16[512,256]{1,0:T(8,128)(2,1)S(1)} %constant_dynamic-update-slice_fusion.refs_8_), channel_id=1, source_target_pairs={{0,8},{2,10},{4,12},{6,14},{8,0},{10,2},{12,4},{14,6},{16,24},{18,... | collective-permute-start | bytes 786440 | tf_op jit(solution)/shard_map/ppermute | solution.py:328
  28.6 8.2 %collective-permute-start.10 = (bf16[512,256]{1,0:T(8,128)(2,1)S(1)}, bf16[512,256]{1,0:T(8,128)(2,1)S(1)}, u32[]{:S(2)}, u32[]{:S(2)}) collective-permute-start(bf16[512,256]{1,0:T(8,128)(2,1)S(1)} %constant_dynamic-update-slice_fusion.refs_8_), channel_id=1, source_target_pairs={{0,16},{2,18},{4,20},{6,22},{8,24},{10,26},{12,28},{14,30},{16,0},... | collective-permute-start | bytes 786440 | tf_op jit(solution)/shard_map/ppermute | solution.py:328
  30.1 7.6 %collective-permute-start.7 = (bf16[128,1024]{1,0:T(8,128)(2,1)S(1)}, bf16[128,1024]{1,0:T(8,128)(2,1)S(1)}, u32[]{:S(2)}, u32[]{:S(2)}) collective-permute-start(bf16[128,1024]{1,0:T(8,128)(2,1)S(1)} %collective-permute-done.6.refs_5_), channel_id=1, source_target_pairs={{0,6},{2,4},{4,2},{6,0},{8,14},{10,12},{12,10},{14,8},{16,22},{18,... | collective-permute-start | bytes 786440 | tf_op jit(solution)/shard_map/ppermute | solution.py:329
  52.0 8.8 %collective-permute-start.16 = (f32[2,12,512]{2,1,0:T(8,128)S(1)}, f32[2,12,512]{2,1,0:T(8,128)S(1)}, u32[]{:S(2)}, u32[]{:S(2)}) collective-permute-start(f32[2,12,512]{2,1,0:T(8,128)S(1)} %pad_maximum_fusion.2.refs_0_), channel_id=1, source_target_pairs={{0,6},{2,4},{4,2},{6,0},{8,14},{10,12},{12,10},{14,8},{16,22},{18,... | collective-permute-start | bytes 147464 | tf_op jit(solution)/shard_map/ppermute | solution.py:352
  68.4 9.2 %collective-permute-start.18 = (bf16[256,256]{1,0:T(8,128)(2,1)S(1)}, bf16[256,256]{1,0:T(8,128)(2,1)S(1)}, u32[]{:S(2)}, u32[]{:S(2)}) collective-permute-start(bf16[256,256]{1,0:T(8,128)(2,1)S(1)} %get-tuple-element.103), channel_id=1, source_target_pairs={{0,64},{2,66},{4,68},{6,70},{8,72},{10,74},{12,76},{14,78},{16,80}... | collective-permute-start | bytes 393224 | tf_op jit(solution)/shard_map/ppermute | solution.py:357
  68.5 9.1 %collective-permute-start.17 = (bf16[256,256]{1,0:T(8,128)(2,1)S(1)}, bf16[256,256]{1,0:T(8,128)(2,1)S(1)}, u32[]{:S(2)}, u32[]{:S(2)}) collective-permute-start(bf16[256,256]{1,0:T(8,128)(2,1)S(1)} %get-tuple-element.104), channel_id=1, source_target_pairs={{0,192},{2,194},{4,196},{6,198},{8,200},{10,202},{12,204},{14,206}... | collective-permute-start | bytes 393224 | tf_op jit(solution)/shard_map/ppermute | solution.py:357
  68.6 9.1 %collective-permute-start.19 = (bf16[2,512,128]{2,1,0:T(8,128)(2,1)S(1)}, bf16[2,512,128]{2,1,0:T(8,128)(2,1)S(1)}, u32[]{:S(2)}, u32[]{:S(2)}) collective-permute-start(bf16[2,512,128]{2,1,0:T(8,128)(2,1)S(1)} %get-tuple-element.68), channel_id=1, source_target_pairs={{0,2},{2,0},{4,6},{6,4},{8,10},{10,8},{12,14},{14,12},{16,18},{18,... | collective-permute-start | bytes 786440 | tf_op jit(solution)/shard_map/ppermute | solution.py:358
  68.7 9.8 %collective-permute-start.20 = (bf16[2,512,128]{2,1,0:T(8,128)(2,1)S(1)}, bf16[2,512,128]{2,1,0:T(8,128)(2,1)S(1)}, u32[]{:S(2)}, u32[]{:S(2)}) collective-permute-start(bf16[2,512,128]{2,1,0:T(8,128)(2,1)S(1)} %get-tuple-element.69), channel_id=1, source_target_pairs={{0,4},{2,6},{4,0},{6,2},{8,12},{10,14},{12,8},{14,10},{16,20},{18,... | collective-permute-start | bytes 786440 | tf_op jit(solution)/shard_map/ppermute | solution.py:358
  71.2 10.0 %collective-permute-start.21 = (bf16[2,512,128]{2,1,0:T(8,128)(2,1)S(1)}, bf16[2,512,128]{2,1,0:T(8,128)(2,1)S(1)}, u32[]{:S(2)}, u32[]{:S(2)}) collective-permute-start(bf16[2,512,128]{2,1,0:T(8,128)(2,1)S(1)} %get-tuple-element.70), channel_id=1, source_target_pairs={{0,6},{2,4},{4,2},{6,0},{8,14},{10,12},{12,10},{14,8},{16,22},{18,... | collective-permute-start | bytes 786440 | tf_op jit(solution)/shard_map/ppermute | solution.py:358
  81.4 14.7 %collective-permute-start.22 = (bf16[512,256]{1,0:T(8,128)(2,1)S(1)}, bf16[512,256]{1,0:T(8,128)(2,1)S(1)}, u32[]{:S(2)}, u32[]{:S(2)}) collective-permute-start(bf16[512,256]{1,0:T(8,128)(2,1)S(1)} %get-tuple-element.78), channel_id=1, source_target_pairs={{0,64},{2,66},{4,68},{6,70},{8,72},{10,74},{12,76},{14,78},{16,80}... | collective-permute-start | bytes 786440 | tf_op jit(solution)/shard_map/ppermute | solution.py:363
  84.2 11.9 %collective-permute-start.23 = (bf16[512,256]{1,0:T(8,128)(2,1)S(1)}, bf16[512,256]{1,0:T(8,128)(2,1)S(1)}, u32[]{:S(2)}, u32[]{:S(2)}) collective-permute-start(bf16[512,256]{1,0:T(8,128)(2,1)S(1)} %get-tuple-element.79), channel_id=1, source_target_pairs={{0,192},{2,194},{4,196},{6,198},{8,200},{10,202},{12,204},{14,206}... | collective-permute-start | bytes 786440 | tf_op jit(solution)/shard_map/ppermute | solution.py:363
  90.9 6.5 %collective-permute-start.24 = (bf16[2,512,128]{2,1,0:T(8,128)(2,1)S(1)}, bf16[2,512,128]{2,1,0:T(8,128)(2,1)S(1)}, u32[]{:S(2)}, u32[]{:S(2)}) collective-permute-start(bf16[2,512,128]{2,1,0:T(8,128)(2,1)S(1)} %get-tuple-element.82), channel_id=1, source_target_pairs={{0,2},{2,0},{4,6},{6,4},{8,10},{10,8},{12,14},{14,12},{16,18},{18,... | collective-permute-start | bytes 786440 | tf_op jit(solution)/shard_map/ppermute | solution.py:365
  91.0 12.3 %collective-permute-start.25 = (bf16[2,512,128]{2,1,0:T(8,128)(2,1)S(1)}, bf16[2,512,128]{2,1,0:T(8,128)(2,1)S(1)}, u32[]{:S(2)}, u32[]{:S(2)}) collective-permute-start(bf16[2,512,128]{2,1,0:T(8,128)(2,1)S(1)} %get-tuple-element.83), channel_id=1, source_target_pairs={{0,4},{2,6},{4,0},{6,2},{8,12},{10,14},{12,8},{14,10},{16,20},{18,... | collective-permute-start | bytes 786440 | tf_op jit(solution)/shard_map/ppermute | solution.py:365
  96.0 10.0 %collective-permute-start.26 = (bf16[2,512,128]{2,1,0:T(8,128)(2,1)S(1)}, bf16[2,512,128]{2,1,0:T(8,128)(2,1)S(1)}, u32[]{:S(2)}, u32[]{:S(2)}) collective-permute-start(bf16[2,512,128]{2,1,0:T(8,128)(2,1)S(1)} %get-tuple-element.84), channel_id=1, source_target_pairs={{0,6},{2,4},{4,2},{6,0},{8,14},{10,12},{12,10},{14,8},{16,22},{18,... | collective-permute-start | bytes 786440 | tf_op jit(solution)/shard_map/ppermute | solution.py:365
  106.0 11.6 %collective-permute-start.27 = (bf16[512,128]{1,0:T(8,128)(2,1)S(1)}, bf16[512,128]{1,0:T(8,128)(2,1)S(1)}, u32[]{:S(2)}, u32[]{:S(2)}) collective-permute-start(bf16[512,128]{1,0:T(8,128)(2,1)S(1)} %get-tuple-element.101), channel_id=1, source_target_pairs={{0,32},{2,34},{4,36},{6,38},{8,40},{10,42},{12,44},{14,46},{16,48}... | collective-permute-start | bytes 393224 | tf_op jit(solution)/shard_map/ppermute | solution.py:368
  (9 other events, 43.0 us)
where the time goes:
time: 120 us; the launch traced here: 118 us
  starting transfers between devices  50.9 us (42%)
  waiting for transfers between devices  39.7 us (33%)
  Pallas kernels  22.5 us (19%)
  local copies, waits for them, and re-layouts  2.66 us (2%)
  other arithmetic  1.77 us (1%)
    pallas_call x3, Pallas kernels, run_backward(): pl.pallas_call(functools.partial(backward, group, width, span, begins, en...  11 us
    ppermute x3, waiting for transfers between devices, local(): dq = [dq[0]] + [send(dq[s], perm=Y[s]) for s in range(1, SLOTS)]  9.79 us
    pallas_call x1, Pallas kernels, run_forward(): pl.pallas_call(functools.partial(forward, group, width), out_shape=[jax.S...  8.93 us
    ppermute x3, starting transfers between devices, local(): stats = [merged] + [send(merged, perm=Y[s]) for s in range(1, SLOTS)]  7.26 us
    ppermute x2, starting transfers between devices, local(): ga, gb = (send(ga, perm=NEAR), send(gb, perm=REST))  6.95 us
    ppermute x2, waiting for transfers between devices, local(): a, b = (send(key_home, perm=NEAR), send(key_home, perm=REST))  6.68 us
    ppermute x3, starting transfers between devices, local(): dq = [dq[0]] + [send(dq[s], perm=Y[s]) for s in range(1, SLOTS)]  5.12 us
    ppermute x3, starting transfers between devices, local(): keys = [held] + [send(held, perm=X[n]) for n in range(1, 4)]  5.05 us
  transfers between devices with their start and end apart: 32, of which 16 were waited for; matrix products, arithmetic and copies ran while one was open for 3% of the time, Pallas kernels for 6%

commit v1 on v0

--- a/solution.py
+++ b/solution.py
@@ -35,6 +35,8 @@
 NEAR = flip(32)
 REST = [(d, (d + (32 if d // 32 % 2 else -32)) % DEVICES) for d in range(DEVICES)]
 
+OPPOSITE = flip(64)
+
 
 def dot(a, b):
     return lax.dot_general(a, b, (((1,), (0,)), ((), ())), preferred_element_type=F32)
@@ -45,12 +47,19 @@
 
 
 def fill(rows, keys, q_s, do_s, k_s, v_s, kt_s, vt_s, group, width):
+    own, other, near, last, far_own, far_other = rows
+    top, low = pl.ds(0, CHUNK), pl.ds(CHUNK, CHUNK)
+    parts = [
+        [(own, top), (near, top), (far_own, top), (last, top)],
+        [(other, top), (near, low), (far_other, top), (last, low)],
+    ]
     for t in range(TILES):
         for s in range(SLOTS):
-            ref, to = rows[t * SLOTS + s], pl.ds(s * CHUNK, CHUNK)
+            ref, at = parts[t][s]
+            part, to = ref[at, :], pl.ds(s * CHUNK, CHUNK)
             for h in range(group):
-                q_s[t, h, to, :] = ref[:, h * width : (h + 1) * width]
-                do_s[t, h, to, :] = ref[:, (group + h) * width : (group + h + 1) * width]
+                q_s[t, h, to, :] = part[:, h * width : (h + 1) * width]
+                do_s[t, h, to, :] = part[:, (group + h) * width : (group + h + 1) * width]
     for piece in range(PIECES):
         for m, ref in enumerate(keys):
             part = ref[pl.ds(piece * CHUNK, CHUNK), :]
@@ -94,7 +103,7 @@
 
 
 def forward(group, width, sc, *refs):
-    rows, keys, refs = refs[: TILES * SLOTS], refs[TILES * SLOTS :][:4], refs[TILES * SLOTS + 4 :]
+    rows, keys, refs = refs[:6], refs[6:10], refs[10:]
     values, stat, q_s, do_s, k_s, v_s, kt_s, t_s, acc, high, total, mixed = refs
     unit = LOG2E / math.sqrt(width)
     heads = range(group)
@@ -267,7 +276,7 @@
     return pl.pallas_call(
         functools.partial(forward, group, width),
         out_shape=[jax.ShapeDtypeStruct(acc.shape, BF16), stat, row, row, key, key, turned],
-        in_specs=[SMEM] + [VMEM] * (TILES * SLOTS + 4),
+        in_specs=[SMEM] + [VMEM] * 10,
         out_specs=[VMEM] * 7,
         scratch_shapes=[pltpu.VMEM(turned.shape, BF16), pltpu.VMEM(acc.shape, F32)]
         + [pltpu.VMEM(line.shape, F32)] * 3,
@@ -320,14 +329,14 @@
         name="pack",
     )(query, key, value, dout)
     row_other = send(row_home, perm=NEXT)
-    near, last = send(row_home, perm=Y[1]), send(row_home, perm=Y[3])
     a, b = send(key_home, perm=NEAR), send(key_home, perm=REST)
-    row_other, near, last, a, b = lax.optimization_barrier((row_other, near, last, a, b))
-    near_other, last_other = send(row_other, perm=Y[1]), send(row_other, perm=Y[3])
+    row_other, a, b = lax.optimization_barrier((row_other, a, b))
+    both = jnp.concatenate([row_home, row_other], axis=0)
+    near, last = send(both, perm=Y[1]), send(both, perm=Y[3])
     held = jnp.concatenate([key_home, a, b, send(b, perm=NEAR)], axis=0)
     keys = [held] + [send(held, perm=X[n]) for n in range(1, 4)]
-    far, far_other = send(last, perm=Y[1]), send(near_other, perm=Y[3])
-    rows = [row_home, near, far, last, row_other, near_other, far_other, last_other]
+    far_own, far_other = send(last[:CHUNK], perm=Y[1]), send(near[CHUNK:], perm=Y[3])
+    rows = [row_home, row_other, near, last, far_own, far_other]
 
     numbers = jnp.arange(DOCS, dtype=jnp.int32)
     starts = jnp.sum((document[None, :] < numbers[:, None]).astype(jnp.int32), axis=1)
@@ -354,17 +363,18 @@
     back = functools.partial(run_backward, group, width)
     out = back((3, 4), True, False, sc, held, *stats, stat, values)
     far, mixed, carried = out[0], out[1 : 1 + SLOTS], out[1 + SLOTS :]
-    one, two = send(far[0], perm=NEAR), send(far[1], perm=REST)
-    mixed = add(mixed[0], *[send(mixed[s], perm=Y[s]) for s in range(1, SLOTS)])
+    flat = (2 * PAIR, 2 * width)
+    gc = send(far.reshape(flat), perm=OPPOSITE)
+    mixed = [mixed[0]] + [send(mixed[s], perm=Y[s]) for s in range(1, SLOTS)]
     near_by, *carried = back((1, 3), False, False, sc, held, *carried)
-    ga = jnp.concatenate([near_by[0], add(near_by[1], two)], axis=0)
-    gb = jnp.concatenate([add(near_by[2], one), near_by[3]], axis=0)
-    ga, gb, mixed, carried = lax.optimization_barrier((ga, gb, mixed, carried))
-    ga, gb = send(ga, perm=NEAR), send(gb, perm=REST)
+    near_by, mixed, carried = lax.optimization_barrier((near_by, mixed, carried))
+    ga = send(near_by[:2].reshape(flat), perm=NEAR)
+    gb = send(near_by[2:].reshape(flat), perm=REST)
     close, *dq = back((0, 1), False, True, sc, held, *carried)
     dq = [dq[0]] + [send(dq[s], perm=Y[s]) for s in range(1, SLOTS)]
-    grad = add(close.reshape(2 * PAIR, 2 * width), ga, gb)
+    grad = add(close.reshape(flat), ga, gb, gc)
     _, mixed, dq = lax.optimization_barrier((grad, mixed, dq))
+    mixed = add(*mixed)
     mixed = [mixed[0], send(mixed[1], perm=NEXT)]
     grad = grad.reshape(4, CHUNK, 2 * width)
     grad = add(grad[0], *[send(grad[n], perm=X[n]) for n in range(1, 4)])

time: 120 us -> 113 us (0.942)
  the two profiles are of different devices: /device:TPU:128 before, /device:TPU:32 now
where the time goes in v1:
time: 113 us; the launch traced here: 112 us
  starting transfers between devices  57.4 us (51%)
  waiting for transfers between devices  32.4 us (29%)
  Pallas kernels  16.9 us (15%)
  local copies, waits for them, and re-layouts  3.4 us (3%)
    pallas_call x3, Pallas kernels, run_backward(): pl.pallas_call(functools.partial(backward, group, width, span, begins, en...  8.05 us
    pallas_call x1, Pallas kernels, run_forward(): pl.pallas_call(functools.partial(forward, group, width), out_shape=[jax.S...  6.28 us
    ppermute x2, starting transfers between devices, local(): a, b = (send(key_home, perm=NEAR), send(key_home, perm=REST))  6.02 us
    ppermute x1, starting transfers between devices, local(): gc = send(far.reshape(flat), perm=OPPOSITE)  5.81 us
    ppermute x3, waiting for transfers between devices, local(): keys = [held] + [send(held, perm=X[n]) for n in range(1, 4)]  5.56 us
    ppermute x3, starting transfers between devices, local(): grad = add(grad[0], *[send(grad[n], perm=X[n]) for n in range(1, 4)])  5.55 us
    ppermute x3, waiting for transfers between devices, local(): dq = [dq[0]] + [send(dq[s], perm=Y[s]) for s in range(1, SLOTS)]  5.53 us
    ppermute x3, waiting for transfers between devices, local(): grad = add(grad[0], *[send(grad[n], perm=X[n]) for n in range(1, 4)])  4.94 us
  transfers between devices with their start and end apart: 29, of which 15 were waited for; matrix products, arithmetic and copies ran while one was open for 3% of the time, Pallas kernels for 5%

profile of v1, /device:TPU:32, one launch (start us, length us, event | category | flops | bytes accessed | tf_op | source)
XLA Modules:
  0.0 111.9 jit_solution(1631568118210014347)
XLA Ops:
  4.3 4.6 %collective-permute-start.2 = (bf16[128,256]{1,0:T(8,128)(2,1)}, bf16[128,256]{1,0:T(8,128)(2,1)S(1)}, u32[]{:S(2)}, u32[]{:S(2)}) collective-permute-start(bf16[128,256]{1,0:T(8,128)(2,1)} %get-tuple-element.52), channel_id=1, source_target_pairs={{0,192},{2,194},{4,196},{6,198},{8,200},{10,202},{12,204},{14,206}... | collective-permute-start | bytes 196616 | tf_op jit(solution)/shard_map/ppermute | solution.py:332
  11.7 3.4 %collective-permute-done.1 = bf16[128,256]{1,0:T(8,128)(2,1)S(1)} collective-permute-done((bf16[128,256]{1,0:T(8,128)(2,1)}, bf16[128,256]{1,0:T(8,128)(2,1)S(1)}, u32[]{:S(2)}, u32[]{:S(2)}) %collective-permute-start.1) | collective-permute-done | bytes 65568 | tf_op jit(solution)/shard_map/ppermute | solution.py:332
  15.1 3.1 %collective-permute-start.4 = (bf16[256,1024]{1,0:T(8,128)(2,1)S(1)}, bf16[256,1024]{1,0:T(8,128)(2,1)S(1)}, u32[]{:S(2)}, u32[]{:S(2)}) collective-permute-start(bf16[256,1024]{1,0:T(8,128)(2,1)S(1)} %constant_dynamic-update-slice_fusion), channel_id=1, source_target_pairs={{0,6},{2,4},{4,2},{6,0},{8,14},{10,12},{12,10},{14,8},{16,22},{18,... | collective-permute-start | bytes 1572872 | tf_op jit(solution)/shard_map/ppermute | solution.py:335
  19.2 4.2 %collective-permute-start.7 = (bf16[128,256]{1,0:T(8,128)(2,1)S(1)}, bf16[128,256]{1,0:T(8,128)(2,1)S(1)}, u32[]{:S(2)}, u32[]{:S(2)}) collective-permute-start(bf16[128,256]{1,0:T(8,128)(2,1)S(1)} %collective-permute-done.2), channel_id=1, source_target_pairs={{0,64},{2,66},{4,68},{6,70},{8,72},{10,74},{12,76},{14,78},{16,80}... | collective-permute-start | bytes 196616 | tf_op jit(solution)/shard_map/ppermute | solution.py:336
  23.5 2.2 %collective-permute-done.7 = bf16[128,256]{1,0:T(8,128)(2,1)S(1)} collective-permute-done((bf16[128,256]{1,0:T(8,128)(2,1)S(1)}, bf16[128,256]{1,0:T(8,128)(2,1)S(1)}, u32[]{:S(2)}, u32[]{:S(2)}) %collective-permute-start.7) | collective-permute-done | bytes 65568 | tf_op jit(solution)/shard_map/ppermute | solution.py:336
  25.7 2.8 %collective-permute-start.10 = (bf16[512,256]{1,0:T(8,128)(2,1)S(1)}, bf16[512,256]{1,0:T(8,128)(2,1)S(1)}, u32[]{:S(2)}, u32[]{:S(2)}) collective-permute-start(bf16[512,256]{1,0:T(8,128)(2,1)S(1)} %constant_dynamic-update-slice_fusion.2.refs_6_), channel_id=1, source_target_pairs={{0,24},{2,26},{4,28},{6,30},{8,16},{10,18},{12,20},{14,22},{16,8},... | collective-permute-start | bytes 786440 | tf_op jit(solution)/shard_map/ppermute | solution.py:337
  33.5 4.1 %collective-permute-done.10.refs_9_ = bf16[512,256]{1,0:T(8,128)(2,1)S(1)} collective-permute-done((bf16[512,256]{1,0:T(8,128)(2,1)S(1)}, bf16[512,256]{1,0:T(8,128)(2,1)S(1)}, u32[]{:S(2)}, u32[]{:S(2)}) %collective-permute-start.10) | collective-permute-done | bytes 262176 | tf_op jit(solution)/shard_map/ppermute | solution.py:337
  40.3 6.3 %forward.1 = (bf16[2,4,128,512]{3,2,1,0:T(8,128)(2,1)S(1)}, f32[2,12,512]{2,1,0:T(8,128)S(1)}, bf16[2,4,512,128]{3,2,1,0:T(8,128)(2,1)S(1)}, bf16[2,4,512,128]{3...) custom-call(s32[16]{0:T(128)S(1)} %concatenate.12.sc, ...), custom_call_target="tpu_custom_call" | custom-call | flops 12884901888 | bytes 8388608 | tf_op jit(solution)/shard_map/forward/pallas_call | solution.py:276
  46.6 3.6 %collective-permute-start.11 = (f32[2,12,512]{2,1,0:T(8,128)S(1)}, f32[2,12,512]{2,1,0:T(8,128)S(1)}, u32[]{:S(2)}, u32[]{:S(2)}) collective-permute-start(f32[2,12,512]{2,1,0:T(8,128)S(1)} %get-tuple-element.61.refs_4_), channel_id=1, source_target_pairs={{0,32},{2,34},{4,36},{6,38},{8,40},{10,42},{12,44},{14,46},{16,48}... | collective-permute-start | bytes 147464 | tf_op jit(solution)/shard_map/ppermute | solution.py:349
  50.1 2.2 %collective-permute-done.11 = f32[2,12,512]{2,1,0:T(8,128)S(1)} collective-permute-done((f32[2,12,512]{2,1,0:T(8,128)S(1)}, f32[2,12,512]{2,1,0:T(8,128)S(1)}, u32[]{:S(2)}, u32[]{:S(2)}) %collective-permute-start.11) | collective-permute-done | bytes 49184 | tf_op jit(solution)/shard_map/ppermute | solution.py:349
  52.7 4.0 %collective-permute-start.12 = (f32[2,12,512]{2,1,0:T(8,128)S(1)}, f32[2,12,512]{2,1,0:T(8,128)S(1)}, u32[]{:S(2)}, u32[]{:S(2)}) collective-permute-start(f32[2,12,512]{2,1,0:T(8,128)S(1)} %pad_maximum_fusion.refs_0_), channel_id=1, source_target_pairs={{0,2},{2,0},{4,6},{6,4},{8,10},{10,8},{12,14},{14,12},{16,18},{18,... | collective-permute-start | bytes 147464 | tf_op jit(solution)/shard_map/ppermute | solution.py:361
  60.8 2.7 %backward_begin.1 = (bf16[2,256,256]{2,1,0:T(8,128)(2,1)S(1)}, bf16[2,512,128]{2,1,0:T(8,128)(2,1)S(1)}, bf16[2,512,128]{2,1,0:T(8,128)(2,1)S(1)}, bf16[2,512,12...) custom-call(s32[16]{0:T(128)S(1)} %concatenate.12.sc, ...), custom_call_target="tpu_custom_call" | custom-call | flops 5368709120 | bytes 8388608 | tf_op jit(solution)/shard_map/backward_begin/pallas_call | solution.py:300
  64.8 3.4 %collective-permute-start.17 = (bf16[2,512,128]{2,1,0:T(8,128)(2,1)S(1)}, bf16[2,512,128]{2,1,0:T(8,128)(2,1)S(1)}, u32[]{:S(2)}, u32[]{:S(2)}) collective-permute-start(bf16[2,512,128]{2,1,0:T(8,128)(2,1)S(1)} %get-tuple-element.70), channel_id=1, source_target_pairs={{0,6},{2,4},{4,2},{6,0},{8,14},{10,12},{12,10},{14,8},{16,22},{18,... | collective-permute-start | bytes 786440 | tf_op jit(solution)/shard_map/ppermute | solution.py:368
  68.3 5.8 %collective-permute-start.20 = (bf16[512,256]{1,0:T(8,128)(2,1)S(1)}, bf16[512,256]{1,0:T(8,128)(2,1)S(1)}, u32[]{:S(2)}, u32[]{:S(2)}) collective-permute-start(bf16[512,256]{1,0:T(8,128)(2,1)S(1)} %bitcast.21), channel_id=1, source_target_pairs={{0,128},{2,130},{4,132},{6,134},{8,136},{10,138},{12,140},{14,142}... | collective-permute-start | bytes 786440 | tf_op jit(solution)/shard_map/ppermute | solution.py:367
  74.1 2.7 %backward_middle.1 = (bf16[4,256,256]{2,1,0:T(8,128)(2,1)S(1)}, f32[2,4,128,512]{3,2,1,0:T(8,128)S(1)}, f32[2,4,1,512]{3,2,1,0:T(1,128)S(1)}, f32[2,4,1,512]{3,2,1,0:T(1,128)S(1)}) custom-call(s32[16]{0:T(128)S(1)} %concatenate.12.sc, bf16[2,4,512,128]{3,2,1,0:T(8,128)(2,1)S(1)} %get-tuple-element.56.q_s, ...), custom_call_target="tpu_custom_call" | custom-call | flops 10737418240 | bytes 8388608 | tf_op jit(solution)/shard_map/backward_middle/pallas_call | solution.py:300
  76.8 3.7 %collective-permute-start.19 = (bf16[512,256]{1,0:T(8,128)(2,1)S(1)}, bf16[512,256]{1,0:T(8,128)(2,1)S(1)}, u32[]{:S(2)}, u32[]{:S(2)}) collective-permute-start(bf16[512,256]{1,0:T(8,128)(2,1)S(1)} %bitcast.23), channel_id=1, source_target_pairs={{0,192},{2,194},{4,196},{6,198},{8,200},{10,202},{12,204},{14,206}... | collective-permute-start | bytes 786440 | tf_op jit(solution)/shard_map/ppermute | solution.py:372
  80.6 2.2 %collective-permute-start.18 = (bf16[512,256]{1,0:T(8,128)(2,1)S(1)}, bf16[512,256]{1,0:T(8,128)(2,1)S(1)}, u32[]{:S(2)}, u32[]{:S(2)}) collective-permute-start(bf16[512,256]{1,0:T(8,128)(2,1)S(1)} %bitcast.22), channel_id=1, source_target_pairs={{0,64},{2,66},{4,68},{6,70},{8,72},{10,74},{12,76},{14,78},{16,80}... | collective-permute-start | bytes 786440 | tf_op jit(solution)/shard_map/ppermute | solution.py:371
  82.8 2.7 %backward_end.1 = (bf16[2,256,256]{2,1,0:T(8,128)(2,1)S(1)}, bf16[2,512,128]{2,1,0:T(8,128)(2,1)S(1)}, bf16[2,512,128]{2,1,0:T(8,128)(2,1)S(1)}, bf16[2,512,128]...) custom-call(s32[16]{0:T(128)S(1)} %concatenate.12.sc, bf16[2,4,512,128]{3,2,1,0:T(8,128)(2,1)S(1)} %get-tuple-element.56.q_s, ...), custom_call_target="tpu_custom_call" | custom-call | flops 5368709120 | bytes 8388608 | tf_op jit(solution)/shard_map/backward_end/pallas_call | solution.py:300
  85.6 3.1 %collective-permute-start.22 = (bf16[2,512,128]{2,1,0:T(8,128)(2,1)S(1)}, bf16[2,512,128]{2,1,0:T(8,128)(2,1)S(1)}, u32[]{:S(2)}, u32[]{:S(2)}) collective-permute-start(bf16[2,512,128]{2,1,0:T(8,128)(2,1)S(1)} %get-tuple-element.86), channel_id=1, source_target_pairs={{0,4},{2,6},{4,0},{6,2},{8,12},{10,14},{12,8},{14,10},{16,20},{18,... | collective-permute-start | bytes 786440 | tf_op jit(solution)/shard_map/ppermute | solution.py:374
  90.2 2.7 %collective-permute-done.19 = bf16[512,256]{1,0:T(8,128)(2,1)S(1)} collective-permute-done((bf16[512,256]{1,0:T(8,128)(2,1)S(1)}, bf16[512,256]{1,0:T(8,128)(2,1)S(1)}, u32[]{:S(2)}, u32[]{:S(2)}) %collective-permute-start.19) | collective-permute-done | bytes 262176 | tf_op jit(solution)/shard_map/ppermute | solution.py:372
  93.1 2.8 %collective-permute-done.22 = bf16[2,512,128]{2,1,0:T(8,128)(2,1)S(1)} collective-permute-done((bf16[2,512,128]{2,1,0:T(8,128)(2,1)S(1)}, bf16[2,512,128]{2,1,0:T(8,128)(2,1)S(1)}, u32[]{:S(2)}, u32[]{:S(2)}) %collective-permute-start.22) | collective-permute-done | bytes 262176 | tf_op jit(solution)/shard_map/ppermute | solution.py:374
  96.0 2.7 %collective-permute-done.23 = bf16[2,512,128]{2,1,0:T(8,128)(2,1)S(1)} collective-permute-done((bf16[2,512,128]{2,1,0:T(8,128)(2,1)S(1)}, bf16[2,512,128]{2,1,0:T(8,128)(2,1)S(1)}, u32[]{:S(2)}, u32[]{:S(2)}) %collective-permute-start.23) | collective-permute-done | bytes 262176 | tf_op jit(solution)/shard_map/ppermute | solution.py:374
  100.6 4.0 %collective-permute-start.28 = (bf16[128,256]{1,0:T(8,128)(2,1)S(1)}, bf16[128,256]{1,0:T(8,128)(2,1)S(1)}, u32[]{:S(2)}, u32[]{:S(2)}) collective-permute-start(bf16[128,256]{1,0:T(8,128)(2,1)S(1)} %get-tuple-element.101), channel_id=1, source_target_pairs={{0,24},{2,26},{4,28},{6,30},{8,16},{10,18},{12,20},{14,22},{16,8},... | collective-permute-start | bytes 196616 | tf_op jit(solution)/shard_map/ppermute | solution.py:380
  107.1 3.3 %collective-permute-done.27 = bf16[128,256]{1,0:T(8,128)(2,1)S(1)} collective-permute-done((bf16[128,256]{1,0:T(8,128)(2,1)S(1)}, bf16[128,256]{1,0:T(8,128)(2,1)S(1)}, u32[]{:S(2)}, u32[]{:S(2)}) %collective-permute-start.27) | collective-permute-done | bytes 65568 | tf_op jit(solution)/shard_map/ppermute | solution.py:380
  (66 shorter events, 28.7 us)
Async XLA Ops:
  2.4 12.7 %collective-permute-start = (bf16[128,1024]{1,0:T(8,128)(2,1)}, bf16[128,1024]{1,0:T(8,128)(2,1)S(1)}, u32[]{:S(2)}, u32[]{:S(2)}) collective-permute-start(bf16[128,1024]{1,0:T(8,128)(2,1)} %get-tuple-element.51.refs_0_), channel_id=1, source_target_pairs={{0,32},{2,34},{4,36},{6,38},{8,40},{10,42},{12,44},{14,46},{16,48}... | collective-permute-start | bytes 786440 | tf_op jit(solution)/shard_map/ppermute | solution.py:331
  4.3 7.4 %collective-permute-start.2 = (bf16[128,256]{1,0:T(8,128)(2,1)}, bf16[128,256]{1,0:T(8,128)(2,1)S(1)}, u32[]{:S(2)}, u32[]{:S(2)}) collective-permute-start(bf16[128,256]{1,0:T(8,128)(2,1)} %get-tuple-element.52), channel_id=1, source_target_pairs={{0,192},{2,194},{4,196},{6,198},{8,200},{10,202},{12,204},{14,206}... | collective-permute-start | bytes 196616 | tf_op jit(solution)/shard_map/ppermute | solution.py:332
  15.1 14.7 %collective-permute-start.4 = (bf16[256,1024]{1,0:T(8,128)(2,1)S(1)}, bf16[256,1024]{1,0:T(8,128)(2,1)S(1)}, u32[]{:S(2)}, u32[]{:S(2)}) collective-permute-start(bf16[256,1024]{1,0:T(8,128)(2,1)S(1)} %constant_dynamic-update-slice_fusion), channel_id=1, source_target_pairs={{0,6},{2,4},{4,2},{6,0},{8,14},{10,12},{12,10},{14,8},{16,22},{18,... | collective-permute-start | bytes 1572872 | tf_op jit(solution)/shard_map/ppermute | solution.py:335
  18.2 13.6 %collective-permute-start.3 = (bf16[256,1024]{1,0:T(8,128)(2,1)S(1)}, bf16[256,1024]{1,0:T(8,128)(2,1)S(1)}, u32[]{:S(2)}, u32[]{:S(2)}) collective-permute-start(bf16[256,1024]{1,0:T(8,128)(2,1)S(1)} %constant_dynamic-update-slice_fusion), channel_id=1, source_target_pairs={{0,2},{2,0},{4,6},{6,4},{8,10},{10,8},{12,14},{14,12},{16,18},{18,... | collective-permute-start | bytes 1572872 | tf_op jit(solution)/shard_map/ppermute | solution.py:335
  19.2 6.5 %collective-permute-start.7 = (bf16[128,256]{1,0:T(8,128)(2,1)S(1)}, bf16[128,256]{1,0:T(8,128)(2,1)S(1)}, u32[]{:S(2)}, u32[]{:S(2)}) collective-permute-start(bf16[128,256]{1,0:T(8,128)(2,1)S(1)} %collective-permute-done.2), channel_id=1, source_target_pairs={{0,64},{2,66},{4,68},{6,70},{8,72},{10,74},{12,76},{14,78},{16,80}... | collective-permute-start | bytes 196616 | tf_op jit(solution)/shard_map/ppermute | solution.py:336
  25.7 11.9 %collective-permute-start.10 = (bf16[512,256]{1,0:T(8,128)(2,1)S(1)}, bf16[512,256]{1,0:T(8,128)(2,1)S(1)}, u32[]{:S(2)}, u32[]{:S(2)}) collective-permute-start(bf16[512,256]{1,0:T(8,128)(2,1)S(1)} %constant_dynamic-update-slice_fusion.2.refs_6_), channel_id=1, source_target_pairs={{0,24},{2,26},{4,28},{6,30},{8,16},{10,18},{12,20},{14,22},{16,8},... | collective-permute-start | bytes 786440 | tf_op jit(solution)/shard_map/ppermute | solution.py:337
  28.4 10.0 %collective-permute-start.9 = (bf16[512,256]{1,0:T(8,128)(2,1)S(1)}, bf16[512,256]{1,0:T(8,128)(2,1)S(1)}, u32[]{:S(2)}, u32[]{:S(2)}) collective-permute-start(bf16[512,256]{1,0:T(8,128)(2,1)S(1)} %constant_dynamic-update-slice_fusion.2.refs_6_), channel_id=1, source_target_pairs={{0,8},{2,10},{4,12},{6,14},{8,0},{10,2},{12,4},{14,6},{16,24},{18,... | collective-permute-start | bytes 786440 | tf_op jit(solution)/shard_map/ppermute | solution.py:337
  29.2 9.8 %collective-permute-start.8 = (bf16[512,256]{1,0:T(8,128)(2,1)S(1)}, bf16[512,256]{1,0:T(8,128)(2,1)S(1)}, u32[]{:S(2)}, u32[]{:S(2)}) collective-permute-start(bf16[512,256]{1,0:T(8,128)(2,1)S(1)} %constant_dynamic-update-slice_fusion.2.refs_6_), channel_id=1, source_target_pairs={{0,16},{2,18},{4,20},{6,22},{8,24},{10,26},{12,28},{14,30},{16,0},... | collective-permute-start | bytes 786440 | tf_op jit(solution)/shard_map/ppermute | solution.py:337
  29.8 9.2 %collective-permute-start.5 = (bf16[128,1024]{1,0:T(8,128)(2,1)S(1)}, bf16[128,1024]{1,0:T(8,128)(2,1)S(1)}, u32[]{:S(2)}, u32[]{:S(2)}) collective-permute-start(bf16[128,1024]{1,0:T(8,128)(2,1)S(1)} %slice.98), channel_id=1, source_target_pairs={{0,2},{2,0},{4,6},{6,4},{8,10},{10,8},{12,14},{14,12},{16,18},{18,... | collective-permute-start | bytes 786440 | tf_op jit(solution)/shard_map/ppermute | solution.py:338
  32.5 7.8 %collective-permute-start.6 = (bf16[128,1024]{1,0:T(8,128)(2,1)}, bf16[128,1024]{1,0:T(8,128)(2,1)S(1)}, u32[]{:S(2)}, u32[]{:S(2)}) collective-permute-start(bf16[128,1024]{1,0:T(8,128)(2,1)} %slice.99), channel_id=1, source_target_pairs={{0,6},{2,4},{4,2},{6,0},{8,14},{10,12},{12,10},{14,8},{16,22},{18,... | collective-permute-start | bytes 786440 | tf_op jit(solution)/shard_map/ppermute | solution.py:338
  52.7 8.1 %collective-permute-start.12 = (f32[2,12,512]{2,1,0:T(8,128)S(1)}, f32[2,12,512]{2,1,0:T(8,128)S(1)}, u32[]{:S(2)}, u32[]{:S(2)}) collective-permute-start(f32[2,12,512]{2,1,0:T(8,128)S(1)} %pad_maximum_fusion.refs_0_), channel_id=1, source_target_pairs={{0,2},{2,0},{4,6},{6,4},{8,10},{10,8},{12,14},{14,12},{16,18},{18,... | collective-permute-start | bytes 147464 | tf_op jit(solution)/shard_map/ppermute | solution.py:361
  63.5 13.3 %collective-permute-start.15 = (bf16[2,512,128]{2,1,0:T(8,128)(2,1)S(1)}, bf16[2,512,128]{2,1,0:T(8,128)(2,1)S(1)}, u32[]{:S(2)}, u32[]{:S(2)}) collective-permute-start(bf16[2,512,128]{2,1,0:T(8,128)(2,1)S(1)} %get-tuple-element.68), channel_id=1, source_target_pairs={{0,2},{2,0},{4,6},{6,4},{8,10},{10,8},{12,14},{14,12},{16,18},{18,... | collective-permute-start | bytes 786440 | tf_op jit(solution)/shard_map/ppermute | solution.py:368
  63.6 13.2 %collective-permute-start.16 = (bf16[2,512,128]{2,1,0:T(8,128)(2,1)S(1)}, bf16[2,512,128]{2,1,0:T(8,128)(2,1)S(1)}, u32[]{:S(2)}, u32[]{:S(2)}) collective-permute-start(bf16[2,512,128]{2,1,0:T(8,128)(2,1)S(1)} %get-tuple-element.69), channel_id=1, source_target_pairs={{0,4},{2,6},{4,0},{6,2},{8,12},{10,14},{12,8},{14,10},{16,20},{18,... | collective-permute-start | bytes 786440 | tf_op jit(solution)/shard_map/ppermute | solution.py:368
  64.8 12.0 %collective-permute-start.17 = (bf16[2,512,128]{2,1,0:T(8,128)(2,1)S(1)}, bf16[2,512,128]{2,1,0:T(8,128)(2,1)S(1)}, u32[]{:S(2)}, u32[]{:S(2)}) collective-permute-start(bf16[2,512,128]{2,1,0:T(8,128)(2,1)S(1)} %get-tuple-element.70), channel_id=1, source_target_pairs={{0,6},{2,4},{4,2},{6,0},{8,14},{10,12},{12,10},{14,8},{16,22},{18,... | collective-permute-start | bytes 786440 | tf_op jit(solution)/shard_map/ppermute | solution.py:368
  68.3 20.4 %collective-permute-start.20 = (bf16[512,256]{1,0:T(8,128)(2,1)S(1)}, bf16[512,256]{1,0:T(8,128)(2,1)S(1)}, u32[]{:S(2)}, u32[]{:S(2)}) collective-permute-start(bf16[512,256]{1,0:T(8,128)(2,1)S(1)} %bitcast.21), channel_id=1, source_target_pairs={{0,128},{2,130},{4,132},{6,134},{8,136},{10,138},{12,140},{14,142}... | collective-permute-start | bytes 786440 | tf_op jit(solution)/shard_map/ppermute | solution.py:367
  76.8 16.1 %collective-permute-start.19 = (bf16[512,256]{1,0:T(8,128)(2,1)S(1)}, bf16[512,256]{1,0:T(8,128)(2,1)S(1)}, u32[]{:S(2)}, u32[]{:S(2)}) collective-permute-start(bf16[512,256]{1,0:T(8,128)(2,1)S(1)} %bitcast.23), channel_id=1, source_target_pairs={{0,192},{2,194},{4,196},{6,198},{8,200},{10,202},{12,204},{14,206}... | collective-permute-start | bytes 786440 | tf_op jit(solution)/shard_map/ppermute | solution.py:372
  80.6 12.4 %collective-permute-start.18 = (bf16[512,256]{1,0:T(8,128)(2,1)S(1)}, bf16[512,256]{1,0:T(8,128)(2,1)S(1)}, u32[]{:S(2)}, u32[]{:S(2)}) collective-permute-start(bf16[512,256]{1,0:T(8,128)(2,1)S(1)} %bitcast.22), channel_id=1, source_target_pairs={{0,64},{2,66},{4,68},{6,70},{8,72},{10,74},{12,76},{14,78},{16,80}... | collective-permute-start | bytes 786440 | tf_op jit(solution)/shard_map/ppermute | solution.py:371
  85.5 7.7 %collective-permute-start.21 = (bf16[2,512,128]{2,1,0:T(8,128)(2,1)S(1)}, bf16[2,512,128]{2,1,0:T(8,128)(2,1)S(1)}, u32[]{:S(2)}, u32[]{:S(2)}) collective-permute-start(bf16[2,512,128]{2,1,0:T(8,128)(2,1)S(1)} %get-tuple-element.85), channel_id=1, source_target_pairs={{0,2},{2,0},{4,6},{6,4},{8,10},{10,8},{12,14},{14,12},{16,18},{18,... | collective-permute-start | bytes 786440 | tf_op jit(solution)/shard_map/ppermute | solution.py:374
  85.6 10.4 %collective-permute-start.22 = (bf16[2,512,128]{2,1,0:T(8,128)(2,1)S(1)}, bf16[2,512,128]{2,1,0:T(8,128)(2,1)S(1)}, u32[]{:S(2)}, u32[]{:S(2)}) collective-permute-start(bf16[2,512,128]{2,1,0:T(8,128)(2,1)S(1)} %get-tuple-element.86), channel_id=1, source_target_pairs={{0,4},{2,6},{4,0},{6,2},{8,12},{10,14},{12,8},{14,10},{16,20},{18,... | collective-permute-start | bytes 786440 | tf_op jit(solution)/shard_map/ppermute | solution.py:374
  88.7 10.0 %collective-permute-start.23 = (bf16[2,512,128]{2,1,0:T(8,128)(2,1)S(1)}, bf16[2,512,128]{2,1,0:T(8,128)(2,1)S(1)}, u32[]{:S(2)}, u32[]{:S(2)}) collective-permute-start(bf16[2,512,128]{2,1,0:T(8,128)(2,1)S(1)} %get-tuple-element.87), channel_id=1, source_target_pairs={{0,6},{2,4},{4,2},{6,0},{8,14},{10,12},{12,10},{14,8},{16,22},{18,... | collective-permute-start | bytes 786440 | tf_op jit(solution)/shard_map/ppermute | solution.py:374
  99.0 12.1 %collective-permute-start.25 = (bf16[512,128]{1,0:T(8,128)(2,1)S(1)}, bf16[512,128]{1,0:T(8,128)(2,1)S(1)}, u32[]{:S(2)}, u32[]{:S(2)}) collective-permute-start(bf16[512,128]{1,0:T(8,128)(2,1)S(1)} %get-tuple-element.103), channel_id=1, source_target_pairs={{0,32},{2,34},{4,36},{6,38},{8,40},{10,42},{12,44},{14,46},{16,48}... | collective-permute-start | bytes 393224 | tf_op jit(solution)/shard_map/ppermute | solution.py:382
  99.1 6.4 %collective-permute-start.26 = (bf16[128,256]{1,0:T(8,128)(2,1)S(1)}, bf16[128,256]{1,0:T(8,128)(2,1)S(1)}, u32[]{:S(2)}, u32[]{:S(2)}) collective-permute-start(bf16[128,256]{1,0:T(8,128)(2,1)S(1)} %get-tuple-element.100), channel_id=1, source_target_pairs={{0,16},{2,18},{4,20},{6,22},{8,24},{10,26},{12,28},{14,30},{16,0},... | collective-permute-start | bytes 196616 | tf_op jit(solution)/shard_map/ppermute | solution.py:380
  100.6 6.5 %collective-permute-start.28 = (bf16[128,256]{1,0:T(8,128)(2,1)S(1)}, bf16[128,256]{1,0:T(8,128)(2,1)S(1)}, u32[]{:S(2)}, u32[]{:S(2)}) collective-permute-start(bf16[128,256]{1,0:T(8,128)(2,1)S(1)} %get-tuple-element.101), channel_id=1, source_target_pairs={{0,24},{2,26},{4,28},{6,30},{8,16},{10,18},{12,20},{14,22},{16,8},... | collective-permute-start | bytes 196616 | tf_op jit(solution)/shard_map/ppermute | solution.py:380
  104.6 6.4 %collective-permute-start.24 = (bf16[512,128]{1,0:T(8,128)(2,1)S(1)}, bf16[512,128]{1,0:T(8,128)(2,1)S(1)}, u32[]{:S(2)}, u32[]{:S(2)}) collective-permute-start(bf16[512,128]{1,0:T(8,128)(2,1)S(1)} %get-tuple-element.105), channel_id=1, source_target_pairs={{0,32},{2,34},{4,36},{6,38},{8,40},{10,42},{12,44},{14,46},{16,48}... | collective-permute-start | bytes 393224 | tf_op jit(solution)/shard_map/ppermute | solution.py:378
  (7 other events, 100.6 us)

commit v2 on v1

--- a/solution.py
+++ b/solution.py
@@ -20,6 +20,7 @@
 DOCS = 8
 NEG = -1e30
 FLOOR = -1e29
+SAFE = 60.0
 LOG2E = math.log2(math.e)
 F32 = jnp.float32
 BF16 = jnp.bfloat16
@@ -104,58 +105,83 @@
 
 def forward(group, width, sc, *refs):
     rows, keys, refs = refs[:6], refs[6:10], refs[10:]
-    values, stat, q_s, do_s, k_s, v_s, kt_s, t_s, acc, high, total, mixed = refs
+    values, stat, q_s, do_s, k_s, v_s, kt_s, t_s, acc, high, total = refs
     unit = LOG2E / math.sqrt(width)
     heads = range(group)
     fill(rows, keys, q_s, do_s, k_s, v_s, kt_s, t_s, group, width)
     acc[...] = jnp.zeros_like(acc)
     high[...] = jnp.full_like(high, FLOOR)
     total[...] = jnp.zeros_like(total)
-    mixed[...] = jnp.zeros_like(mixed)
-
-    def block(b, t, base, row, masked):
+
+    def widest(parts):
+        ones = jnp.ones((width, width), BF16)
+        return jnp.max(functools.reduce(jnp.maximum, [dot(p * p, ones) for p in parts]))
+
+    rows_widest = widest([q_s[t, h] for t in range(TILES) for h in heads])
+    keys_widest = widest([k_s[b] for b in range(2 * PIECES)])
+    small = rows_widest * keys_widest * (unit * unit) <= SAFE * SAFE
+
+    def scores_of(b, t, base, row, masked):
         scores = [dot_t(k_s[b], q_s[t, h]) for h in heads]
-        dprobs = [dot_t(v_s[b], do_s[t, h]) for h in heads]
         if masked:
             allowed = allowed_of(sc, base, row)
             scores = [jnp.where(allowed, s, NEG) for s in scores]
+        return scores
+
+    def shifted(b, t, base, row, masked):
+        scores = scores_of(b, t, base, row, masked)
         olds = [high[t, h] for h in heads]
         news = [jnp.maximum(o, jnp.max(s, axis=0, keepdims=True)) for o, s in zip(olds, scores)]
         shrinks = [jnp.exp2((o - n) * unit) for o, n in zip(olds, news)]
         es = [jnp.exp2(s * unit - n * unit) for s, n in zip(scores, news)]
         totals = [total[t, h] * shrinks[h] + jnp.sum(es[h], axis=0, keepdims=True) for h in heads]
-        mixeds = [
-            mixed[t, h] * shrinks[h] + jnp.sum(es[h] * dprobs[h], axis=0, keepdims=True)
-            for h in heads
-        ]
         accs = [acc[t, h] * shrinks[h] + dot(t_s[b], es[h].astype(BF16)) for h in heads]
         for h in heads:
             high[t, h] = news[h]
             total[t, h] = totals[h]
-            mixed[t, h] = mixeds[h]
             acc[t, h] = accs[h]
 
-    def step(n, carry):
-        b, t = n // 2, n & 1
-        base, row, needed, whole = place(sc, b, t)
-
-        @pl.when(needed & whole)
-        def _():
-            block(b, t, base, row, False)
-
-        @pl.when(needed & jnp.logical_not(whole))
-        def _():
-            block(b, t, base, row, True)
-
-        return carry
-
-    lax.fori_loop(0, 4 * PIECES, step, 0)
+    def direct(b, t, base, row, masked):
+        es = [jnp.exp2(s * unit) for s in scores_of(b, t, base, row, masked)]
+        totals = [total[t, h] + jnp.sum(es[h], axis=0, keepdims=True) for h in heads]
+        accs = [acc[t, h] + dot(t_s[b], es[h].astype(BF16)) for h in heads]
+        for h in heads:
+            total[t, h] = totals[h]
+            acc[t, h] = accs[h]
+
+    def over_blocks(block):
+        def step(n, carry):
+            b, t = n // 2, n & 1
+            base, row, needed, whole = place(sc, b, t)
+
+            @pl.when(needed & whole)
+            def _():
+                block(b, t, base, row, False)
+
+            @pl.when(needed & jnp.logical_not(whole))
+            def _():
+                block(b, t, base, row, True)
+
+            return carry
+
+        lax.fori_loop(0, 4 * PIECES, step, 0)
+
+    @pl.when(small)
+    def _():
+        over_blocks(direct)
+        high[...] = jnp.where(total[...] > 0.0, 0.0, FLOOR)
+
+    @pl.when(jnp.logical_not(small))
+    def _():
+        over_blocks(shifted)
+
     for t in range(TILES):
         for h in heads:
+            product = acc[t, h] * jnp.transpose(do_s[t, h]).astype(F32)
             values[t, h] = (acc[t, h] * (1.0 / jnp.maximum(total[t, h], 1e-30))).astype(BF16)
             stat[t, h : h + 1, :] = high[t, h]
             stat[t, group + h : group + h + 1, :] = total[t, h]
-            stat[t, 2 * group + h : 2 * group + h + 1, :] = mixed[t, h]
+            stat[t, 2 * group + h : 2 * group + h + 1, :] = jnp.sum(product, axis=0, keepdims=True)
 
 
 def backward(group, width, span, begins, ends, sc, q_s, do_s, k_s, v_s, t_s, *refs):
@@ -279,7 +305,7 @@
         in_specs=[SMEM] + [VMEM] * 10,
         out_specs=[VMEM] * 7,
         scratch_shapes=[pltpu.VMEM(turned.shape, BF16), pltpu.VMEM(acc.shape, F32)]
-        + [pltpu.VMEM(line.shape, F32)] * 3,
+        + [pltpu.VMEM(line.shape, F32)] * 2,
         compiler_params=PARAMS,
         cost_estimate=cost(group, width, 3, PIECES),
         name="forward",

time: 113 us -> 114 us (level); the launches traced: 112 us -> 111 us
  waiting for transfers between devices: 32.4 us -> 28.1 us
  starting transfers between devices: 57.4 us -> 60.9 us
    ppermute x1, starting transfers between devices: 5.81 us -> 10.2 us  [local(): gc = send(far.reshape(flat), perm=OPPOSITE)]
    ppermute x1, starting transfers between devices: 3.74 us -> 0.09 us  [local(): gb = send(near_by[2:].reshape(flat), perm=REST)]
    ppermute x1, starting transfers between devices: 2.2 us -> 5.68 us  [local(): ga = send(near_by[:2].reshape(flat), perm=NEAR)]
    ppermute x3, waiting for transfers between devices: 4.94 us -> 2.47 us  [local(): grad = add(grad[0], *[send(grad[n], perm=X[n]) for n in range(1, 4)])]
    ppermute x1, waiting for transfers between devices: 2.67 us -> 0.58 us  [local(): gb = send(near_by[2:].reshape(flat), perm=REST)]
    ppermute x1, starting transfers between devices: 3.56 us -> 2.21 us  [local(): other = send(stat, perm=NEXT)[::-1]]
    ppermute x1, starting transfers between devices: 0.81 us -> 2.01 us  [local(): mixed = [mixed[0], send(mixed[1], perm=NEXT)]]
  transfers between devices with their start and end apart: 29 -> 29, of which waited for: 15 -> 17; matrix products, arithmetic and copies ran while one was open for 3% -> 3% of each run, Pallas kernels for 5% -> 5%
where the time goes in v2:
time: 114 us; the launch traced here: 111 us
  starting transfers between devices  60.9 us (53%)
  waiting for transfers between devices  28.1 us (25%)
  Pallas kernels  17.3 us (15%)
  local copies, waits for them, and re-layouts  3.4 us (3%)
    ppermute x1, starting transfers between devices, local(): gc = send(far.reshape(flat), perm=OPPOSITE)  10.2 us
    pallas_call x3, Pallas kernels, run_backward(): pl.pallas_call(functools.partial(backward, group, width, span, begins, en...  8.19 us
    pallas_call x1, Pallas kernels, run_forward(): pl.pallas_call(functools.partial(forward, group, width), out_shape=[jax.S...  6.53 us
    ppermute x3, waiting for transfers between devices, local(): dq = [dq[0]] + [send(dq[s], perm=Y[s]) for s in range(1, SLOTS)]  6.06 us
    ppermute x2, starting transfers between devices, local(): a, b = (send(key_home, perm=NEAR), send(key_home, perm=REST))  6.02 us
    ppermute x1, starting transfers between devices, local(): ga = send(near_by[:2].reshape(flat), perm=NEAR)  5.68 us
    ppermute x3, waiting for transfers between devices, local(): keys = [held] + [send(held, perm=X[n]) for n in range(1, 4)]  5.56 us
    ppermute x3, starting transfers between devices, local(): grad = add(grad[0], *[send(grad[n], perm=X[n]) for n in range(1, 4)])  4.81 us
  transfers between devices with their start and end apart: 29, of which 17 were waited for; matrix products, arithmetic and copies ran while one was open for 3% of the time, Pallas kernels for 5%

profile of v2, /device:TPU:32, one launch (start us, length us, event | category | flops | bytes accessed | tf_op | source)
XLA Modules:
  0.0 111.5 jit_solution(5079179331972906989)
XLA Ops:
  4.3 4.6 %collective-permute-start.2 = (bf16[128,256]{1,0:T(8,128)(2,1)}, bf16[128,256]{1,0:T(8,128)(2,1)S(1)}, u32[]{:S(2)}, u32[]{:S(2)}) collective-permute-start(bf16[128,256]{1,0:T(8,128)(2,1)} %get-tuple-element.52), channel_id=1, source_target_pairs={{0,192},{2,194},{4,196},{6,198},{8,200},{10,202},{12,204},{14,206}... | collective-permute-start | bytes 196616 | tf_op jit(solution)/shard_map/ppermute | solution.py:358
  11.7 3.4 %collective-permute-done.1 = bf16[128,256]{1,0:T(8,128)(2,1)S(1)} collective-permute-done((bf16[128,256]{1,0:T(8,128)(2,1)}, bf16[128,256]{1,0:T(8,128)(2,1)S(1)}, u32[]{:S(2)}, u32[]{:S(2)}) %collective-permute-start.1) | collective-permute-done | bytes 65568 | tf_op jit(solution)/shard_map/ppermute | solution.py:358
  15.1 3.1 %collective-permute-start.4 = (bf16[256,1024]{1,0:T(8,128)(2,1)S(1)}, bf16[256,1024]{1,0:T(8,128)(2,1)S(1)}, u32[]{:S(2)}, u32[]{:S(2)}) collective-permute-start(bf16[256,1024]{1,0:T(8,128)(2,1)S(1)} %constant_dynamic-update-slice_fusion), channel_id=1, source_target_pairs={{0,6},{2,4},{4,2},{6,0},{8,14},{10,12},{12,10},{14,8},{16,22},{18,... | collective-permute-start | bytes 1572872 | tf_op jit(solution)/shard_map/ppermute | solution.py:361
  19.2 4.2 %collective-permute-start.7 = (bf16[128,256]{1,0:T(8,128)(2,1)S(1)}, bf16[128,256]{1,0:T(8,128)(2,1)S(1)}, u32[]{:S(2)}, u32[]{:S(2)}) collective-permute-start(bf16[128,256]{1,0:T(8,128)(2,1)S(1)} %collective-permute-done.2), channel_id=1, source_target_pairs={{0,64},{2,66},{4,68},{6,70},{8,72},{10,74},{12,76},{14,78},{16,80}... | collective-permute-start | bytes 196616 | tf_op jit(solution)/shard_map/ppermute | solution.py:362
  23.5 2.2 %collective-permute-done.7 = bf16[128,256]{1,0:T(8,128)(2,1)S(1)} collective-permute-done((bf16[128,256]{1,0:T(8,128)(2,1)S(1)}, bf16[128,256]{1,0:T(8,128)(2,1)S(1)}, u32[]{:S(2)}, u32[]{:S(2)}) %collective-permute-start.7) | collective-permute-done | bytes 65568 | tf_op jit(solution)/shard_map/ppermute | solution.py:362
  25.7 2.8 %collective-permute-start.10 = (bf16[512,256]{1,0:T(8,128)(2,1)S(1)}, bf16[512,256]{1,0:T(8,128)(2,1)S(1)}, u32[]{:S(2)}, u32[]{:S(2)}) collective-permute-start(bf16[512,256]{1,0:T(8,128)(2,1)S(1)} %constant_dynamic-update-slice_fusion.2.refs_6_), channel_id=1, source_target_pairs={{0,24},{2,26},{4,28},{6,30},{8,16},{10,18},{12,20},{14,22},{16,8},... | collective-permute-start | bytes 786440 | tf_op jit(solution)/shard_map/ppermute | solution.py:363
  33.5 4.1 %collective-permute-done.10.refs_9_ = bf16[512,256]{1,0:T(8,128)(2,1)S(1)} collective-permute-done((bf16[512,256]{1,0:T(8,128)(2,1)S(1)}, bf16[512,256]{1,0:T(8,128)(2,1)S(1)}, u32[]{:S(2)}, u32[]{:S(2)}) %collective-permute-start.10) | collective-permute-done | bytes 262176 | tf_op jit(solution)/shard_map/ppermute | solution.py:363
  40.3 6.5 %forward.1 = (bf16[2,4,128,512]{3,2,1,0:T(8,128)(2,1)S(1)}, f32[2,12,512]{2,1,0:T(8,128)S(1)}, bf16[2,4,512,128]{3,2,1,0:T(8,128)(2,1)S(1)}, bf16[2,4,512,128]{3...) custom-call(s32[16]{0:T(128)S(1)} %concatenate.12.sc, ...), custom_call_target="tpu_custom_call" | custom-call | flops 12884901888 | bytes 8388608 | tf_op jit(solution)/shard_map/forward/pallas_call | solution.py:302
  46.8 2.2 %collective-permute-start.11 = (f32[2,12,512]{2,1,0:T(8,128)S(1)}, f32[2,12,512]{2,1,0:T(8,128)S(1)}, u32[]{:S(2)}, u32[]{:S(2)}) collective-permute-start(f32[2,12,512]{2,1,0:T(8,128)S(1)} %get-tuple-element.61.refs_4_), channel_id=1, source_target_pairs={{0,32},{2,34},{4,36},{6,38},{8,40},{10,42},{12,44},{14,46},{16,48}... | collective-permute-start | bytes 147464 | tf_op jit(solution)/shard_map/ppermute | solution.py:375
  49.0 2.2 %collective-permute-done.11 = f32[2,12,512]{2,1,0:T(8,128)S(1)} collective-permute-done((f32[2,12,512]{2,1,0:T(8,128)S(1)}, f32[2,12,512]{2,1,0:T(8,128)S(1)}, u32[]{:S(2)}, u32[]{:S(2)}) %collective-permute-start.11) | collective-permute-done | bytes 49184 | tf_op jit(solution)/shard_map/ppermute | solution.py:375
  51.7 4.0 %collective-permute-start.12 = (f32[2,12,512]{2,1,0:T(8,128)S(1)}, f32[2,12,512]{2,1,0:T(8,128)S(1)}, u32[]{:S(2)}, u32[]{:S(2)}) collective-permute-start(f32[2,12,512]{2,1,0:T(8,128)S(1)} %pad_maximum_fusion.refs_0_), channel_id=1, source_target_pairs={{0,2},{2,0},{4,6},{6,4},{8,10},{10,8},{12,14},{14,12},{16,18},{18,... | collective-permute-start | bytes 147464 | tf_op jit(solution)/shard_map/ppermute | solution.py:387
  55.7 2.1 %collective-permute-done.14.refs_3_ = f32[2,12,512]{2,1,0:T(8,128)S(1)} collective-permute-done((f32[2,12,512]{2,1,0:T(8,128)S(1)}, f32[2,12,512]{2,1,0:T(8,128)S(1)}, u32[]{:S(2)}, u32[]{:S(2)}) %collective-permute-start.14) | collective-permute-done | bytes 49184 | tf_op jit(solution)/shard_map/ppermute | solution.py:387
  59.2 2.8 %backward_begin.1 = (bf16[2,256,256]{2,1,0:T(8,128)(2,1)S(1)}, bf16[2,512,128]{2,1,0:T(8,128)(2,1)S(1)}, bf16[2,512,128]{2,1,0:T(8,128)(2,1)S(1)}, bf16[2,512,12...) custom-call(s32[16]{0:T(128)S(1)} %concatenate.12.sc, ...), custom_call_target="tpu_custom_call" | custom-call | flops 5368709120 | bytes 8388608 | tf_op jit(solution)/shard_map/backward_begin/pallas_call | solution.py:326
  63.4 3.4 %collective-permute-start.17 = (bf16[2,512,128]{2,1,0:T(8,128)(2,1)S(1)}, bf16[2,512,128]{2,1,0:T(8,128)(2,1)S(1)}, u32[]{:S(2)}, u32[]{:S(2)}) collective-permute-start(bf16[2,512,128]{2,1,0:T(8,128)(2,1)S(1)} %get-tuple-element.70), channel_id=1, source_target_pairs={{0,6},{2,4},{4,2},{6,0},{8,14},{10,12},{12,10},{14,8},{16,22},{18,... | collective-permute-start | bytes 786440 | tf_op jit(solution)/shard_map/ppermute | solution.py:394
  66.8 10.2 %collective-permute-start.20 = (bf16[512,256]{1,0:T(8,128)(2,1)S(1)}, bf16[512,256]{1,0:T(8,128)(2,1)S(1)}, u32[]{:S(2)}, u32[]{:S(2)}) collective-permute-start(bf16[512,256]{1,0:T(8,128)(2,1)S(1)} %bitcast.21), channel_id=1, source_target_pairs={{0,128},{2,130},{4,132},{6,134},{8,136},{10,138},{12,140},{14,142}... | collective-permute-start | bytes 786440 | tf_op jit(solution)/shard_map/ppermute | solution.py:393
  77.0 2.7 %backward_middle.1 = (bf16[4,256,256]{2,1,0:T(8,128)(2,1)S(1)}, f32[2,4,128,512]{3,2,1,0:T(8,128)S(1)}, f32[2,4,1,512]{3,2,1,0:T(1,128)S(1)}, f32[2,4,1,512]{3,2,1,0:T(1,128)S(1)}) custom-call(s32[16]{0:T(128)S(1)} %concatenate.12.sc, bf16[2,4,512,128]{3,2,1,0:T(8,128)(2,1)S(1)} %get-tuple-element.56.q_s, ...), custom_call_target="tpu_custom_call" | custom-call | flops 10737418240 | bytes 8388608 | tf_op jit(solution)/shard_map/backward_middle/pallas_call | solution.py:326
  79.8 5.7 %collective-permute-start.18 = (bf16[512,256]{1,0:T(8,128)(2,1)S(1)}, bf16[512,256]{1,0:T(8,128)(2,1)S(1)}, u32[]{:S(2)}, u32[]{:S(2)}) collective-permute-start(bf16[512,256]{1,0:T(8,128)(2,1)S(1)} %bitcast.22), channel_id=1, source_target_pairs={{0,64},{2,66},{4,68},{6,70},{8,72},{10,74},{12,76},{14,78},{16,80}... | collective-permute-start | bytes 786440 | tf_op jit(solution)/shard_map/ppermute | solution.py:397
  85.5 2.7 %backward_end.1 = (bf16[2,256,256]{2,1,0:T(8,128)(2,1)S(1)}, bf16[2,512,128]{2,1,0:T(8,128)(2,1)S(1)}, bf16[2,512,128]{2,1,0:T(8,128)(2,1)S(1)}, bf16[2,512,128]...) custom-call(s32[16]{0:T(128)S(1)} %concatenate.12.sc, bf16[2,4,512,128]{3,2,1,0:T(8,128)(2,1)S(1)} %get-tuple-element.56.q_s, ...), custom_call_target="tpu_custom_call" | custom-call | flops 5368709120 | bytes 8388608 | tf_op jit(solution)/shard_map/backward_end/pallas_call | solution.py:326
  90.3 2.7 %collective-permute-start.23 = (bf16[2,512,128]{2,1,0:T(8,128)(2,1)S(1)}, bf16[2,512,128]{2,1,0:T(8,128)(2,1)S(1)}, u32[]{:S(2)}, u32[]{:S(2)}) collective-permute-start(bf16[2,512,128]{2,1,0:T(8,128)(2,1)S(1)} %get-tuple-element.87), channel_id=1, source_target_pairs={{0,6},{2,4},{4,2},{6,0},{8,14},{10,12},{12,10},{14,8},{16,22},{18,... | collective-permute-start | bytes 786440 | tf_op jit(solution)/shard_map/ppermute | solution.py:400
  94.7 2.9 %collective-permute-done.22 = bf16[2,512,128]{2,1,0:T(8,128)(2,1)S(1)} collective-permute-done((bf16[2,512,128]{2,1,0:T(8,128)(2,1)S(1)}, bf16[2,512,128]{2,1,0:T(8,128)(2,1)S(1)}, u32[]{:S(2)}, u32[]{:S(2)}) %collective-permute-start.22) | collective-permute-done | bytes 262176 | tf_op jit(solution)/shard_map/ppermute | solution.py:400
  97.5 2.7 %collective-permute-done.23 = bf16[2,512,128]{2,1,0:T(8,128)(2,1)S(1)} collective-permute-done((bf16[2,512,128]{2,1,0:T(8,128)(2,1)S(1)}, bf16[2,512,128]{2,1,0:T(8,128)(2,1)S(1)}, u32[]{:S(2)}, u32[]{:S(2)}) %collective-permute-start.23) | collective-permute-done | bytes 262176 | tf_op jit(solution)/shard_map/ppermute | solution.py:400
  102.1 2.1 %collective-permute-start.28 = (bf16[128,256]{1,0:T(8,128)(2,1)S(1)}, bf16[128,256]{1,0:T(8,128)(2,1)S(1)}, u32[]{:S(2)}, u32[]{:S(2)}) collective-permute-start(bf16[128,256]{1,0:T(8,128)(2,1)S(1)} %get-tuple-element.101), channel_id=1, source_target_pairs={{0,24},{2,26},{4,28},{6,30},{8,16},{10,18},{12,20},{14,22},{16,8},... | collective-permute-start | bytes 196616 | tf_op jit(solution)/shard_map/ppermute | solution.py:406
  105.5 2.0 %collective-permute-start.24 = (bf16[512,128]{1,0:T(8,128)(2,1)S(1)}, bf16[512,128]{1,0:T(8,128)(2,1)S(1)}, u32[]{:S(2)}, u32[]{:S(2)}) collective-permute-start(bf16[512,128]{1,0:T(8,128)(2,1)S(1)} %get-tuple-element.105), channel_id=1, source_target_pairs={{0,32},{2,34},{4,36},{6,38},{8,40},{10,42},{12,44},{14,46},{16,48}... | collective-permute-start | bytes 393224 | tf_op jit(solution)/shard_map/ppermute | solution.py:404
  107.6 2.4 %collective-permute-done.27 = bf16[128,256]{1,0:T(8,128)(2,1)S(1)} collective-permute-done((bf16[128,256]{1,0:T(8,128)(2,1)S(1)}, bf16[128,256]{1,0:T(8,128)(2,1)S(1)}, u32[]{:S(2)}, u32[]{:S(2)}) %collective-permute-start.27) | collective-permute-done | bytes 65568 | tf_op jit(solution)/shard_map/ppermute | solution.py:406
  (66 shorter events, 26.9 us)
Async XLA Ops:
  2.4 12.7 %collective-permute-start = (bf16[128,1024]{1,0:T(8,128)(2,1)}, bf16[128,1024]{1,0:T(8,128)(2,1)S(1)}, u32[]{:S(2)}, u32[]{:S(2)}) collective-permute-start(bf16[128,1024]{1,0:T(8,128)(2,1)} %get-tuple-element.51.refs_0_), channel_id=1, source_target_pairs={{0,32},{2,34},{4,36},{6,38},{8,40},{10,42},{12,44},{14,46},{16,48}... | collective-permute-start | bytes 786440 | tf_op jit(solution)/shard_map/ppermute | solution.py:357
  4.3 7.4 %collective-permute-start.2 = (bf16[128,256]{1,0:T(8,128)(2,1)}, bf16[128,256]{1,0:T(8,128)(2,1)S(1)}, u32[]{:S(2)}, u32[]{:S(2)}) collective-permute-start(bf16[128,256]{1,0:T(8,128)(2,1)} %get-tuple-element.52), channel_id=1, source_target_pairs={{0,192},{2,194},{4,196},{6,198},{8,200},{10,202},{12,204},{14,206}... | collective-permute-start | bytes 196616 | tf_op jit(solution)/shard_map/ppermute | solution.py:358
  8.8 6.3 %collective-permute-start.1 = (bf16[128,256]{1,0:T(8,128)(2,1)}, bf16[128,256]{1,0:T(8,128)(2,1)S(1)}, u32[]{:S(2)}, u32[]{:S(2)}) collective-permute-start(bf16[128,256]{1,0:T(8,128)(2,1)} %get-tuple-element.52), channel_id=1, source_target_pairs={{0,64},{2,66},{4,68},{6,70},{8,72},{10,74},{12,76},{14,78},{16,80}... | collective-permute-start | bytes 196616 | tf_op jit(solution)/shard_map/ppermute | solution.py:358
  15.1 14.7 %collective-permute-start.4 = (bf16[256,1024]{1,0:T(8,128)(2,1)S(1)}, bf16[256,1024]{1,0:T(8,128)(2,1)S(1)}, u32[]{:S(2)}, u32[]{:S(2)}) collective-permute-start(bf16[256,1024]{1,0:T(8,128)(2,1)S(1)} %constant_dynamic-update-slice_fusion), channel_id=1, source_target_pairs={{0,6},{2,4},{4,2},{6,0},{8,14},{10,12},{12,10},{14,8},{16,22},{18,... | collective-permute-start | bytes 1572872 | tf_op jit(solution)/shard_map/ppermute | solution.py:361
  18.2 13.6 %collective-permute-start.3 = (bf16[256,1024]{1,0:T(8,128)(2,1)S(1)}, bf16[256,1024]{1,0:T(8,128)(2,1)S(1)}, u32[]{:S(2)}, u32[]{:S(2)}) collective-permute-start(bf16[256,1024]{1,0:T(8,128)(2,1)S(1)} %constant_dynamic-update-slice_fusion), channel_id=1, source_target_pairs={{0,2},{2,0},{4,6},{6,4},{8,10},{10,8},{12,14},{14,12},{16,18},{18,... | collective-permute-start | bytes 1572872 | tf_op jit(solution)/shard_map/ppermute | solution.py:361
  19.2 6.5 %collective-permute-start.7 = (bf16[128,256]{1,0:T(8,128)(2,1)S(1)}, bf16[128,256]{1,0:T(8,128)(2,1)S(1)}, u32[]{:S(2)}, u32[]{:S(2)}) collective-permute-start(bf16[128,256]{1,0:T(8,128)(2,1)S(1)} %collective-permute-done.2), channel_id=1, source_target_pairs={{0,64},{2,66},{4,68},{6,70},{8,72},{10,74},{12,76},{14,78},{16,80}... | collective-permute-start | bytes 196616 | tf_op jit(solution)/shard_map/ppermute | solution.py:362
  25.7 11.9 %collective-permute-start.10 = (bf16[512,256]{1,0:T(8,128)(2,1)S(1)}, bf16[512,256]{1,0:T(8,128)(2,1)S(1)}, u32[]{:S(2)}, u32[]{:S(2)}) collective-permute-start(bf16[512,256]{1,0:T(8,128)(2,1)S(1)} %constant_dynamic-update-slice_fusion.2.refs_6_), channel_id=1, source_target_pairs={{0,24},{2,26},{4,28},{6,30},{8,16},{10,18},{12,20},{14,22},{16,8},... | collective-permute-start | bytes 786440 | tf_op jit(solution)/shard_map/ppermute | solution.py:363
  28.4 10.0 %collective-permute-start.9 = (bf16[512,256]{1,0:T(8,128)(2,1)S(1)}, bf16[512,256]{1,0:T(8,128)(2,1)S(1)}, u32[]{:S(2)}, u32[]{:S(2)}) collective-permute-start(bf16[512,256]{1,0:T(8,128)(2,1)S(1)} %constant_dynamic-update-slice_fusion.2.refs_6_), channel_id=1, source_target_pairs={{0,8},{2,10},{4,12},{6,14},{8,0},{10,2},{12,4},{14,6},{16,24},{18,... | collective-permute-start | bytes 786440 | tf_op jit(solution)/shard_map/ppermute | solution.py:363
  29.2 9.8 %collective-permute-start.8 = (bf16[512,256]{1,0:T(8,128)(2,1)S(1)}, bf16[512,256]{1,0:T(8,128)(2,1)S(1)}, u32[]{:S(2)}, u32[]{:S(2)}) collective-permute-start(bf16[512,256]{1,0:T(8,128)(2,1)S(1)} %constant_dynamic-update-slice_fusion.2.refs_6_), channel_id=1, source_target_pairs={{0,16},{2,18},{4,20},{6,22},{8,24},{10,26},{12,28},{14,30},{16,0},... | collective-permute-start | bytes 786440 | tf_op jit(solution)/shard_map/ppermute | solution.py:363
  29.8 9.2 %collective-permute-start.5 = (bf16[128,1024]{1,0:T(8,128)(2,1)S(1)}, bf16[128,1024]{1,0:T(8,128)(2,1)S(1)}, u32[]{:S(2)}, u32[]{:S(2)}) collective-permute-start(bf16[128,1024]{1,0:T(8,128)(2,1)S(1)} %slice.98), channel_id=1, source_target_pairs={{0,2},{2,0},{4,6},{6,4},{8,10},{10,8},{12,14},{14,12},{16,18},{18,... | collective-permute-start | bytes 786440 | tf_op jit(solution)/shard_map/ppermute | solution.py:364
  32.5 7.8 %collective-permute-start.6 = (bf16[128,1024]{1,0:T(8,128)(2,1)}, bf16[128,1024]{1,0:T(8,128)(2,1)S(1)}, u32[]{:S(2)}, u32[]{:S(2)}) collective-permute-start(bf16[128,1024]{1,0:T(8,128)(2,1)} %slice.99), channel_id=1, source_target_pairs={{0,6},{2,4},{4,2},{6,0},{8,14},{10,12},{12,10},{14,8},{16,22},{18,... | collective-permute-start | bytes 786440 | tf_op jit(solution)/shard_map/ppermute | solution.py:364
  51.4 6.4 %collective-permute-start.14 = (f32[2,12,512]{2,1,0:T(8,128)S(1)}, f32[2,12,512]{2,1,0:T(8,128)S(1)}, u32[]{:S(2)}, u32[]{:S(2)}) collective-permute-start(f32[2,12,512]{2,1,0:T(8,128)S(1)} %pad_maximum_fusion.refs_0_), channel_id=1, source_target_pairs={{0,6},{2,4},{4,2},{6,0},{8,14},{10,12},{12,10},{14,8},{16,22},{18,... | collective-permute-start | bytes 147464 | tf_op jit(solution)/shard_map/ppermute | solution.py:387
  51.7 7.4 %collective-permute-start.12 = (f32[2,12,512]{2,1,0:T(8,128)S(1)}, f32[2,12,512]{2,1,0:T(8,128)S(1)}, u32[]{:S(2)}, u32[]{:S(2)}) collective-permute-start(f32[2,12,512]{2,1,0:T(8,128)S(1)} %pad_maximum_fusion.refs_0_), channel_id=1, source_target_pairs={{0,2},{2,0},{4,6},{6,4},{8,10},{10,8},{12,14},{14,12},{16,18},{18,... | collective-permute-start | bytes 147464 | tf_op jit(solution)/shard_map/ppermute | solution.py:387
  62.0 17.7 %collective-permute-start.15 = (bf16[2,512,128]{2,1,0:T(8,128)(2,1)S(1)}, bf16[2,512,128]{2,1,0:T(8,128)(2,1)S(1)}, u32[]{:S(2)}, u32[]{:S(2)}) collective-permute-start(bf16[2,512,128]{2,1,0:T(8,128)(2,1)S(1)} %get-tuple-element.68), channel_id=1, source_target_pairs={{0,2},{2,0},{4,6},{6,4},{8,10},{10,8},{12,14},{14,12},{16,18},{18,... | collective-permute-start | bytes 786440 | tf_op jit(solution)/shard_map/ppermute | solution.py:394
  62.1 17.6 %collective-permute-start.16 = (bf16[2,512,128]{2,1,0:T(8,128)(2,1)S(1)}, bf16[2,512,128]{2,1,0:T(8,128)(2,1)S(1)}, u32[]{:S(2)}, u32[]{:S(2)}) collective-permute-start(bf16[2,512,128]{2,1,0:T(8,128)(2,1)S(1)} %get-tuple-element.69), channel_id=1, source_target_pairs={{0,4},{2,6},{4,0},{6,2},{8,12},{10,14},{12,8},{14,10},{16,20},{18,... | collective-permute-start | bytes 786440 | tf_op jit(solution)/shard_map/ppermute | solution.py:394
  63.4 16.3 %collective-permute-start.17 = (bf16[2,512,128]{2,1,0:T(8,128)(2,1)S(1)}, bf16[2,512,128]{2,1,0:T(8,128)(2,1)S(1)}, u32[]{:S(2)}, u32[]{:S(2)}) collective-permute-start(bf16[2,512,128]{2,1,0:T(8,128)(2,1)S(1)} %get-tuple-element.70), channel_id=1, source_target_pairs={{0,6},{2,4},{4,2},{6,0},{8,14},{10,12},{12,10},{14,8},{16,22},{18,... | collective-permute-start | bytes 786440 | tf_op jit(solution)/shard_map/ppermute | solution.py:394
  66.8 23.5 %collective-permute-start.20 = (bf16[512,256]{1,0:T(8,128)(2,1)S(1)}, bf16[512,256]{1,0:T(8,128)(2,1)S(1)}, u32[]{:S(2)}, u32[]{:S(2)}) collective-permute-start(bf16[512,256]{1,0:T(8,128)(2,1)S(1)} %bitcast.21), channel_id=1, source_target_pairs={{0,128},{2,130},{4,132},{6,134},{8,136},{10,138},{12,140},{14,142}... | collective-permute-start | bytes 786440 | tf_op jit(solution)/shard_map/ppermute | solution.py:393
  79.7 13.8 %collective-permute-start.19 = (bf16[512,256]{1,0:T(8,128)(2,1)S(1)}, bf16[512,256]{1,0:T(8,128)(2,1)S(1)}, u32[]{:S(2)}, u32[]{:S(2)}) collective-permute-start(bf16[512,256]{1,0:T(8,128)(2,1)S(1)} %bitcast.23), channel_id=1, source_target_pairs={{0,192},{2,194},{4,196},{6,198},{8,200},{10,202},{12,204},{14,206}... | collective-permute-start | bytes 786440 | tf_op jit(solution)/shard_map/ppermute | solution.py:398
  79.8 14.2 %collective-permute-start.18 = (bf16[512,256]{1,0:T(8,128)(2,1)S(1)}, bf16[512,256]{1,0:T(8,128)(2,1)S(1)}, u32[]{:S(2)}, u32[]{:S(2)}) collective-permute-start(bf16[512,256]{1,0:T(8,128)(2,1)S(1)} %bitcast.22), channel_id=1, source_target_pairs={{0,64},{2,66},{4,68},{6,70},{8,72},{10,74},{12,76},{14,78},{16,80}... | collective-permute-start | bytes 786440 | tf_op jit(solution)/shard_map/ppermute | solution.py:397
  88.2 6.5 %collective-permute-start.21 = (bf16[2,512,128]{2,1,0:T(8,128)(2,1)S(1)}, bf16[2,512,128]{2,1,0:T(8,128)(2,1)S(1)}, u32[]{:S(2)}, u32[]{:S(2)}) collective-permute-start(bf16[2,512,128]{2,1,0:T(8,128)(2,1)S(1)} %get-tuple-element.85), channel_id=1, source_target_pairs={{0,2},{2,0},{4,6},{6,4},{8,10},{10,8},{12,14},{14,12},{16,18},{18,... | collective-permute-start | bytes 786440 | tf_op jit(solution)/shard_map/ppermute | solution.py:400
  88.3 9.2 %collective-permute-start.22 = (bf16[2,512,128]{2,1,0:T(8,128)(2,1)S(1)}, bf16[2,512,128]{2,1,0:T(8,128)(2,1)S(1)}, u32[]{:S(2)}, u32[]{:S(2)}) collective-permute-start(bf16[2,512,128]{2,1,0:T(8,128)(2,1)S(1)} %get-tuple-element.86), channel_id=1, source_target_pairs={{0,4},{2,6},{4,0},{6,2},{8,12},{10,14},{12,8},{14,10},{16,20},{18,... | collective-permute-start | bytes 786440 | tf_op jit(solution)/shard_map/ppermute | solution.py:400
  90.3 10.0 %collective-permute-start.23 = (bf16[2,512,128]{2,1,0:T(8,128)(2,1)S(1)}, bf16[2,512,128]{2,1,0:T(8,128)(2,1)S(1)}, u32[]{:S(2)}, u32[]{:S(2)}) collective-permute-start(bf16[2,512,128]{2,1,0:T(8,128)(2,1)S(1)} %get-tuple-element.87), channel_id=1, source_target_pairs={{0,6},{2,4},{4,2},{6,0},{8,14},{10,12},{12,10},{14,8},{16,22},{18,... | collective-permute-start | bytes 786440 | tf_op jit(solution)/shard_map/ppermute | solution.py:400
  100.6 10.1 %collective-permute-start.25 = (bf16[512,128]{1,0:T(8,128)(2,1)S(1)}, bf16[512,128]{1,0:T(8,128)(2,1)S(1)}, u32[]{:S(2)}, u32[]{:S(2)}) collective-permute-start(bf16[512,128]{1,0:T(8,128)(2,1)S(1)} %get-tuple-element.103), channel_id=1, source_target_pairs={{0,32},{2,34},{4,36},{6,38},{8,40},{10,42},{12,44},{14,46},{16,48}... | collective-permute-start | bytes 393224 | tf_op jit(solution)/shard_map/ppermute | solution.py:408
  100.7 6.8 %collective-permute-start.26 = (bf16[128,256]{1,0:T(8,128)(2,1)S(1)}, bf16[128,256]{1,0:T(8,128)(2,1)S(1)}, u32[]{:S(2)}, u32[]{:S(2)}) collective-permute-start(bf16[128,256]{1,0:T(8,128)(2,1)S(1)} %get-tuple-element.100), channel_id=1, source_target_pairs={{0,16},{2,18},{4,20},{6,22},{8,24},{10,26},{12,28},{14,30},{16,0},... | collective-permute-start | bytes 196616 | tf_op jit(solution)/shard_map/ppermute | solution.py:406
  (7 other events, 97.4 us)

commit v3 on v2

--- a/solution.py
+++ b/solution.py
@@ -393,18 +393,20 @@
     gc = send(far.reshape(flat), perm=OPPOSITE)
     mixed = [mixed[0]] + [send(mixed[s], perm=Y[s]) for s in range(1, SLOTS)]
     near_by, *carried = back((1, 3), False, False, sc, held, *carried)
-    near_by, mixed, carried = lax.optimization_barrier((near_by, mixed, carried))
+    near_by, carried = lax.optimization_barrier((near_by, carried))
     ga = send(near_by[:2].reshape(flat), perm=NEAR)
     gb = send(near_by[2:].reshape(flat), perm=REST)
     close, *dq = back((0, 1), False, True, sc, held, *carried)
+    close, dq, mixed = lax.optimization_barrier((close, dq, mixed))
     dq = [dq[0]] + [send(dq[s], perm=Y[s]) for s in range(1, SLOTS)]
     grad = add(close.reshape(flat), ga, gb, gc)
-    _, mixed, dq = lax.optimization_barrier((grad, mixed, dq))
+    _, mixed = lax.optimization_barrier((grad, mixed))
+    grad = grad.reshape(4, CHUNK, 2 * width)
+    grad = [grad[0]] + [send(grad[n], perm=X[n]) for n in range(1, 4)]
     mixed = add(*mixed)
     mixed = [mixed[0], send(mixed[1], perm=NEXT)]
-    grad = grad.reshape(4, CHUNK, 2 * width)
-    grad = add(grad[0], *[send(grad[n], perm=X[n]) for n in range(1, 4)])
-    dq = add(*dq)
+    grad, dq = lax.optimization_barrier((grad, dq))
+    grad, dq = add(*grad), add(*dq)
     dq = [dq[0], send(dq[1], perm=NEXT)]
     out_shape = jax.ShapeDtypeStruct((CHUNK, group * width), BF16)
     attended, grad_query = pl.pallas_call(

time: 114 us -> 112 us (0.982)
  starting transfers between devices: 60.9 us -> 51.9 us
  waiting for transfers between devices: 28.1 us -> 33.3 us
  Pallas kernels: 17.3 us -> 19.8 us
    ppermute x3, waiting for transfers between devices: 6.06 us -> 0.01 us  [local(): dq = [dq[0]] + [send(dq[s], perm=Y[s]) for s in range(1, SLOTS)]]
    ppermute x3, starting transfers between devices: 4.78 us -> 0.65 us  [local(): dq = [dq[0]] + [send(dq[s], perm=Y[s]) for s in range(1, SLOTS)]]
    ppermute x1, waiting for transfers between devices: 0.01 us -> 4.13 us  [local(): gc = send(far.reshape(flat), perm=OPPOSITE)]
    ppermute x3, waiting for transfers between devices: 2.47 us -> 6.47 us  [local(): grad = [grad[0]] + [send(grad[n], perm=X[n]) for n in range(1, 4)]]
    ppermute x1, waiting for transfers between devices: 0.01 us -> 2.33 us  [local(): mixed = [mixed[0], send(mixed[1], perm=NEXT)]]
    ppermute x1, starting transfers between devices: 5.68 us -> 3.74 us  [local(): ga = send(near_by[:2].reshape(flat), perm=NEAR)]
    ppermute x1, starting transfers between devices: 2.01 us -> 0.52 us  [local(): mixed = [mixed[0], send(mixed[1], perm=NEXT)]]
    ppermute x1, starting transfers between devices: 10.2 us -> 8.74 us  [local(): gc = send(far.reshape(flat), perm=OPPOSITE)]
  transfers between devices with their start and end apart: 29 -> 29, of which waited for: 17 -> 17; matrix products, arithmetic and copies ran while one was open for 3% -> 4% of each run, Pallas kernels for 5% -> 6%
where the time goes in v3:
time: 112 us; the launch traced here: 110 us
  starting transfers between devices  51.9 us (46%)
  waiting for transfers between devices  33.3 us (30%)
  Pallas kernels  19.8 us (18%)
  local copies, waits for them, and re-layouts  3.4 us (3%)
    pallas_call x3, Pallas kernels, run_backward(): pl.pallas_call(functools.partial(backward, group, width, span, begins, en...  9.64 us
    ppermute x1, starting transfers between devices, local(): gc = send(far.reshape(flat), perm=OPPOSITE)  8.74 us
    pallas_call x1, Pallas kernels, run_forward(): pl.pallas_call(functools.partial(forward, group, width), out_shape=[jax.S...  7.61 us
    ppermute x3, waiting for transfers between devices, local(): grad = [grad[0]] + [send(grad[n], perm=X[n]) for n in range(1, 4)]  6.47 us
    ppermute x2, starting transfers between devices, local(): a, b = (send(key_home, perm=NEAR), send(key_home, perm=REST))  6.02 us
    ppermute x3, waiting for transfers between devices, local(): keys = [held] + [send(held, perm=X[n]) for n in range(1, 4)]  5.57 us
    ppermute x3, starting transfers between devices, local(): mixed = [mixed[0]] + [send(mixed[s], perm=Y[s]) for s in range(1, SLOTS)]  4.78 us
    ppermute x3, starting transfers between devices, local(): stats = [merged] + [send(merged, perm=Y[s]) for s in range(1, SLOTS)]  4.35 us
  transfers between devices with their start and end apart: 29, of which 17 were waited for; matrix products, arithmetic and copies ran while one was open for 4% of the time, Pallas kernels for 6%

profile of v3, /device:TPU:32, one launch (start us, length us, event | category | flops | bytes accessed | tf_op | source)
XLA Modules:
  0.0 110.2 jit_solution(9063279241140553879)
XLA Ops:
  4.3 4.6 %collective-permute-start.2 = (bf16[128,256]{1,0:T(8,128)(2,1)}, bf16[128,256]{1,0:T(8,128)(2,1)S(1)}, u32[]{:S(2)}, u32[]{:S(2)}) collective-permute-start(bf16[128,256]{1,0:T(8,128)(2,1)} %get-tuple-element.57), channel_id=1, source_target_pairs={{0,192},{2,194},{4,196},{6,198},{8,200},{10,202},{12,204},{14,206}... | collective-permute-start | bytes 196616 | tf_op jit(solution)/shard_map/ppermute | solution.py:358
  11.7 3.4 %collective-permute-done.1 = bf16[128,256]{1,0:T(8,128)(2,1)S(1)} collective-permute-done((bf16[128,256]{1,0:T(8,128)(2,1)}, bf16[128,256]{1,0:T(8,128)(2,1)S(1)}, u32[]{:S(2)}, u32[]{:S(2)}) %collective-permute-start.1) | collective-permute-done | bytes 65568 | tf_op jit(solution)/shard_map/ppermute | solution.py:358
  15.1 3.1 %collective-permute-start.4 = (bf16[256,1024]{1,0:T(8,128)(2,1)S(1)}, bf16[256,1024]{1,0:T(8,128)(2,1)S(1)}, u32[]{:S(2)}, u32[]{:S(2)}) collective-permute-start(bf16[256,1024]{1,0:T(8,128)(2,1)S(1)} %constant_dynamic-update-slice_fusion), channel_id=1, source_target_pairs={{0,6},{2,4},{4,2},{6,0},{8,14},{10,12},{12,10},{14,8},{16,22},{18,... | collective-permute-start | bytes 1572872 | tf_op jit(solution)/shard_map/ppermute | solution.py:361
  19.2 4.2 %collective-permute-start.7 = (bf16[128,256]{1,0:T(8,128)(2,1)S(1)}, bf16[128,256]{1,0:T(8,128)(2,1)S(1)}, u32[]{:S(2)}, u32[]{:S(2)}) collective-permute-start(bf16[128,256]{1,0:T(8,128)(2,1)S(1)} %collective-permute-done.2), channel_id=1, source_target_pairs={{0,64},{2,66},{4,68},{6,70},{8,72},{10,74},{12,76},{14,78},{16,80}... | collective-permute-start | bytes 196616 | tf_op jit(solution)/shard_map/ppermute | solution.py:362
  23.5 2.2 %collective-permute-done.7 = bf16[128,256]{1,0:T(8,128)(2,1)S(1)} collective-permute-done((bf16[128,256]{1,0:T(8,128)(2,1)S(1)}, bf16[128,256]{1,0:T(8,128)(2,1)S(1)}, u32[]{:S(2)}, u32[]{:S(2)}) %collective-permute-start.7) | collective-permute-done | bytes 65568 | tf_op jit(solution)/shard_map/ppermute | solution.py:362
  25.7 2.8 %collective-permute-start.10 = (bf16[512,256]{1,0:T(8,128)(2,1)S(1)}, bf16[512,256]{1,0:T(8,128)(2,1)S(1)}, u32[]{:S(2)}, u32[]{:S(2)}) collective-permute-start(bf16[512,256]{1,0:T(8,128)(2,1)S(1)} %constant_dynamic-update-slice_fusion.2.refs_6_), channel_id=1, source_target_pairs={{0,24},{2,26},{4,28},{6,30},{8,16},{10,18},{12,20},{14,22},{16,8},... | collective-permute-start | bytes 786440 | tf_op jit(solution)/shard_map/ppermute | solution.py:363
  29.8 2.0 %collective-permute-start.5 = (bf16[128,1024]{1,0:T(8,128)(2,1)S(1)}, bf16[128,1024]{1,0:T(8,128)(2,1)S(1)}, u32[]{:S(2)}, u32[]{:S(2)}) collective-permute-start(bf16[128,1024]{1,0:T(8,128)(2,1)S(1)} %slice.98), channel_id=1, source_target_pairs={{0,2},{2,0},{4,6},{6,4},{8,10},{10,8},{12,14},{14,12},{16,18},{18,... | collective-permute-start | bytes 786440 | tf_op jit(solution)/shard_map/ppermute | solution.py:364
  33.5 4.1 %collective-permute-done.10.refs_9_ = bf16[512,256]{1,0:T(8,128)(2,1)S(1)} collective-permute-done((bf16[512,256]{1,0:T(8,128)(2,1)S(1)}, bf16[512,256]{1,0:T(8,128)(2,1)S(1)}, u32[]{:S(2)}, u32[]{:S(2)}) %collective-permute-start.10) | collective-permute-done | bytes 262176 | tf_op jit(solution)/shard_map/ppermute | solution.py:363
  40.3 7.6 %forward.1 = (bf16[2,4,128,512]{3,2,1,0:T(8,128)(2,1)S(1)}, f32[2,12,512]{2,1,0:T(8,128)S(1)}, bf16[2,4,512,128]{3,2,1,0:T(8,128)(2,1)S(1)}, bf16[2,4,512,128]{3...) custom-call(s32[16]{0:T(128)S(1)} %concatenate.12.sc, ...), custom_call_target="tpu_custom_call" | custom-call | flops 12884901888 | bytes 8388608 | tf_op jit(solution)/shard_map/forward/pallas_call | solution.py:302
  47.9 2.2 %collective-permute-start.11 = (f32[2,12,512]{2,1,0:T(8,128)S(1)}, f32[2,12,512]{2,1,0:T(8,128)S(1)}, u32[]{:S(2)}, u32[]{:S(2)}) collective-permute-start(f32[2,12,512]{2,1,0:T(8,128)S(1)} %get-tuple-element.66.refs_4_), channel_id=1, source_target_pairs={{0,32},{2,34},{4,36},{6,38},{8,40},{10,42},{12,44},{14,46},{16,48}... | collective-permute-start | bytes 147464 | tf_op jit(solution)/shard_map/ppermute | solution.py:375
  50.1 2.2 %collective-permute-done.11 = f32[2,12,512]{2,1,0:T(8,128)S(1)} collective-permute-done((f32[2,12,512]{2,1,0:T(8,128)S(1)}, f32[2,12,512]{2,1,0:T(8,128)S(1)}, u32[]{:S(2)}, u32[]{:S(2)}) %collective-permute-start.11) | collective-permute-done | bytes 49184 | tf_op jit(solution)/shard_map/ppermute | solution.py:375
  52.8 4.0 %collective-permute-start.12 = (f32[2,12,512]{2,1,0:T(8,128)S(1)}, f32[2,12,512]{2,1,0:T(8,128)S(1)}, u32[]{:S(2)}, u32[]{:S(2)}) collective-permute-start(f32[2,12,512]{2,1,0:T(8,128)S(1)} %pad_maximum_fusion.refs_0_), channel_id=1, source_target_pairs={{0,2},{2,0},{4,6},{6,4},{8,10},{10,8},{12,14},{14,12},{16,18},{18,... | collective-permute-start | bytes 147464 | tf_op jit(solution)/shard_map/ppermute | solution.py:387
  56.8 2.1 %collective-permute-done.14.refs_3_ = f32[2,12,512]{2,1,0:T(8,128)S(1)} collective-permute-done((f32[2,12,512]{2,1,0:T(8,128)S(1)}, f32[2,12,512]{2,1,0:T(8,128)S(1)}, u32[]{:S(2)}, u32[]{:S(2)}) %collective-permute-start.14) | collective-permute-done | bytes 49184 | tf_op jit(solution)/shard_map/ppermute | solution.py:387
  60.4 2.7 %backward_begin.1 = (bf16[2,256,256]{2,1,0:T(8,128)(2,1)S(1)}, bf16[2,512,128]{2,1,0:T(8,128)(2,1)S(1)}, bf16[2,512,128]{2,1,0:T(8,128)(2,1)S(1)}, bf16[2,512,12...) custom-call(s32[16]{0:T(128)S(1)} %concatenate.12.sc, ...), custom_call_target="tpu_custom_call" | custom-call | flops 5368709120 | bytes 8388608 | tf_op jit(solution)/shard_map/backward_begin/pallas_call | solution.py:326
  64.5 3.4 %collective-permute-start.17 = (bf16[2,512,128]{2,1,0:T(8,128)(2,1)S(1)}, bf16[2,512,128]{2,1,0:T(8,128)(2,1)S(1)}, u32[]{:S(2)}, u32[]{:S(2)}) collective-permute-start(bf16[2,512,128]{2,1,0:T(8,128)(2,1)S(1)} %get-tuple-element.82), channel_id=1, source_target_pairs={{0,6},{2,4},{4,2},{6,0},{8,14},{10,12},{12,10},{14,8},{16,22},{18,... | collective-permute-start | bytes 786440 | tf_op jit(solution)/shard_map/ppermute | solution.py:394
  67.9 8.7 %collective-permute-start.20 = (bf16[512,256]{1,0:T(8,128)(2,1)S(1)}, bf16[512,256]{1,0:T(8,128)(2,1)S(1)}, u32[]{:S(2)}, u32[]{:S(2)}) collective-permute-start(bf16[512,256]{1,0:T(8,128)(2,1)S(1)} %bitcast.21), channel_id=1, source_target_pairs={{0,128},{2,130},{4,132},{6,134},{8,136},{10,138},{12,140},{14,142}... | collective-permute-start | bytes 786440 | tf_op jit(solution)/shard_map/ppermute | solution.py:393
  76.6 4.3 %backward_middle.1 = (bf16[4,256,256]{2,1,0:T(8,128)(2,1)S(1)}, f32[2,4,128,512]{3,2,1,0:T(8,128)S(1)}, f32[2,4,1,512]{3,2,1,0:T(1,128)S(1)}, f32[2,4,1,512]{3,2,1,0:T(1,128)S(1)}) custom-call(s32[16]{0:T(128)S(1)} %concatenate.12.sc, bf16[2,4,512,128]{3,2,1,0:T(8,128)(2,1)S(1)} %get-tuple-element.61.q_s, ...), custom_call_target="tpu_custom_call" | custom-call | flops 10737418240 | bytes 8388608 | tf_op jit(solution)/shard_map/backward_middle/pallas_call | solution.py:326
  81.0 3.7 %collective-permute-start.18 = (bf16[512,256]{1,0:T(8,128)(2,1)S(1)}, bf16[512,256]{1,0:T(8,128)(2,1)S(1)}, u32[]{:S(2)}, u32[]{:S(2)}) collective-permute-start(bf16[512,256]{1,0:T(8,128)(2,1)S(1)} %bitcast.22), channel_id=1, source_target_pairs={{0,64},{2,66},{4,68},{6,70},{8,72},{10,74},{12,76},{14,78},{16,80}... | collective-permute-start | bytes 786440 | tf_op jit(solution)/shard_map/ppermute | solution.py:397
  84.8 2.7 %backward_end.1 = (bf16[2,256,256]{2,1,0:T(8,128)(2,1)S(1)}, bf16[2,512,128]{2,1,0:T(8,128)(2,1)S(1)}, bf16[2,512,128]{2,1,0:T(8,128)(2,1)S(1)}, bf16[2,512,128]...) custom-call(s32[16]{0:T(128)S(1)} %concatenate.12.sc, bf16[2,4,512,128]{3,2,1,0:T(8,128)(2,1)S(1)} %get-tuple-element.61.q_s, ...), custom_call_target="tpu_custom_call" | custom-call | flops 5368709120 | bytes 8388608 | tf_op jit(solution)/shard_map/backward_end/pallas_call | solution.py:326
  87.7 4.1 %collective-permute-done.20 = bf16[512,256]{1,0:T(8,128)(2,1)S(1)} collective-permute-done((bf16[512,256]{1,0:T(8,128)(2,1)S(1)}, bf16[512,256]{1,0:T(8,128)(2,1)S(1)}, u32[]{:S(2)}, u32[]{:S(2)}) %collective-permute-start.20) | collective-permute-done | bytes 262176 | tf_op jit(solution)/shard_map/ppermute | solution.py:393
  92.8 4.1 %collective-permute-start.23 = (bf16[128,256]{1,0:T(8,128)(2,1)S(1)}, bf16[128,256]{1,0:T(8,128)(2,1)S(1)}, u32[]{:S(2)}, u32[]{:S(2)}) collective-permute-start(bf16[128,256]{1,0:T(8,128)(2,1)S(1)} %get-tuple-element.114), channel_id=1, source_target_pairs={{0,24},{2,26},{4,28},{6,30},{8,16},{10,18},{12,20},{14,22},{16,8},... | collective-permute-start | bytes 196616 | tf_op jit(solution)/shard_map/ppermute | solution.py:405
  97.0 2.7 %collective-permute-done.23 = bf16[128,256]{1,0:T(8,128)(2,1)S(1)} collective-permute-done((bf16[128,256]{1,0:T(8,128)(2,1)S(1)}, bf16[128,256]{1,0:T(8,128)(2,1)S(1)}, u32[]{:S(2)}, u32[]{:S(2)}) %collective-permute-start.23) | collective-permute-done | bytes 65568 | tf_op jit(solution)/shard_map/ppermute | solution.py:405
  99.8 2.9 %collective-permute-done.22 = bf16[128,256]{1,0:T(8,128)(2,1)S(1)} collective-permute-done((bf16[128,256]{1,0:T(8,128)(2,1)S(1)}, bf16[128,256]{1,0:T(8,128)(2,1)S(1)}, u32[]{:S(2)}, u32[]{:S(2)}) %collective-permute-start.22) | collective-permute-done | bytes 65568 | tf_op jit(solution)/shard_map/ppermute | solution.py:405
  105.6 2.3 %collective-permute-done.27.refs_2_ = bf16[512,128]{1,0:T(8,128)(2,1)S(1)} collective-permute-done((bf16[512,128]{1,0:T(8,128)(2,1)S(1)}, bf16[512,128]{1,0:T(8,128)(2,1)S(1)}, u32[]{:S(2)}, u32[]{:S(2)}) %collective-permute-start.27) | collective-permute-done | bytes 131104 | tf_op jit(solution)/shard_map/ppermute | solution.py:407
  (67 shorter events, 23.1 us)
Async XLA Ops:
  2.4 12.7 %collective-permute-start = (bf16[128,1024]{1,0:T(8,128)(2,1)}, bf16[128,1024]{1,0:T(8,128)(2,1)S(1)}, u32[]{:S(2)}, u32[]{:S(2)}) collective-permute-start(bf16[128,1024]{1,0:T(8,128)(2,1)} %get-tuple-element.56.refs_0_), channel_id=1, source_target_pairs={{0,32},{2,34},{4,36},{6,38},{8,40},{10,42},{12,44},{14,46},{16,48}... | collective-permute-start | bytes 786440 | tf_op jit(solution)/shard_map/ppermute | solution.py:357
  4.3 7.4 %collective-permute-start.2 = (bf16[128,256]{1,0:T(8,128)(2,1)}, bf16[128,256]{1,0:T(8,128)(2,1)S(1)}, u32[]{:S(2)}, u32[]{:S(2)}) collective-permute-start(bf16[128,256]{1,0:T(8,128)(2,1)} %get-tuple-element.57), channel_id=1, source_target_pairs={{0,192},{2,194},{4,196},{6,198},{8,200},{10,202},{12,204},{14,206}... | collective-permute-start | bytes 196616 | tf_op jit(solution)/shard_map/ppermute | solution.py:358
  8.8 6.3 %collective-permute-start.1 = (bf16[128,256]{1,0:T(8,128)(2,1)}, bf16[128,256]{1,0:T(8,128)(2,1)S(1)}, u32[]{:S(2)}, u32[]{:S(2)}) collective-permute-start(bf16[128,256]{1,0:T(8,128)(2,1)} %get-tuple-element.57), channel_id=1, source_target_pairs={{0,64},{2,66},{4,68},{6,70},{8,72},{10,74},{12,76},{14,78},{16,80}... | collective-permute-start | bytes 196616 | tf_op jit(solution)/shard_map/ppermute | solution.py:358
  15.1 14.7 %collective-permute-start.4 = (bf16[256,1024]{1,0:T(8,128)(2,1)S(1)}, bf16[256,1024]{1,0:T(8,128)(2,1)S(1)}, u32[]{:S(2)}, u32[]{:S(2)}) collective-permute-start(bf16[256,1024]{1,0:T(8,128)(2,1)S(1)} %constant_dynamic-update-slice_fusion), channel_id=1, source_target_pairs={{0,6},{2,4},{4,2},{6,0},{8,14},{10,12},{12,10},{14,8},{16,22},{18,... | collective-permute-start | bytes 1572872 | tf_op jit(solution)/shard_map/ppermute | solution.py:361
  18.2 13.6 %collective-permute-start.3 = (bf16[256,1024]{1,0:T(8,128)(2,1)S(1)}, bf16[256,1024]{1,0:T(8,128)(2,1)S(1)}, u32[]{:S(2)}, u32[]{:S(2)}) collective-permute-start(bf16[256,1024]{1,0:T(8,128)(2,1)S(1)} %constant_dynamic-update-slice_fusion), channel_id=1, source_target_pairs={{0,2},{2,0},{4,6},{6,4},{8,10},{10,8},{12,14},{14,12},{16,18},{18,... | collective-permute-start | bytes 1572872 | tf_op jit(solution)/shard_map/ppermute | solution.py:361
  19.2 6.5 %collective-permute-start.7 = (bf16[128,256]{1,0:T(8,128)(2,1)S(1)}, bf16[128,256]{1,0:T(8,128)(2,1)S(1)}, u32[]{:S(2)}, u32[]{:S(2)}) collective-permute-start(bf16[128,256]{1,0:T(8,128)(2,1)S(1)} %collective-permute-done.2), channel_id=1, source_target_pairs={{0,64},{2,66},{4,68},{6,70},{8,72},{10,74},{12,76},{14,78},{16,80}... | collective-permute-start | bytes 196616 | tf_op jit(solution)/shard_map/ppermute | solution.py:362
  25.7 11.9 %collective-permute-start.10 = (bf16[512,256]{1,0:T(8,128)(2,1)S(1)}, bf16[512,256]{1,0:T(8,128)(2,1)S(1)}, u32[]{:S(2)}, u32[]{:S(2)}) collective-permute-start(bf16[512,256]{1,0:T(8,128)(2,1)S(1)} %constant_dynamic-update-slice_fusion.2.refs_6_), channel_id=1, source_target_pairs={{0,24},{2,26},{4,28},{6,30},{8,16},{10,18},{12,20},{14,22},{16,8},... | collective-permute-start | bytes 786440 | tf_op jit(solution)/shard_map/ppermute | solution.py:363
  28.4 10.0 %collective-permute-start.9 = (bf16[512,256]{1,0:T(8,128)(2,1)S(1)}, bf16[512,256]{1,0:T(8,128)(2,1)S(1)}, u32[]{:S(2)}, u32[]{:S(2)}) collective-permute-start(bf16[512,256]{1,0:T(8,128)(2,1)S(1)} %constant_dynamic-update-slice_fusion.2.refs_6_), channel_id=1, source_target_pairs={{0,8},{2,10},{4,12},{6,14},{8,0},{10,2},{12,4},{14,6},{16,24},{18,... | collective-permute-start | bytes 786440 | tf_op jit(solution)/shard_map/ppermute | solution.py:363
  29.2 9.8 %collective-permute-start.8 = (bf16[512,256]{1,0:T(8,128)(2,1)S(1)}, bf16[512,256]{1,0:T(8,128)(2,1)S(1)}, u32[]{:S(2)}, u32[]{:S(2)}) collective-permute-start(bf16[512,256]{1,0:T(8,128)(2,1)S(1)} %constant_dynamic-update-slice_fusion.2.refs_6_), channel_id=1, source_target_pairs={{0,16},{2,18},{4,20},{6,22},{8,24},{10,26},{12,28},{14,30},{16,0},... | collective-permute-start | bytes 786440 | tf_op jit(solution)/shard_map/ppermute | solution.py:363
  29.8 9.2 %collective-permute-start.5 = (bf16[128,1024]{1,0:T(8,128)(2,1)S(1)}, bf16[128,1024]{1,0:T(8,128)(2,1)S(1)}, u32[]{:S(2)}, u32[]{:S(2)}) collective-permute-start(bf16[128,1024]{1,0:T(8,128)(2,1)S(1)} %slice.98), channel_id=1, source_target_pairs={{0,2},{2,0},{4,6},{6,4},{8,10},{10,8},{12,14},{14,12},{16,18},{18,... | collective-permute-start | bytes 786440 | tf_op jit(solution)/shard_map/ppermute | solution.py:364
  32.5 7.8 %collective-permute-start.6 = (bf16[128,1024]{1,0:T(8,128)(2,1)}, bf16[128,1024]{1,0:T(8,128)(2,1)S(1)}, u32[]{:S(2)}, u32[]{:S(2)}) collective-permute-start(bf16[128,1024]{1,0:T(8,128)(2,1)} %slice.99), channel_id=1, source_target_pairs={{0,6},{2,4},{4,2},{6,0},{8,14},{10,12},{12,10},{14,8},{16,22},{18,... | collective-permute-start | bytes 786440 | tf_op jit(solution)/shard_map/ppermute | solution.py:364
  52.4 6.4 %collective-permute-start.14 = (f32[2,12,512]{2,1,0:T(8,128)S(1)}, f32[2,12,512]{2,1,0:T(8,128)S(1)}, u32[]{:S(2)}, u32[]{:S(2)}) collective-permute-start(f32[2,12,512]{2,1,0:T(8,128)S(1)} %pad_maximum_fusion.refs_0_), channel_id=1, source_target_pairs={{0,6},{2,4},{4,2},{6,0},{8,14},{10,12},{12,10},{14,8},{16,22},{18,... | collective-permute-start | bytes 147464 | tf_op jit(solution)/shard_map/ppermute | solution.py:387
  52.7 6.2 %collective-permute-start.13 = (f32[2,12,512]{2,1,0:T(8,128)S(1)}, f32[2,12,512]{2,1,0:T(8,128)S(1)}, u32[]{:S(2)}, u32[]{:S(2)}) collective-permute-start(f32[2,12,512]{2,1,0:T(8,128)S(1)} %pad_maximum_fusion.refs_0_), channel_id=1, source_target_pairs={{0,4},{2,6},{4,0},{6,2},{8,12},{10,14},{12,8},{14,10},{16,20},{18,... | collective-permute-start | bytes 147464 | tf_op jit(solution)/shard_map/ppermute | solution.py:387
  52.8 7.6 %collective-permute-start.12 = (f32[2,12,512]{2,1,0:T(8,128)S(1)}, f32[2,12,512]{2,1,0:T(8,128)S(1)}, u32[]{:S(2)}, u32[]{:S(2)}) collective-permute-start(f32[2,12,512]{2,1,0:T(8,128)S(1)} %pad_maximum_fusion.refs_0_), channel_id=1, source_target_pairs={{0,2},{2,0},{4,6},{6,4},{8,10},{10,8},{12,14},{14,12},{16,18},{18,... | collective-permute-start | bytes 147464 | tf_op jit(solution)/shard_map/ppermute | solution.py:387
  63.1 17.9 %collective-permute-start.15 = (bf16[2,512,128]{2,1,0:T(8,128)(2,1)S(1)}, bf16[2,512,128]{2,1,0:T(8,128)(2,1)S(1)}, u32[]{:S(2)}, u32[]{:S(2)}) collective-permute-start(bf16[2,512,128]{2,1,0:T(8,128)(2,1)S(1)} %get-tuple-element.80), channel_id=1, source_target_pairs={{0,2},{2,0},{4,6},{6,4},{8,10},{10,8},{12,14},{14,12},{16,18},{18,... | collective-permute-start | bytes 786440 | tf_op jit(solution)/shard_map/ppermute | solution.py:394
  63.2 24.3 %collective-permute-start.16 = (bf16[2,512,128]{2,1,0:T(8,128)(2,1)S(1)}, bf16[2,512,128]{2,1,0:T(8,128)(2,1)S(1)}, u32[]{:S(2)}, u32[]{:S(2)}) collective-permute-start(bf16[2,512,128]{2,1,0:T(8,128)(2,1)S(1)} %get-tuple-element.81), channel_id=1, source_target_pairs={{0,4},{2,6},{4,0},{6,2},{8,12},{10,14},{12,8},{14,10},{16,20},{18,... | collective-permute-start | bytes 786440 | tf_op jit(solution)/shard_map/ppermute | solution.py:394
  64.5 23.0 %collective-permute-start.17 = (bf16[2,512,128]{2,1,0:T(8,128)(2,1)S(1)}, bf16[2,512,128]{2,1,0:T(8,128)(2,1)S(1)}, u32[]{:S(2)}, u32[]{:S(2)}) collective-permute-start(bf16[2,512,128]{2,1,0:T(8,128)(2,1)S(1)} %get-tuple-element.82), channel_id=1, source_target_pairs={{0,6},{2,4},{4,2},{6,0},{8,14},{10,12},{12,10},{14,8},{16,22},{18,... | collective-permute-start | bytes 786440 | tf_op jit(solution)/shard_map/ppermute | solution.py:394
  67.9 24.0 %collective-permute-start.20 = (bf16[512,256]{1,0:T(8,128)(2,1)S(1)}, bf16[512,256]{1,0:T(8,128)(2,1)S(1)}, u32[]{:S(2)}, u32[]{:S(2)}) collective-permute-start(bf16[512,256]{1,0:T(8,128)(2,1)S(1)} %bitcast.21), channel_id=1, source_target_pairs={{0,128},{2,130},{4,132},{6,134},{8,136},{10,138},{12,140},{14,142}... | collective-permute-start | bytes 786440 | tf_op jit(solution)/shard_map/ppermute | solution.py:393
  80.9 11.6 %collective-permute-start.19 = (bf16[512,256]{1,0:T(8,128)(2,1)S(1)}, bf16[512,256]{1,0:T(8,128)(2,1)S(1)}, u32[]{:S(2)}, u32[]{:S(2)}) collective-permute-start(bf16[512,256]{1,0:T(8,128)(2,1)S(1)} %bitcast.23), channel_id=1, source_target_pairs={{0,192},{2,194},{4,196},{6,198},{8,200},{10,202},{12,204},{14,206}... | collective-permute-start | bytes 786440 | tf_op jit(solution)/shard_map/ppermute | solution.py:398
  81.0 11.5 %collective-permute-start.18 = (bf16[512,256]{1,0:T(8,128)(2,1)S(1)}, bf16[512,256]{1,0:T(8,128)(2,1)S(1)}, u32[]{:S(2)}, u32[]{:S(2)}) collective-permute-start(bf16[512,256]{1,0:T(8,128)(2,1)S(1)} %bitcast.22), channel_id=1, source_target_pairs={{0,64},{2,66},{4,68},{6,70},{8,72},{10,74},{12,76},{14,78},{16,80}... | collective-permute-start | bytes 786440 | tf_op jit(solution)/shard_map/ppermute | solution.py:397
  87.5 16.5 %collective-permute-start.24 = (bf16[2,512,128]{2,1,0:T(8,128)(2,1)S(1)}, bf16[2,512,128]{2,1,0:T(8,128)(2,1)S(1)}, u32[]{:S(2)}, u32[]{:S(2)}) collective-permute-start(bf16[2,512,128]{2,1,0:T(8,128)(2,1)S(1)} %get-tuple-element.95), channel_id=1, source_target_pairs={{0,2},{2,0},{4,6},{6,4},{8,10},{10,8},{12,14},{14,12},{16,18},{18,... | collective-permute-start | bytes 786440 | tf_op jit(solution)/shard_map/ppermute | solution.py:401
  87.6 16.4 %collective-permute-start.25 = (bf16[2,512,128]{2,1,0:T(8,128)(2,1)S(1)}, bf16[2,512,128]{2,1,0:T(8,128)(2,1)S(1)}, u32[]{:S(2)}, u32[]{:S(2)}) collective-permute-start(bf16[2,512,128]{2,1,0:T(8,128)(2,1)S(1)} %get-tuple-element.96), channel_id=1, source_target_pairs={{0,4},{2,6},{4,0},{6,2},{8,12},{10,14},{12,8},{14,10},{16,20},{18,... | collective-permute-start | bytes 786440 | tf_op jit(solution)/shard_map/ppermute | solution.py:401
  91.8 12.2 %collective-permute-start.26 = (bf16[2,512,128]{2,1,0:T(8,128)(2,1)S(1)}, bf16[2,512,128]{2,1,0:T(8,128)(2,1)S(1)}, u32[]{:S(2)}, u32[]{:S(2)}) collective-permute-start(bf16[2,512,128]{2,1,0:T(8,128)(2,1)S(1)} %get-tuple-element.97), channel_id=1, source_target_pairs={{0,6},{2,4},{4,2},{6,0},{8,14},{10,12},{12,10},{14,8},{16,22},{18,... | collective-permute-start | bytes 786440 | tf_op jit(solution)/shard_map/ppermute | solution.py:401
  92.8 7.0 %collective-permute-start.23 = (bf16[128,256]{1,0:T(8,128)(2,1)S(1)}, bf16[128,256]{1,0:T(8,128)(2,1)S(1)}, u32[]{:S(2)}, u32[]{:S(2)}) collective-permute-start(bf16[128,256]{1,0:T(8,128)(2,1)S(1)} %get-tuple-element.114), channel_id=1, source_target_pairs={{0,24},{2,26},{4,28},{6,30},{8,16},{10,18},{12,20},{14,22},{16,8},... | collective-permute-start | bytes 196616 | tf_op jit(solution)/shard_map/ppermute | solution.py:405
  (7 other events, 95.3 us)

commit v4 on v3

--- a/solution.py
+++ b/solution.py
@@ -35,8 +35,6 @@
 NEXT = flip(16)
 NEAR = flip(32)
 REST = [(d, (d + (32 if d // 32 % 2 else -32)) % DEVICES) for d in range(DEVICES)]
-
-OPPOSITE = flip(64)
 
 
 def dot(a, b):
@@ -390,16 +388,17 @@
     out = back((3, 4), True, False, sc, held, *stats, stat, values)
     far, mixed, carried = out[0], out[1 : 1 + SLOTS], out[1 + SLOTS :]
     flat = (2 * PAIR, 2 * width)
-    gc = send(far.reshape(flat), perm=OPPOSITE)
+    one, two = send(far[0], perm=NEAR), send(far[1], perm=REST)
     mixed = [mixed[0]] + [send(mixed[s], perm=Y[s]) for s in range(1, SLOTS)]
     near_by, *carried = back((1, 3), False, False, sc, held, *carried)
-    near_by, carried = lax.optimization_barrier((near_by, carried))
-    ga = send(near_by[:2].reshape(flat), perm=NEAR)
-    gb = send(near_by[2:].reshape(flat), perm=REST)
+    ga = jnp.concatenate([near_by[0], add(near_by[1], two)], axis=0)
+    gb = jnp.concatenate([add(near_by[2], one), near_by[3]], axis=0)
+    ga, gb, carried = lax.optimization_barrier((ga, gb, carried))
+    ga, gb = send(ga, perm=NEAR), send(gb, perm=REST)
     close, *dq = back((0, 1), False, True, sc, held, *carried)
     close, dq, mixed = lax.optimization_barrier((close, dq, mixed))
-    dq = [dq[0]] + [send(dq[s], perm=Y[s]) for s in range(1, SLOTS)]
-    grad = add(close.reshape(flat), ga, gb, gc)
+    dq = [dq[0]] + [send(dq[s], perm=Y[s]) for s in (2, 1, 3)]
+    grad = add(close.reshape(flat), ga, gb)
     _, mixed = lax.optimization_barrier((grad, mixed))
     grad = grad.reshape(4, CHUNK, 2 * width)
     grad = [grad[0]] + [send(grad[n], perm=X[n]) for n in range(1, 4)]

time: 112 us -> 112 us (level); the launches traced: 110 us -> 113 us
  starting transfers between devices: 51.9 us -> 59.2 us
  Pallas kernels: 19.8 us -> 14.5 us
    ppermute x3, waiting for transfers between devices: 0.01 us -> 6.13 us  [local(): mixed = [mixed[0]] + [send(mixed[s], perm=Y[s]) for s in range(1, SLOTS)]]
    ppermute x6 -> x7, starting transfers between devices: 13.2 us -> 18.7 us  [the longest x2 12.8 us: local(): one, two = (send(far[0], perm=NEAR), send(far[1], perm=REST))]
    ppermute x6 -> x7, waiting for transfers between devices: 4.39 us -> 0.02 us  [the longest x3 0.01 us: local(): dq = [dq[0]] + [send(dq[s], perm=Y[s]) for s in (2, 1, 3)]]
    pallas_call x3, Pallas kernels: 9.64 us -> 6.58 us  [run_backward(): pl.pallas_call(functools.partial(backward, group, width, span, begins, en...]
    pallas_call x1, Pallas kernels: 7.61 us -> 5.33 us  [run_forward(): pl.pallas_call(functools.partial(forward, group, width), out_shape=[jax.S...]
    ppermute x1, starting transfers between devices: 2.21 us -> 3.54 us  [local(): other = send(stat, perm=NEXT)[::-1]]
  transfers between devices with their start and end apart: 29 -> 30, of which waited for: 17 -> 16; matrix products, arithmetic and copies ran while one was open for 4% -> 4% of each run, Pallas kernels for 6% -> 5%
where the time goes in v4:
time: 112 us; the launch traced here: 113 us
  starting transfers between devices  59.2 us (53%)
  waiting for transfers between devices  34.1 us (30%)
  Pallas kernels  14.5 us (13%)
  local copies, waits for them, and re-layouts  3.42 us (3%)
    ppermute x2, starting transfers between devices, local(): one, two = (send(far[0], perm=NEAR), send(far[1], perm=REST))  12.8 us
    pallas_call x3, Pallas kernels, run_backward(): pl.pallas_call(functools.partial(backward, group, width, span, begins, en...  6.58 us
    ppermute x3, waiting for transfers between devices, local(): grad = [grad[0]] + [send(grad[n], perm=X[n]) for n in range(1, 4)]  6.51 us
    ppermute x3, waiting for transfers between devices, local(): mixed = [mixed[0]] + [send(mixed[s], perm=Y[s]) for s in range(1, SLOTS)]  6.13 us
    ppermute x2, starting transfers between devices, local(): a, b = (send(key_home, perm=NEAR), send(key_home, perm=REST))  6.02 us
    ppermute x3, waiting for transfers between devices, local(): keys = [held] + [send(held, perm=X[n]) for n in range(1, 4)]  5.55 us
    pallas_call x1, Pallas kernels, run_forward(): pl.pallas_call(functools.partial(forward, group, width), out_shape=[jax.S...  5.33 us
    ppermute x3, starting transfers between devices, local(): grad = [grad[0]] + [send(grad[n], perm=X[n]) for n in range(1, 4)]  4.74 us
  transfers between devices with their start and end apart: 30, of which 16 were waited for; matrix products, arithmetic and copies ran while one was open for 4% of the time, Pallas kernels for 5%

profile of v4, /device:TPU:32, one launch (start us, length us, event | category | flops | bytes accessed | tf_op | source)
XLA Modules:
  0.0 113.0 jit_solution(9019561243230567768)
XLA Ops:
  4.3 4.6 %collective-permute-start.2 = (bf16[128,256]{1,0:T(8,128)(2,1)}, bf16[128,256]{1,0:T(8,128)(2,1)S(1)}, u32[]{:S(2)}, u32[]{:S(2)}) collective-permute-start(bf16[128,256]{1,0:T(8,128)(2,1)} %get-tuple-element.62), channel_id=1, source_target_pairs={{0,192},{2,194},{4,196},{6,198},{8,200},{10,202},{12,204},{14,206}... | collective-permute-start | bytes 196616 | tf_op jit(solution)/shard_map/ppermute | solution.py:356
  11.7 3.4 %collective-permute-done.1 = bf16[128,256]{1,0:T(8,128)(2,1)S(1)} collective-permute-done((bf16[128,256]{1,0:T(8,128)(2,1)}, bf16[128,256]{1,0:T(8,128)(2,1)S(1)}, u32[]{:S(2)}, u32[]{:S(2)}) %collective-permute-start.1) | collective-permute-done | bytes 65568 | tf_op jit(solution)/shard_map/ppermute | solution.py:356
  15.1 3.1 %collective-permute-start.4 = (bf16[256,1024]{1,0:T(8,128)(2,1)S(1)}, bf16[256,1024]{1,0:T(8,128)(2,1)S(1)}, u32[]{:S(2)}, u32[]{:S(2)}) collective-permute-start(bf16[256,1024]{1,0:T(8,128)(2,1)S(1)} %constant_dynamic-update-slice_fusion), channel_id=1, source_target_pairs={{0,6},{2,4},{4,2},{6,0},{8,14},{10,12},{12,10},{14,8},{16,22},{18,... | collective-permute-start | bytes 1572872 | tf_op jit(solution)/shard_map/ppermute | solution.py:359
  19.2 4.2 %collective-permute-start.7 = (bf16[128,256]{1,0:T(8,128)(2,1)S(1)}, bf16[128,256]{1,0:T(8,128)(2,1)S(1)}, u32[]{:S(2)}, u32[]{:S(2)}) collective-permute-start(bf16[128,256]{1,0:T(8,128)(2,1)S(1)} %collective-permute-done.2), channel_id=1, source_target_pairs={{0,64},{2,66},{4,68},{6,70},{8,72},{10,74},{12,76},{14,78},{16,80}... | collective-permute-start | bytes 196616 | tf_op jit(solution)/shard_map/ppermute | solution.py:360
  23.5 2.2 %collective-permute-done.7 = bf16[128,256]{1,0:T(8,128)(2,1)S(1)} collective-permute-done((bf16[128,256]{1,0:T(8,128)(2,1)S(1)}, bf16[128,256]{1,0:T(8,128)(2,1)S(1)}, u32[]{:S(2)}, u32[]{:S(2)}) %collective-permute-start.7) | collective-permute-done | bytes 65568 | tf_op jit(solution)/shard_map/ppermute | solution.py:360
  25.7 2.8 %collective-permute-start.10 = (bf16[512,256]{1,0:T(8,128)(2,1)S(1)}, bf16[512,256]{1,0:T(8,128)(2,1)S(1)}, u32[]{:S(2)}, u32[]{:S(2)}) collective-permute-start(bf16[512,256]{1,0:T(8,128)(2,1)S(1)} %constant_dynamic-update-slice_fusion.2.refs_6_), channel_id=1, source_target_pairs={{0,24},{2,26},{4,28},{6,30},{8,16},{10,18},{12,20},{14,22},{16,8},... | collective-permute-start | bytes 786440 | tf_op jit(solution)/shard_map/ppermute | solution.py:361
  33.5 4.1 %collective-permute-done.10.refs_9_ = bf16[512,256]{1,0:T(8,128)(2,1)S(1)} collective-permute-done((bf16[512,256]{1,0:T(8,128)(2,1)S(1)}, bf16[512,256]{1,0:T(8,128)(2,1)S(1)}, u32[]{:S(2)}, u32[]{:S(2)}) %collective-permute-start.10) | collective-permute-done | bytes 262176 | tf_op jit(solution)/shard_map/ppermute | solution.py:361
  40.3 5.3 %forward.1 = (bf16[2,4,128,512]{3,2,1,0:T(8,128)(2,1)S(1)}, f32[2,12,512]{2,1,0:T(8,128)S(1)}, bf16[2,4,512,128]{3,2,1,0:T(8,128)(2,1)S(1)}, bf16[2,4,512,128]{3...) custom-call(s32[16]{0:T(128)S(1)} %concatenate.18.sc, ...), custom_call_target="tpu_custom_call" | custom-call | flops 12884901888 | bytes 8388608 | tf_op jit(solution)/shard_map/forward/pallas_call | solution.py:300
  45.6 3.5 %collective-permute-start.11 = (f32[2,12,512]{2,1,0:T(8,128)S(1)}, f32[2,12,512]{2,1,0:T(8,128)S(1)}, u32[]{:S(2)}, u32[]{:S(2)}) collective-permute-start(f32[2,12,512]{2,1,0:T(8,128)S(1)} %get-tuple-element.71.refs_4_), channel_id=1, source_target_pairs={{0,32},{2,34},{4,36},{6,38},{8,40},{10,42},{12,44},{14,46},{16,48}... | collective-permute-start | bytes 147464 | tf_op jit(solution)/shard_map/ppermute | solution.py:373
  49.2 2.2 %collective-permute-done.11 = f32[2,12,512]{2,1,0:T(8,128)S(1)} collective-permute-done((f32[2,12,512]{2,1,0:T(8,128)S(1)}, f32[2,12,512]{2,1,0:T(8,128)S(1)}, u32[]{:S(2)}, u32[]{:S(2)}) %collective-permute-start.11) | collective-permute-done | bytes 49184 | tf_op jit(solution)/shard_map/ppermute | solution.py:373
  51.9 4.0 %collective-permute-start.12 = (f32[2,12,512]{2,1,0:T(8,128)S(1)}, f32[2,12,512]{2,1,0:T(8,128)S(1)}, u32[]{:S(2)}, u32[]{:S(2)}) collective-permute-start(f32[2,12,512]{2,1,0:T(8,128)S(1)} %pad_maximum_fusion.2.refs_0_), channel_id=1, source_target_pairs={{0,2},{2,0},{4,6},{6,4},{8,10},{10,8},{12,14},{14,12},{16,18},{18,... | collective-permute-start | bytes 147464 | tf_op jit(solution)/shard_map/ppermute | solution.py:385
  55.9 2.1 %collective-permute-done.14.refs_3_ = f32[2,12,512]{2,1,0:T(8,128)S(1)} collective-permute-done((f32[2,12,512]{2,1,0:T(8,128)S(1)}, f32[2,12,512]{2,1,0:T(8,128)S(1)}, u32[]{:S(2)}, u32[]{:S(2)}) %collective-permute-start.14) | collective-permute-done | bytes 49184 | tf_op jit(solution)/shard_map/ppermute | solution.py:385
  60.1 4.0 %collective-permute-start.16 = (bf16[256,256]{1,0:T(8,128)(2,1)S(1)}, bf16[256,256]{1,0:T(8,128)(2,1)S(1)}, u32[]{:S(2)}, u32[]{:S(2)}) collective-permute-start(bf16[256,256]{1,0:T(8,128)(2,1)S(1)} %get-tuple-element.130), channel_id=1, source_target_pairs={{0,64},{2,66},{4,68},{6,70},{8,72},{10,74},{12,76},{14,78},{16,80}... | collective-permute-start | bytes 393224 | tf_op jit(solution)/shard_map/ppermute | solution.py:391
  64.0 8.9 %collective-permute-start.15 = (bf16[256,256]{1,0:T(8,128)(2,1)S(1)}, bf16[256,256]{1,0:T(8,128)(2,1)S(1)}, u32[]{:S(2)}, u32[]{:S(2)}) collective-permute-start(bf16[256,256]{1,0:T(8,128)(2,1)S(1)} %get-tuple-element.131), channel_id=1, source_target_pairs={{0,192},{2,194},{4,196},{6,198},{8,200},{10,202},{12,204},{14,206}... | collective-permute-start | bytes 393224 | tf_op jit(solution)/shard_map/ppermute | solution.py:391
  72.9 2.7 %collective-permute-start.18 = (bf16[2,512,128]{2,1,0:T(8,128)(2,1)S(1)}, bf16[2,512,128]{2,1,0:T(8,128)(2,1)S(1)}, u32[]{:S(2)}, u32[]{:S(2)}) collective-permute-start(bf16[2,512,128]{2,1,0:T(8,128)(2,1)S(1)} %get-tuple-element.91), channel_id=1, source_target_pairs={{0,4},{2,6},{4,0},{6,2},{8,12},{10,14},{12,8},{14,10},{16,20},{18,... | collective-permute-start | bytes 786440 | tf_op jit(solution)/shard_map/ppermute | solution.py:392
  75.6 2.0 %collective-permute-start.19 = (bf16[2,512,128]{2,1,0:T(8,128)(2,1)S(1)}, bf16[2,512,128]{2,1,0:T(8,128)(2,1)S(1)}, u32[]{:S(2)}, u32[]{:S(2)}) collective-permute-start(bf16[2,512,128]{2,1,0:T(8,128)(2,1)S(1)} %get-tuple-element.92), channel_id=1, source_target_pairs={{0,6},{2,4},{4,2},{6,0},{8,14},{10,12},{12,10},{14,8},{16,22},{18,... | collective-permute-start | bytes 786440 | tf_op jit(solution)/shard_map/ppermute | solution.py:392
  77.6 2.7 %backward_middle.1 = (bf16[4,256,256]{2,1,0:T(8,128)(2,1)S(1)}, f32[2,4,128,512]{3,2,1,0:T(8,128)S(1)}, f32[2,4,1,512]{3,2,1,0:T(1,128)S(1)}, f32[2,4,1,512]{3,2,1,0:T(1,128)S(1)}) custom-call(s32[16]{0:T(128)S(1)} %concatenate.18.sc, bf16[2,4,512,128]{3,2,1,0:T(8,128)(2,1)S(1)} %get-tuple-element.66.q_s, ...), custom_call_target="tpu_custom_call" | custom-call | flops 10737418240 | bytes 8388608 | tf_op jit(solution)/shard_map/backward_middle/pallas_call | solution.py:324
  82.2 2.7 %backward_end.1 = (bf16[2,256,256]{2,1,0:T(8,128)(2,1)S(1)}, bf16[2,512,128]{2,1,0:T(8,128)(2,1)S(1)}, bf16[2,512,128]{2,1,0:T(8,128)(2,1)S(1)}, bf16[2,512,128]...) custom-call(s32[16]{0:T(128)S(1)} %concatenate.18.sc, bf16[2,4,512,128]{3,2,1,0:T(8,128)(2,1)S(1)} %get-tuple-element.66.q_s, ...), custom_call_target="tpu_custom_call" | custom-call | flops 5368709120 | bytes 8388608 | tf_op jit(solution)/shard_map/backward_end/pallas_call | solution.py:324
  84.9 6.1 %collective-permute-done.19 = bf16[2,512,128]{2,1,0:T(8,128)(2,1)S(1)} collective-permute-done((bf16[2,512,128]{2,1,0:T(8,128)(2,1)S(1)}, bf16[2,512,128]{2,1,0:T(8,128)(2,1)S(1)}, u32[]{:S(2)}, u32[]{:S(2)}) %collective-permute-start.19) | collective-permute-done | bytes 262176 | tf_op jit(solution)/shard_map/ppermute | solution.py:392
  91.0 2.9 %collective-permute-start.26 = (bf16[2,512,128]{2,1,0:T(8,128)(2,1)S(1)}, bf16[2,512,128]{2,1,0:T(8,128)(2,1)S(1)}, u32[]{:S(2)}, u32[]{:S(2)}) collective-permute-start(bf16[2,512,128]{2,1,0:T(8,128)(2,1)S(1)} %get-tuple-element.106), channel_id=1, source_target_pairs={{0,2},{2,0},{4,6},{6,4},{8,10},{10,8},{12,14},{14,12},{16,18},{18,... | collective-permute-start | bytes 786440 | tf_op jit(solution)/shard_map/ppermute | solution.py:400
  95.3 4.7 %collective-permute-start.24 = (bf16[128,256]{1,0:T(8,128)(2,1)S(1)}, bf16[128,256]{1,0:T(8,128)(2,1)S(1)}, u32[]{:S(2)}, u32[]{:S(2)}) collective-permute-start(bf16[128,256]{1,0:T(8,128)(2,1)S(1)} %get-tuple-element.126), channel_id=1, source_target_pairs={{0,24},{2,26},{4,28},{6,30},{8,16},{10,18},{12,20},{14,22},{16,8},... | collective-permute-start | bytes 196616 | tf_op jit(solution)/shard_map/ppermute | solution.py:404
  100.2 2.4 %collective-permute-done.24 = bf16[128,256]{1,0:T(8,128)(2,1)S(1)} collective-permute-done((bf16[128,256]{1,0:T(8,128)(2,1)S(1)}, bf16[128,256]{1,0:T(8,128)(2,1)S(1)}, u32[]{:S(2)}, u32[]{:S(2)}) %collective-permute-start.24) | collective-permute-done | bytes 65568 | tf_op jit(solution)/shard_map/ppermute | solution.py:404
  102.6 3.2 %collective-permute-done.23 = bf16[128,256]{1,0:T(8,128)(2,1)S(1)} collective-permute-done((bf16[128,256]{1,0:T(8,128)(2,1)S(1)}, bf16[128,256]{1,0:T(8,128)(2,1)S(1)}, u32[]{:S(2)}, u32[]{:S(2)}) %collective-permute-start.23) | collective-permute-done | bytes 65568 | tf_op jit(solution)/shard_map/ppermute | solution.py:404
  108.8 2.0 %collective-permute-done.28.refs_2_ = bf16[512,128]{1,0:T(8,128)(2,1)S(1)} collective-permute-done((bf16[512,128]{1,0:T(8,128)(2,1)S(1)}, bf16[512,128]{1,0:T(8,128)(2,1)S(1)}, u32[]{:S(2)}, u32[]{:S(2)}) %collective-permute-start.28) | collective-permute-done | bytes 131104 | tf_op jit(solution)/shard_map/ppermute | solution.py:406
  (72 shorter events, 26.3 us)
Async XLA Ops:
  2.4 12.7 %collective-permute-start = (bf16[128,1024]{1,0:T(8,128)(2,1)}, bf16[128,1024]{1,0:T(8,128)(2,1)S(1)}, u32[]{:S(2)}, u32[]{:S(2)}) collective-permute-start(bf16[128,1024]{1,0:T(8,128)(2,1)} %get-tuple-element.61.refs_0_), channel_id=1, source_target_pairs={{0,32},{2,34},{4,36},{6,38},{8,40},{10,42},{12,44},{14,46},{16,48}... | collective-permute-start | bytes 786440 | tf_op jit(solution)/shard_map/ppermute | solution.py:355
  4.3 7.4 %collective-permute-start.2 = (bf16[128,256]{1,0:T(8,128)(2,1)}, bf16[128,256]{1,0:T(8,128)(2,1)S(1)}, u32[]{:S(2)}, u32[]{:S(2)}) collective-permute-start(bf16[128,256]{1,0:T(8,128)(2,1)} %get-tuple-element.62), channel_id=1, source_target_pairs={{0,192},{2,194},{4,196},{6,198},{8,200},{10,202},{12,204},{14,206}... | collective-permute-start | bytes 196616 | tf_op jit(solution)/shard_map/ppermute | solution.py:356
  8.8 6.3 %collective-permute-start.1 = (bf16[128,256]{1,0:T(8,128)(2,1)}, bf16[128,256]{1,0:T(8,128)(2,1)S(1)}, u32[]{:S(2)}, u32[]{:S(2)}) collective-permute-start(bf16[128,256]{1,0:T(8,128)(2,1)} %get-tuple-element.62), channel_id=1, source_target_pairs={{0,64},{2,66},{4,68},{6,70},{8,72},{10,74},{12,76},{14,78},{16,80}... | collective-permute-start | bytes 196616 | tf_op jit(solution)/shard_map/ppermute | solution.py:356
  15.1 14.7 %collective-permute-start.4 = (bf16[256,1024]{1,0:T(8,128)(2,1)S(1)}, bf16[256,1024]{1,0:T(8,128)(2,1)S(1)}, u32[]{:S(2)}, u32[]{:S(2)}) collective-permute-start(bf16[256,1024]{1,0:T(8,128)(2,1)S(1)} %constant_dynamic-update-slice_fusion), channel_id=1, source_target_pairs={{0,6},{2,4},{4,2},{6,0},{8,14},{10,12},{12,10},{14,8},{16,22},{18,... | collective-permute-start | bytes 1572872 | tf_op jit(solution)/shard_map/ppermute | solution.py:359
  18.2 13.6 %collective-permute-start.3 = (bf16[256,1024]{1,0:T(8,128)(2,1)S(1)}, bf16[256,1024]{1,0:T(8,128)(2,1)S(1)}, u32[]{:S(2)}, u32[]{:S(2)}) collective-permute-start(bf16[256,1024]{1,0:T(8,128)(2,1)S(1)} %constant_dynamic-update-slice_fusion), channel_id=1, source_target_pairs={{0,2},{2,0},{4,6},{6,4},{8,10},{10,8},{12,14},{14,12},{16,18},{18,... | collective-permute-start | bytes 1572872 | tf_op jit(solution)/shard_map/ppermute | solution.py:359
  19.2 6.5 %collective-permute-start.7 = (bf16[128,256]{1,0:T(8,128)(2,1)S(1)}, bf16[128,256]{1,0:T(8,128)(2,1)S(1)}, u32[]{:S(2)}, u32[]{:S(2)}) collective-permute-start(bf16[128,256]{1,0:T(8,128)(2,1)S(1)} %collective-permute-done.2), channel_id=1, source_target_pairs={{0,64},{2,66},{4,68},{6,70},{8,72},{10,74},{12,76},{14,78},{16,80}... | collective-permute-start | bytes 196616 | tf_op jit(solution)/shard_map/ppermute | solution.py:360
  25.7 11.9 %collective-permute-start.10 = (bf16[512,256]{1,0:T(8,128)(2,1)S(1)}, bf16[512,256]{1,0:T(8,128)(2,1)S(1)}, u32[]{:S(2)}, u32[]{:S(2)}) collective-permute-start(bf16[512,256]{1,0:T(8,128)(2,1)S(1)} %constant_dynamic-update-slice_fusion.2.refs_6_), channel_id=1, source_target_pairs={{0,24},{2,26},{4,28},{6,30},{8,16},{10,18},{12,20},{14,22},{16,8},... | collective-permute-start | bytes 786440 | tf_op jit(solution)/shard_map/ppermute | solution.py:361
  28.4 10.0 %collective-permute-start.9 = (bf16[512,256]{1,0:T(8,128)(2,1)S(1)}, bf16[512,256]{1,0:T(8,128)(2,1)S(1)}, u32[]{:S(2)}, u32[]{:S(2)}) collective-permute-start(bf16[512,256]{1,0:T(8,128)(2,1)S(1)} %constant_dynamic-update-slice_fusion.2.refs_6_), channel_id=1, source_target_pairs={{0,8},{2,10},{4,12},{6,14},{8,0},{10,2},{12,4},{14,6},{16,24},{18,... | collective-permute-start | bytes 786440 | tf_op jit(solution)/shard_map/ppermute | solution.py:361
  29.2 9.8 %collective-permute-start.8 = (bf16[512,256]{1,0:T(8,128)(2,1)S(1)}, bf16[512,256]{1,0:T(8,128)(2,1)S(1)}, u32[]{:S(2)}, u32[]{:S(2)}) collective-permute-start(bf16[512,256]{1,0:T(8,128)(2,1)S(1)} %constant_dynamic-update-slice_fusion.2.refs_6_), channel_id=1, source_target_pairs={{0,16},{2,18},{4,20},{6,22},{8,24},{10,26},{12,28},{14,30},{16,0},... | collective-permute-start | bytes 786440 | tf_op jit(solution)/shard_map/ppermute | solution.py:361
  29.8 9.2 %collective-permute-start.5 = (bf16[128,1024]{1,0:T(8,128)(2,1)S(1)}, bf16[128,1024]{1,0:T(8,128)(2,1)S(1)}, u32[]{:S(2)}, u32[]{:S(2)}) collective-permute-start(bf16[128,1024]{1,0:T(8,128)(2,1)S(1)} %slice.114), channel_id=1, source_target_pairs={{0,2},{2,0},{4,6},{6,4},{8,10},{10,8},{12,14},{14,12},{16,18},{18,... | collective-permute-start | bytes 786440 | tf_op jit(solution)/shard_map/ppermute | solution.py:362
  32.5 7.8 %collective-permute-start.6 = (bf16[128,1024]{1,0:T(8,128)(2,1)}, bf16[128,1024]{1,0:T(8,128)(2,1)S(1)}, u32[]{:S(2)}, u32[]{:S(2)}) collective-permute-start(bf16[128,1024]{1,0:T(8,128)(2,1)} %slice.115), channel_id=1, source_target_pairs={{0,6},{2,4},{4,2},{6,0},{8,14},{10,12},{12,10},{14,8},{16,22},{18,... | collective-permute-start | bytes 786440 | tf_op jit(solution)/shard_map/ppermute | solution.py:362
  51.5 6.4 %collective-permute-start.14 = (f32[2,12,512]{2,1,0:T(8,128)S(1)}, f32[2,12,512]{2,1,0:T(8,128)S(1)}, u32[]{:S(2)}, u32[]{:S(2)}) collective-permute-start(f32[2,12,512]{2,1,0:T(8,128)S(1)} %pad_maximum_fusion.2.refs_0_), channel_id=1, source_target_pairs={{0,6},{2,4},{4,2},{6,0},{8,14},{10,12},{12,10},{14,8},{16,22},{18,... | collective-permute-start | bytes 147464 | tf_op jit(solution)/shard_map/ppermute | solution.py:385
  51.9 6.9 %collective-permute-start.12 = (f32[2,12,512]{2,1,0:T(8,128)S(1)}, f32[2,12,512]{2,1,0:T(8,128)S(1)}, u32[]{:S(2)}, u32[]{:S(2)}) collective-permute-start(f32[2,12,512]{2,1,0:T(8,128)S(1)} %pad_maximum_fusion.2.refs_0_), channel_id=1, source_target_pairs={{0,2},{2,0},{4,6},{6,4},{8,10},{10,8},{12,14},{14,12},{16,18},{18,... | collective-permute-start | bytes 147464 | tf_op jit(solution)/shard_map/ppermute | solution.py:385
  60.1 20.2 %collective-permute-start.16 = (bf16[256,256]{1,0:T(8,128)(2,1)S(1)}, bf16[256,256]{1,0:T(8,128)(2,1)S(1)}, u32[]{:S(2)}, u32[]{:S(2)}) collective-permute-start(bf16[256,256]{1,0:T(8,128)(2,1)S(1)} %get-tuple-element.130), channel_id=1, source_target_pairs={{0,64},{2,66},{4,68},{6,70},{8,72},{10,74},{12,76},{14,78},{16,80}... | collective-permute-start | bytes 393224 | tf_op jit(solution)/shard_map/ppermute | solution.py:391
  64.0 16.3 %collective-permute-start.15 = (bf16[256,256]{1,0:T(8,128)(2,1)S(1)}, bf16[256,256]{1,0:T(8,128)(2,1)S(1)}, u32[]{:S(2)}, u32[]{:S(2)}) collective-permute-start(bf16[256,256]{1,0:T(8,128)(2,1)S(1)} %get-tuple-element.131), channel_id=1, source_target_pairs={{0,192},{2,194},{4,196},{6,198},{8,200},{10,202},{12,204},{14,206}... | collective-permute-start | bytes 393224 | tf_op jit(solution)/shard_map/ppermute | solution.py:391
  72.9 12.0 %collective-permute-start.17 = (bf16[2,512,128]{2,1,0:T(8,128)(2,1)S(1)}, bf16[2,512,128]{2,1,0:T(8,128)(2,1)S(1)}, u32[]{:S(2)}, u32[]{:S(2)}) collective-permute-start(bf16[2,512,128]{2,1,0:T(8,128)(2,1)S(1)} %get-tuple-element.90), channel_id=1, source_target_pairs={{0,2},{2,0},{4,6},{6,4},{8,10},{10,8},{12,14},{14,12},{16,18},{18,... | collective-permute-start | bytes 786440 | tf_op jit(solution)/shard_map/ppermute | solution.py:392
  72.9 12.0 %collective-permute-start.18 = (bf16[2,512,128]{2,1,0:T(8,128)(2,1)S(1)}, bf16[2,512,128]{2,1,0:T(8,128)(2,1)S(1)}, u32[]{:S(2)}, u32[]{:S(2)}) collective-permute-start(bf16[2,512,128]{2,1,0:T(8,128)(2,1)S(1)} %get-tuple-element.91), channel_id=1, source_target_pairs={{0,4},{2,6},{4,0},{6,2},{8,12},{10,14},{12,8},{14,10},{16,20},{18,... | collective-permute-start | bytes 786440 | tf_op jit(solution)/shard_map/ppermute | solution.py:392
  75.6 15.5 %collective-permute-start.19 = (bf16[2,512,128]{2,1,0:T(8,128)(2,1)S(1)}, bf16[2,512,128]{2,1,0:T(8,128)(2,1)S(1)}, u32[]{:S(2)}, u32[]{:S(2)}) collective-permute-start(bf16[2,512,128]{2,1,0:T(8,128)(2,1)S(1)} %get-tuple-element.92), channel_id=1, source_target_pairs={{0,6},{2,4},{4,2},{6,0},{8,14},{10,12},{12,10},{14,8},{16,22},{18,... | collective-permute-start | bytes 786440 | tf_op jit(solution)/shard_map/ppermute | solution.py:392
  80.4 14.7 %collective-permute-start.20 = (bf16[512,256]{1,0:T(8,128)(2,1)S(1)}, bf16[512,256]{1,0:T(8,128)(2,1)S(1)}, u32[]{:S(2)}, u32[]{:S(2)}) collective-permute-start(bf16[512,256]{1,0:T(8,128)(2,1)S(1)} %get-tuple-element.94), channel_id=1, source_target_pairs={{0,64},{2,66},{4,68},{6,70},{8,72},{10,74},{12,76},{14,78},{16,80}... | collective-permute-start | bytes 786440 | tf_op jit(solution)/shard_map/ppermute | solution.py:397
  80.5 14.6 %collective-permute-start.21 = (bf16[512,256]{1,0:T(8,128)(2,1)S(1)}, bf16[512,256]{1,0:T(8,128)(2,1)S(1)}, u32[]{:S(2)}, u32[]{:S(2)}) collective-permute-start(bf16[512,256]{1,0:T(8,128)(2,1)S(1)} %get-tuple-element.95), channel_id=1, source_target_pairs={{0,192},{2,194},{4,196},{6,198},{8,200},{10,202},{12,204},{14,206}... | collective-permute-start | bytes 786440 | tf_op jit(solution)/shard_map/ppermute | solution.py:397
  91.0 15.8 %collective-permute-start.25 = (bf16[2,512,128]{2,1,0:T(8,128)(2,1)S(1)}, bf16[2,512,128]{2,1,0:T(8,128)(2,1)S(1)}, u32[]{:S(2)}, u32[]{:S(2)}) collective-permute-start(bf16[2,512,128]{2,1,0:T(8,128)(2,1)S(1)} %get-tuple-element.105), channel_id=1, source_target_pairs={{0,4},{2,6},{4,0},{6,2},{8,12},{10,14},{12,8},{14,10},{16,20},{18,... | collective-permute-start | bytes 786440 | tf_op jit(solution)/shard_map/ppermute | solution.py:400
  91.0 15.8 %collective-permute-start.26 = (bf16[2,512,128]{2,1,0:T(8,128)(2,1)S(1)}, bf16[2,512,128]{2,1,0:T(8,128)(2,1)S(1)}, u32[]{:S(2)}, u32[]{:S(2)}) collective-permute-start(bf16[2,512,128]{2,1,0:T(8,128)(2,1)S(1)} %get-tuple-element.106), channel_id=1, source_target_pairs={{0,2},{2,0},{4,6},{6,4},{8,10},{10,8},{12,14},{14,12},{16,18},{18,... | collective-permute-start | bytes 786440 | tf_op jit(solution)/shard_map/ppermute | solution.py:400
  93.9 12.9 %collective-permute-start.27 = (bf16[2,512,128]{2,1,0:T(8,128)(2,1)S(1)}, bf16[2,512,128]{2,1,0:T(8,128)(2,1)S(1)}, u32[]{:S(2)}, u32[]{:S(2)}) collective-permute-start(bf16[2,512,128]{2,1,0:T(8,128)(2,1)S(1)} %get-tuple-element.107), channel_id=1, source_target_pairs={{0,6},{2,4},{4,2},{6,0},{8,14},{10,12},{12,10},{14,8},{16,22},{18,... | collective-permute-start | bytes 786440 | tf_op jit(solution)/shard_map/ppermute | solution.py:400
  95.3 7.3 %collective-permute-start.24 = (bf16[128,256]{1,0:T(8,128)(2,1)S(1)}, bf16[128,256]{1,0:T(8,128)(2,1)S(1)}, u32[]{:S(2)}, u32[]{:S(2)}) collective-permute-start(bf16[128,256]{1,0:T(8,128)(2,1)S(1)} %get-tuple-element.126), channel_id=1, source_target_pairs={{0,24},{2,26},{4,28},{6,30},{8,16},{10,18},{12,20},{14,22},{16,8},... | collective-permute-start | bytes 196616 | tf_op jit(solution)/shard_map/ppermute | solution.py:404
  (8 other events, 102.5 us)

commit v5 on v4

--- a/solution.py
+++ b/solution.py
@@ -354,10 +354,10 @@
     )(query, key, value, dout)
     row_other = send(row_home, perm=NEXT)
     a, b = send(key_home, perm=NEAR), send(key_home, perm=REST)
-    row_other, a, b = lax.optimization_barrier((row_other, a, b))
+    row_other, a = lax.optimization_barrier((row_other, a))
     both = jnp.concatenate([row_home, row_other], axis=0)
     near, last = send(both, perm=Y[1]), send(both, perm=Y[3])
-    held = jnp.concatenate([key_home, a, b, send(b, perm=NEAR)], axis=0)
+    held = jnp.concatenate([key_home, a, b, send(a, perm=REST)], axis=0)
     keys = [held] + [send(held, perm=X[n]) for n in range(1, 4)]
     far_own, far_other = send(last[:CHUNK], perm=Y[1]), send(near[CHUNK:], perm=Y[3])
     rows = [row_home, row_other, near, last, far_own, far_other]

time: 112 us -> 112 us (level); the launches traced: 113 us -> 110 us
  starting transfers between devices: 59.2 us -> 46.3 us
  Pallas kernels: 14.5 us -> 19.8 us
  waiting for transfers between devices: 34.1 us -> 38.2 us
    ppermute x2, starting transfers between devices: 12.8 us -> 6.61 us  [local(): one, two = (send(far[0], perm=NEAR), send(far[1], perm=REST))]
    ppermute x3, waiting for transfers between devices: 6.13 us -> 0.01 us  [local(): mixed = [mixed[0]] + [send(mixed[s], perm=Y[s]) for s in range(1, SLOTS)]]
    ppermute x2, waiting for transfers between devices: 3.83 us -> 9.18 us  [local(): a, b = (send(key_home, perm=NEAR), send(key_home, perm=REST))]
    ppermute x1, starting transfers between devices: 4.24 us -> 0.34 us  [local(): held = jnp.concatenate([key_home, a, b, send(a, perm=REST)], axis=0)]
    ppermute x2, waiting for transfers between devices: 0.01 us -> 3.42 us  [local(): one, two = (send(far[0], perm=NEAR), send(far[1], perm=REST))]
    ppermute x1, starting transfers between devices: 3.54 us -> 0.33 us  [local(): other = send(stat, perm=NEXT)[::-1]]
    pallas_call x3, Pallas kernels: 6.58 us -> 9.65 us  [run_backward(): pl.pallas_call(functools.partial(backward, group, width, span, begins, en...]
    pallas_call x1, Pallas kernels: 5.33 us -> 7.62 us  [run_forward(): pl.pallas_call(functools.partial(forward, group, width), out_shape=[jax.S...]
  transfers between devices with their start and end apart: 30 -> 30, of which waited for: 16 -> 16; matrix products, arithmetic and copies ran while one was open for 4% -> 4% of each run, Pallas kernels for 5% -> 6%
where the time goes in v5:
time: 112 us; the launch traced here: 110 us
  starting transfers between devices  46.3 us (41%)
  waiting for transfers between devices  38.2 us (34%)
  Pallas kernels  19.8 us (18%)
  local copies, waits for them, and re-layouts  3.46 us (3%)
    pallas_call x3, Pallas kernels, run_backward(): pl.pallas_call(functools.partial(backward, group, width, span, begins, en...  9.65 us
    ppermute x2, waiting for transfers between devices, local(): a, b = (send(key_home, perm=NEAR), send(key_home, perm=REST))  9.18 us
    pallas_call x1, Pallas kernels, run_forward(): pl.pallas_call(functools.partial(forward, group, width), out_shape=[jax.S...  7.62 us
    ppermute x2, starting transfers between devices, local(): one, two = (send(far[0], perm=NEAR), send(far[1], perm=REST))  6.61 us
    ppermute x3, waiting for transfers between devices, local(): keys = [held] + [send(held, perm=X[n]) for n in range(1, 4)]  6.01 us
    ppermute x2, starting transfers between devices, local(): a, b = (send(key_home, perm=NEAR), send(key_home, perm=REST))  5.33 us
    ppermute x3, starting transfers between devices, local(): grad = [grad[0]] + [send(grad[n], perm=X[n]) for n in range(1, 4)]  5.32 us
    ppermute x3, starting transfers between devices, local(): mixed = [mixed[0]] + [send(mixed[s], perm=Y[s]) for s in range(1, SLOTS)]  4.7 us
  transfers between devices with their start and end apart: 30, of which 16 were waited for; matrix products, arithmetic and copies ran while one was open for 4% of the time, Pallas kernels for 6%

profile of v5, /device:TPU:32, one launch (start us, length us, event | category | flops | bytes accessed | tf_op | source)
XLA Modules:
  0.0 109.6 jit_solution(12241511260224863903)
XLA Ops:
  2.4 1.8 %collective-permute-start = (bf16[128,1024]{1,0:T(8,128)(2,1)}, bf16[128,1024]{1,0:T(8,128)(2,1)S(1)}, u32[]{:S(2)}, u32[]{:S(2)}) collective-permute-start(bf16[128,1024]{1,0:T(8,128)(2,1)} %get-tuple-element.60.refs_0_), channel_id=1, source_target_pairs={{0,32},{2,34},{4,36},{6,38},{8,40},{10,42},{12,44},{14,46},{16,48}... | collective-permute-start | bytes 786440 | tf_op jit(solution)/shard_map/ppermute | solution.py:355
  6.8 6.9 %collective-permute-done.1 = bf16[128,256]{1,0:T(8,128)(2,1)S(1)} collective-permute-done((bf16[128,256]{1,0:T(8,128)(2,1)}, bf16[128,256]{1,0:T(8,128)(2,1)S(1)}, u32[]{:S(2)}, u32[]{:S(2)}) %collective-permute-start.1) | collective-permute-done | bytes 65568 | tf_op jit(solution)/shard_map/ppermute | solution.py:356
  13.7 3.1 %collective-permute-start.3 = (bf16[256,1024]{1,0:T(8,128)(2,1)S(1)}, bf16[256,1024]{1,0:T(8,128)(2,1)S(1)}, u32[]{:S(2)}, u32[]{:S(2)}) collective-permute-start(bf16[256,1024]{1,0:T(8,128)(2,1)S(1)} %constant_dynamic-update-slice_fusion), channel_id=1, source_target_pairs={{0,6},{2,4},{4,2},{6,0},{8,14},{10,12},{12,10},{14,8},{16,22},{18,... | collective-permute-start | bytes 1572872 | tf_op jit(solution)/shard_map/ppermute | solution.py:359
  17.0 3.8 %collective-permute-start.6 = (bf16[128,256]{1,0:T(8,128)(2,1)}, bf16[128,256]{1,0:T(8,128)(2,1)S(1)}, u32[]{:S(2)}, u32[]{:S(2)}) collective-permute-start(bf16[128,256]{1,0:T(8,128)(2,1)} %get-tuple-element.61), channel_id=1, source_target_pairs={{0,192},{2,194},{4,196},{6,198},{8,200},{10,202},{12,204},{14,206}... | collective-permute-start | bytes 196616 | tf_op jit(solution)/shard_map/ppermute | solution.py:356
  22.0 2.3 %collective-permute-done.6 = bf16[128,256]{1,0:T(8,128)(2,1)S(1)} collective-permute-done((bf16[128,256]{1,0:T(8,128)(2,1)}, bf16[128,256]{1,0:T(8,128)(2,1)S(1)}, u32[]{:S(2)}, u32[]{:S(2)}) %collective-permute-start.6) | collective-permute-done | bytes 65568 | tf_op jit(solution)/shard_map/ppermute | solution.py:356
  24.2 3.8 %collective-permute-done.7 = bf16[128,256]{1,0:T(8,128)(2,1)S(1)} collective-permute-done((bf16[128,256]{1,0:T(8,128)(2,1)S(1)}, bf16[128,256]{1,0:T(8,128)(2,1)S(1)}, u32[]{:S(2)}, u32[]{:S(2)}) %collective-permute-start.7) | collective-permute-done | bytes 65568 | tf_op jit(solution)/shard_map/ppermute | solution.py:360
  28.0 2.8 %collective-permute-start.10 = (bf16[512,256]{1,0:T(8,128)(2,1)S(1)}, bf16[512,256]{1,0:T(8,128)(2,1)S(1)}, u32[]{:S(2)}, u32[]{:S(2)}) collective-permute-start(bf16[512,256]{1,0:T(8,128)(2,1)S(1)} %constant_dynamic-update-slice_fusion.2.refs_6_), channel_id=1, source_target_pairs={{0,24},{2,26},{4,28},{6,30},{8,16},{10,18},{12,20},{14,22},{16,8},... | collective-permute-start | bytes 786440 | tf_op jit(solution)/shard_map/ppermute | solution.py:361
  32.1 2.0 %collective-permute-start.4 = (bf16[128,1024]{1,0:T(8,128)(2,1)S(1)}, bf16[128,1024]{1,0:T(8,128)(2,1)S(1)}, u32[]{:S(2)}, u32[]{:S(2)}) collective-permute-start(bf16[128,1024]{1,0:T(8,128)(2,1)S(1)} %slice.114), channel_id=1, source_target_pairs={{0,2},{2,0},{4,6},{6,4},{8,10},{10,8},{12,14},{14,12},{16,18},{18,... | collective-permute-start | bytes 786440 | tf_op jit(solution)/shard_map/ppermute | solution.py:362
  35.5 4.7 %collective-permute-done.10.refs_9_ = bf16[512,256]{1,0:T(8,128)(2,1)S(1)} collective-permute-done((bf16[512,256]{1,0:T(8,128)(2,1)S(1)}, bf16[512,256]{1,0:T(8,128)(2,1)S(1)}, u32[]{:S(2)}, u32[]{:S(2)}) %collective-permute-start.10) | collective-permute-done | bytes 262176 | tf_op jit(solution)/shard_map/ppermute | solution.py:361
  42.6 7.6 %forward.1 = (bf16[2,4,128,512]{3,2,1,0:T(8,128)(2,1)S(1)}, f32[2,12,512]{2,1,0:T(8,128)S(1)}, bf16[2,4,512,128]{3,2,1,0:T(8,128)(2,1)S(1)}, bf16[2,4,512,128]{3...) custom-call(s32[16]{0:T(128)S(1)} %concatenate.18.sc, ...), custom_call_target="tpu_custom_call" | custom-call | flops 12884901888 | bytes 8388608 | tf_op jit(solution)/shard_map/forward/pallas_call | solution.py:300
  50.6 4.0 %collective-permute-done.11 = f32[2,12,512]{2,1,0:T(8,128)S(1)} collective-permute-done((f32[2,12,512]{2,1,0:T(8,128)S(1)}, f32[2,12,512]{2,1,0:T(8,128)S(1)}, u32[]{:S(2)}, u32[]{:S(2)}) %collective-permute-start.11) | collective-permute-done | bytes 49184 | tf_op jit(solution)/shard_map/ppermute | solution.py:373
  55.1 4.0 %collective-permute-start.12 = (f32[2,12,512]{2,1,0:T(8,128)S(1)}, f32[2,12,512]{2,1,0:T(8,128)S(1)}, u32[]{:S(2)}, u32[]{:S(2)}) collective-permute-start(f32[2,12,512]{2,1,0:T(8,128)S(1)} %pad_maximum_fusion.2.refs_0_), channel_id=1, source_target_pairs={{0,2},{2,0},{4,6},{6,4},{8,10},{10,8},{12,14},{14,12},{16,18},{18,... | collective-permute-start | bytes 147464 | tf_op jit(solution)/shard_map/ppermute | solution.py:385
  59.0 2.1 %collective-permute-done.14.refs_3_ = f32[2,12,512]{2,1,0:T(8,128)S(1)} collective-permute-done((f32[2,12,512]{2,1,0:T(8,128)S(1)}, f32[2,12,512]{2,1,0:T(8,128)S(1)}, u32[]{:S(2)}, u32[]{:S(2)}) %collective-permute-start.14) | collective-permute-done | bytes 49184 | tf_op jit(solution)/shard_map/ppermute | solution.py:385
  62.0 2.7 %backward_begin.1 = (bf16[2,256,256]{2,1,0:T(8,128)(2,1)S(1)}, bf16[2,512,128]{2,1,0:T(8,128)(2,1)S(1)}, bf16[2,512,128]{2,1,0:T(8,128)(2,1)S(1)}, bf16[2,512,12...) custom-call(s32[16]{0:T(128)S(1)} %concatenate.18.sc, ...), custom_call_target="tpu_custom_call" | custom-call | flops 5368709120 | bytes 8388608 | tf_op jit(solution)/shard_map/backward_begin/pallas_call | solution.py:324
  64.7 6.6 %collective-permute-start.16 = (bf16[256,256]{1,0:T(8,128)(2,1)S(1)}, bf16[256,256]{1,0:T(8,128)(2,1)S(1)}, u32[]{:S(2)}, u32[]{:S(2)}) collective-permute-start(bf16[256,256]{1,0:T(8,128)(2,1)S(1)} %get-tuple-element.128), channel_id=1, source_target_pairs={{0,64},{2,66},{4,68},{6,70},{8,72},{10,74},{12,76},{14,78},{16,80}... | collective-permute-start | bytes 393224 | tf_op jit(solution)/shard_map/ppermute | solution.py:391
  72.8 3.2 %collective-permute-start.19 = (bf16[2,512,128]{2,1,0:T(8,128)(2,1)S(1)}, bf16[2,512,128]{2,1,0:T(8,128)(2,1)S(1)}, u32[]{:S(2)}, u32[]{:S(2)}) collective-permute-start(bf16[2,512,128]{2,1,0:T(8,128)(2,1)S(1)} %get-tuple-element.90), channel_id=1, source_target_pairs={{0,6},{2,4},{4,2},{6,0},{8,14},{10,12},{12,10},{14,8},{16,22},{18,... | collective-permute-start | bytes 786440 | tf_op jit(solution)/shard_map/ppermute | solution.py:392
  76.0 4.3 %backward_middle.1 = (bf16[4,256,256]{2,1,0:T(8,128)(2,1)S(1)}, f32[2,4,128,512]{3,2,1,0:T(8,128)S(1)}, f32[2,4,1,512]{3,2,1,0:T(1,128)S(1)}, f32[2,4,1,512]{3,2,1,0:T(1,128)S(1)}) custom-call(s32[16]{0:T(128)S(1)} %concatenate.18.sc, bf16[2,4,512,128]{3,2,1,0:T(8,128)(2,1)S(1)} %get-tuple-element.64.q_s, ...), custom_call_target="tpu_custom_call" | custom-call | flops 10737418240 | bytes 8388608 | tf_op jit(solution)/shard_map/backward_middle/pallas_call | solution.py:324
  80.3 3.4 %collective-permute-done.15 = bf16[256,256]{1,0:T(8,128)(2,1)S(1)} collective-permute-done((bf16[256,256]{1,0:T(8,128)(2,1)S(1)}, bf16[256,256]{1,0:T(8,128)(2,1)S(1)}, u32[]{:S(2)}, u32[]{:S(2)}) %collective-permute-start.15) | collective-permute-done | bytes 131104 | tf_op jit(solution)/shard_map/ppermute | solution.py:391
  84.0 2.4 %collective-permute-start.21 = (bf16[512,256]{1,0:T(8,128)(2,1)S(1)}, bf16[512,256]{1,0:T(8,128)(2,1)S(1)}, u32[]{:S(2)}, u32[]{:S(2)}) collective-permute-start(bf16[512,256]{1,0:T(8,128)(2,1)S(1)} %get-tuple-element.93), channel_id=1, source_target_pairs={{0,192},{2,194},{4,196},{6,198},{8,200},{10,202},{12,204},{14,206}... | collective-permute-start | bytes 786440 | tf_op jit(solution)/shard_map/ppermute | solution.py:397
  86.4 2.7 %backward_end.1 = (bf16[2,256,256]{2,1,0:T(8,128)(2,1)S(1)}, bf16[2,512,128]{2,1,0:T(8,128)(2,1)S(1)}, bf16[2,512,128]{2,1,0:T(8,128)(2,1)S(1)}, bf16[2,512,128]...) custom-call(s32[16]{0:T(128)S(1)} %concatenate.18.sc, bf16[2,4,512,128]{3,2,1,0:T(8,128)(2,1)S(1)} %get-tuple-element.64.q_s, ...), custom_call_target="tpu_custom_call" | custom-call | flops 5368709120 | bytes 8388608 | tf_op jit(solution)/shard_map/backward_end/pallas_call | solution.py:324
  89.6 3.6 %collective-permute-start.27 = (bf16[2,512,128]{2,1,0:T(8,128)(2,1)S(1)}, bf16[2,512,128]{2,1,0:T(8,128)(2,1)S(1)}, u32[]{:S(2)}, u32[]{:S(2)}) collective-permute-start(bf16[2,512,128]{2,1,0:T(8,128)(2,1)S(1)} %get-tuple-element.105), channel_id=1, source_target_pairs={{0,6},{2,4},{4,2},{6,0},{8,14},{10,12},{12,10},{14,8},{16,22},{18,... | collective-permute-start | bytes 786440 | tf_op jit(solution)/shard_map/ppermute | solution.py:400
  93.5 3.2 %collective-permute-start.24 = (bf16[128,256]{1,0:T(8,128)(2,1)S(1)}, bf16[128,256]{1,0:T(8,128)(2,1)S(1)}, u32[]{:S(2)}, u32[]{:S(2)}) collective-permute-start(bf16[128,256]{1,0:T(8,128)(2,1)S(1)} %get-tuple-element.124), channel_id=1, source_target_pairs={{0,24},{2,26},{4,28},{6,30},{8,16},{10,18},{12,20},{14,22},{16,8},... | collective-permute-start | bytes 196616 | tf_op jit(solution)/shard_map/ppermute | solution.py:404
  100.0 2.4 %collective-permute-done.23 = bf16[128,256]{1,0:T(8,128)(2,1)S(1)} collective-permute-done((bf16[128,256]{1,0:T(8,128)(2,1)S(1)}, bf16[128,256]{1,0:T(8,128)(2,1)S(1)}, u32[]{:S(2)}, u32[]{:S(2)}) %collective-permute-start.23) | collective-permute-done | bytes 65568 | tf_op jit(solution)/shard_map/ppermute | solution.py:404
  105.4 2.0 %collective-permute-done.28.refs_2_ = bf16[512,128]{1,0:T(8,128)(2,1)S(1)} collective-permute-done((bf16[512,128]{1,0:T(8,128)(2,1)S(1)}, bf16[512,128]{1,0:T(8,128)(2,1)S(1)}, u32[]{:S(2)}, u32[]{:S(2)}) %collective-permute-start.28) | collective-permute-done | bytes 131104 | tf_op jit(solution)/shard_map/ppermute | solution.py:406
  (72 shorter events, 23.4 us)
Async XLA Ops:
  2.4 11.3 %collective-permute-start = (bf16[128,1024]{1,0:T(8,128)(2,1)}, bf16[128,1024]{1,0:T(8,128)(2,1)S(1)}, u32[]{:S(2)}, u32[]{:S(2)}) collective-permute-start(bf16[128,1024]{1,0:T(8,128)(2,1)} %get-tuple-element.60.refs_0_), channel_id=1, source_target_pairs={{0,32},{2,34},{4,36},{6,38},{8,40},{10,42},{12,44},{14,46},{16,48}... | collective-permute-start | bytes 786440 | tf_op jit(solution)/shard_map/ppermute | solution.py:355
  4.3 9.4 %collective-permute-start.1 = (bf16[128,256]{1,0:T(8,128)(2,1)}, bf16[128,256]{1,0:T(8,128)(2,1)S(1)}, u32[]{:S(2)}, u32[]{:S(2)}) collective-permute-start(bf16[128,256]{1,0:T(8,128)(2,1)} %get-tuple-element.61), channel_id=1, source_target_pairs={{0,64},{2,66},{4,68},{6,70},{8,72},{10,74},{12,76},{14,78},{16,80}... | collective-permute-start | bytes 196616 | tf_op jit(solution)/shard_map/ppermute | solution.py:356
  13.7 18.4 %collective-permute-start.3 = (bf16[256,1024]{1,0:T(8,128)(2,1)S(1)}, bf16[256,1024]{1,0:T(8,128)(2,1)S(1)}, u32[]{:S(2)}, u32[]{:S(2)}) collective-permute-start(bf16[256,1024]{1,0:T(8,128)(2,1)S(1)} %constant_dynamic-update-slice_fusion), channel_id=1, source_target_pairs={{0,6},{2,4},{4,2},{6,0},{8,14},{10,12},{12,10},{14,8},{16,22},{18,... | collective-permute-start | bytes 1572872 | tf_op jit(solution)/shard_map/ppermute | solution.py:359
  16.8 17.3 %collective-permute-start.2 = (bf16[256,1024]{1,0:T(8,128)(2,1)S(1)}, bf16[256,1024]{1,0:T(8,128)(2,1)S(1)}, u32[]{:S(2)}, u32[]{:S(2)}) collective-permute-start(bf16[256,1024]{1,0:T(8,128)(2,1)S(1)} %constant_dynamic-update-slice_fusion), channel_id=1, source_target_pairs={{0,2},{2,0},{4,6},{6,4},{8,10},{10,8},{12,14},{14,12},{16,18},{18,... | collective-permute-start | bytes 1572872 | tf_op jit(solution)/shard_map/ppermute | solution.py:359
  17.0 7.3 %collective-permute-start.6 = (bf16[128,256]{1,0:T(8,128)(2,1)}, bf16[128,256]{1,0:T(8,128)(2,1)S(1)}, u32[]{:S(2)}, u32[]{:S(2)}) collective-permute-start(bf16[128,256]{1,0:T(8,128)(2,1)} %get-tuple-element.61), channel_id=1, source_target_pairs={{0,192},{2,194},{4,196},{6,198},{8,200},{10,202},{12,204},{14,206}... | collective-permute-start | bytes 196616 | tf_op jit(solution)/shard_map/ppermute | solution.py:356
  21.6 6.4 %collective-permute-start.7 = (bf16[128,256]{1,0:T(8,128)(2,1)S(1)}, bf16[128,256]{1,0:T(8,128)(2,1)S(1)}, u32[]{:S(2)}, u32[]{:S(2)}) collective-permute-start(bf16[128,256]{1,0:T(8,128)(2,1)S(1)} %collective-permute-done.1), channel_id=1, source_target_pairs={{0,192},{2,194},{4,196},{6,198},{8,200},{10,202},{12,204},{14,206}... | collective-permute-start | bytes 196616 | tf_op jit(solution)/shard_map/ppermute | solution.py:360
  28.0 12.2 %collective-permute-start.10 = (bf16[512,256]{1,0:T(8,128)(2,1)S(1)}, bf16[512,256]{1,0:T(8,128)(2,1)S(1)}, u32[]{:S(2)}, u32[]{:S(2)}) collective-permute-start(bf16[512,256]{1,0:T(8,128)(2,1)S(1)} %constant_dynamic-update-slice_fusion.2.refs_6_), channel_id=1, source_target_pairs={{0,24},{2,26},{4,28},{6,30},{8,16},{10,18},{12,20},{14,22},{16,8},... | collective-permute-start | bytes 786440 | tf_op jit(solution)/shard_map/ppermute | solution.py:361
  30.8 10.1 %collective-permute-start.9 = (bf16[512,256]{1,0:T(8,128)(2,1)S(1)}, bf16[512,256]{1,0:T(8,128)(2,1)S(1)}, u32[]{:S(2)}, u32[]{:S(2)}) collective-permute-start(bf16[512,256]{1,0:T(8,128)(2,1)S(1)} %constant_dynamic-update-slice_fusion.2.refs_6_), channel_id=1, source_target_pairs={{0,8},{2,10},{4,12},{6,14},{8,0},{10,2},{12,4},{14,6},{16,24},{18,... | collective-permute-start | bytes 786440 | tf_op jit(solution)/shard_map/ppermute | solution.py:361
  31.6 9.9 %collective-permute-start.8 = (bf16[512,256]{1,0:T(8,128)(2,1)S(1)}, bf16[512,256]{1,0:T(8,128)(2,1)S(1)}, u32[]{:S(2)}, u32[]{:S(2)}) collective-permute-start(bf16[512,256]{1,0:T(8,128)(2,1)S(1)} %constant_dynamic-update-slice_fusion.2.refs_6_), channel_id=1, source_target_pairs={{0,16},{2,18},{4,20},{6,22},{8,24},{10,26},{12,28},{14,30},{16,0},... | collective-permute-start | bytes 786440 | tf_op jit(solution)/shard_map/ppermute | solution.py:361
  32.1 9.4 %collective-permute-start.4 = (bf16[128,1024]{1,0:T(8,128)(2,1)S(1)}, bf16[128,1024]{1,0:T(8,128)(2,1)S(1)}, u32[]{:S(2)}, u32[]{:S(2)}) collective-permute-start(bf16[128,1024]{1,0:T(8,128)(2,1)S(1)} %slice.114), channel_id=1, source_target_pairs={{0,2},{2,0},{4,6},{6,4},{8,10},{10,8},{12,14},{14,12},{16,18},{18,... | collective-permute-start | bytes 786440 | tf_op jit(solution)/shard_map/ppermute | solution.py:362
  34.8 7.8 %collective-permute-start.5 = (bf16[128,1024]{1,0:T(8,128)(2,1)}, bf16[128,1024]{1,0:T(8,128)(2,1)S(1)}, u32[]{:S(2)}, u32[]{:S(2)}) collective-permute-start(bf16[128,1024]{1,0:T(8,128)(2,1)} %slice.115), channel_id=1, source_target_pairs={{0,6},{2,4},{4,2},{6,0},{8,14},{10,12},{12,10},{14,8},{16,22},{18,... | collective-permute-start | bytes 786440 | tf_op jit(solution)/shard_map/ppermute | solution.py:362
  54.7 6.4 %collective-permute-start.14 = (f32[2,12,512]{2,1,0:T(8,128)S(1)}, f32[2,12,512]{2,1,0:T(8,128)S(1)}, u32[]{:S(2)}, u32[]{:S(2)}) collective-permute-start(f32[2,12,512]{2,1,0:T(8,128)S(1)} %pad_maximum_fusion.2.refs_0_), channel_id=1, source_target_pairs={{0,6},{2,4},{4,2},{6,0},{8,14},{10,12},{12,10},{14,8},{16,22},{18,... | collective-permute-start | bytes 147464 | tf_op jit(solution)/shard_map/ppermute | solution.py:385
  55.0 6.2 %collective-permute-start.13 = (f32[2,12,512]{2,1,0:T(8,128)S(1)}, f32[2,12,512]{2,1,0:T(8,128)S(1)}, u32[]{:S(2)}, u32[]{:S(2)}) collective-permute-start(f32[2,12,512]{2,1,0:T(8,128)S(1)} %pad_maximum_fusion.2.refs_0_), channel_id=1, source_target_pairs={{0,4},{2,6},{4,0},{6,2},{8,12},{10,14},{12,8},{14,10},{16,20},{18,... | collective-permute-start | bytes 147464 | tf_op jit(solution)/shard_map/ppermute | solution.py:385
  55.1 6.9 %collective-permute-start.12 = (f32[2,12,512]{2,1,0:T(8,128)S(1)}, f32[2,12,512]{2,1,0:T(8,128)S(1)}, u32[]{:S(2)}, u32[]{:S(2)}) collective-permute-start(f32[2,12,512]{2,1,0:T(8,128)S(1)} %pad_maximum_fusion.2.refs_0_), channel_id=1, source_target_pairs={{0,2},{2,0},{4,6},{6,4},{8,10},{10,8},{12,14},{14,12},{16,18},{18,... | collective-permute-start | bytes 147464 | tf_op jit(solution)/shard_map/ppermute | solution.py:385
  64.7 15.6 %collective-permute-start.16 = (bf16[256,256]{1,0:T(8,128)(2,1)S(1)}, bf16[256,256]{1,0:T(8,128)(2,1)S(1)}, u32[]{:S(2)}, u32[]{:S(2)}) collective-permute-start(bf16[256,256]{1,0:T(8,128)(2,1)S(1)} %get-tuple-element.128), channel_id=1, source_target_pairs={{0,64},{2,66},{4,68},{6,70},{8,72},{10,74},{12,76},{14,78},{16,80}... | collective-permute-start | bytes 393224 | tf_op jit(solution)/shard_map/ppermute | solution.py:391
  71.3 12.4 %collective-permute-start.15 = (bf16[256,256]{1,0:T(8,128)(2,1)S(1)}, bf16[256,256]{1,0:T(8,128)(2,1)S(1)}, u32[]{:S(2)}, u32[]{:S(2)}) collective-permute-start(bf16[256,256]{1,0:T(8,128)(2,1)S(1)} %get-tuple-element.129), channel_id=1, source_target_pairs={{0,192},{2,194},{4,196},{6,198},{8,200},{10,202},{12,204},{14,206}... | collective-permute-start | bytes 393224 | tf_op jit(solution)/shard_map/ppermute | solution.py:391
  71.3 17.8 %collective-permute-start.17 = (bf16[2,512,128]{2,1,0:T(8,128)(2,1)S(1)}, bf16[2,512,128]{2,1,0:T(8,128)(2,1)S(1)}, u32[]{:S(2)}, u32[]{:S(2)}) collective-permute-start(bf16[2,512,128]{2,1,0:T(8,128)(2,1)S(1)} %get-tuple-element.88), channel_id=1, source_target_pairs={{0,2},{2,0},{4,6},{6,4},{8,10},{10,8},{12,14},{14,12},{16,18},{18,... | collective-permute-start | bytes 786440 | tf_op jit(solution)/shard_map/ppermute | solution.py:392
  72.3 16.8 %collective-permute-start.18 = (bf16[2,512,128]{2,1,0:T(8,128)(2,1)S(1)}, bf16[2,512,128]{2,1,0:T(8,128)(2,1)S(1)}, u32[]{:S(2)}, u32[]{:S(2)}) collective-permute-start(bf16[2,512,128]{2,1,0:T(8,128)(2,1)S(1)} %get-tuple-element.89), channel_id=1, source_target_pairs={{0,4},{2,6},{4,0},{6,2},{8,12},{10,14},{12,8},{14,10},{16,20},{18,... | collective-permute-start | bytes 786440 | tf_op jit(solution)/shard_map/ppermute | solution.py:392
  72.8 16.3 %collective-permute-start.19 = (bf16[2,512,128]{2,1,0:T(8,128)(2,1)S(1)}, bf16[2,512,128]{2,1,0:T(8,128)(2,1)S(1)}, u32[]{:S(2)}, u32[]{:S(2)}) collective-permute-start(bf16[2,512,128]{2,1,0:T(8,128)(2,1)S(1)} %get-tuple-element.90), channel_id=1, source_target_pairs={{0,6},{2,4},{4,2},{6,0},{8,14},{10,12},{12,10},{14,8},{16,22},{18,... | collective-permute-start | bytes 786440 | tf_op jit(solution)/shard_map/ppermute | solution.py:392
  83.9 9.4 %collective-permute-start.20 = (bf16[512,256]{1,0:T(8,128)(2,1)S(1)}, bf16[512,256]{1,0:T(8,128)(2,1)S(1)}, u32[]{:S(2)}, u32[]{:S(2)}) collective-permute-start(bf16[512,256]{1,0:T(8,128)(2,1)S(1)} %get-tuple-element.92), channel_id=1, source_target_pairs={{0,64},{2,66},{4,68},{6,70},{8,72},{10,74},{12,76},{14,78},{16,80}... | collective-permute-start | bytes 786440 | tf_op jit(solution)/shard_map/ppermute | solution.py:397
  84.0 9.3 %collective-permute-start.21 = (bf16[512,256]{1,0:T(8,128)(2,1)S(1)}, bf16[512,256]{1,0:T(8,128)(2,1)S(1)}, u32[]{:S(2)}, u32[]{:S(2)}) collective-permute-start(bf16[512,256]{1,0:T(8,128)(2,1)S(1)} %get-tuple-element.93), channel_id=1, source_target_pairs={{0,192},{2,194},{4,196},{6,198},{8,200},{10,202},{12,204},{14,206}... | collective-permute-start | bytes 786440 | tf_op jit(solution)/shard_map/ppermute | solution.py:397
  89.1 14.2 %collective-permute-start.25 = (bf16[2,512,128]{2,1,0:T(8,128)(2,1)S(1)}, bf16[2,512,128]{2,1,0:T(8,128)(2,1)S(1)}, u32[]{:S(2)}, u32[]{:S(2)}) collective-permute-start(bf16[2,512,128]{2,1,0:T(8,128)(2,1)S(1)} %get-tuple-element.103), channel_id=1, source_target_pairs={{0,4},{2,6},{4,0},{6,2},{8,12},{10,14},{12,8},{14,10},{16,20},{18,... | collective-permute-start | bytes 786440 | tf_op jit(solution)/shard_map/ppermute | solution.py:400
  89.2 14.1 %collective-permute-start.26 = (bf16[2,512,128]{2,1,0:T(8,128)(2,1)S(1)}, bf16[2,512,128]{2,1,0:T(8,128)(2,1)S(1)}, u32[]{:S(2)}, u32[]{:S(2)}) collective-permute-start(bf16[2,512,128]{2,1,0:T(8,128)(2,1)S(1)} %get-tuple-element.104), channel_id=1, source_target_pairs={{0,2},{2,0},{4,6},{6,4},{8,10},{10,8},{12,14},{14,12},{16,18},{18,... | collective-permute-start | bytes 786440 | tf_op jit(solution)/shard_map/ppermute | solution.py:400
  89.6 13.7 %collective-permute-start.27 = (bf16[2,512,128]{2,1,0:T(8,128)(2,1)S(1)}, bf16[2,512,128]{2,1,0:T(8,128)(2,1)S(1)}, u32[]{:S(2)}, u32[]{:S(2)}) collective-permute-start(bf16[2,512,128]{2,1,0:T(8,128)(2,1)S(1)} %get-tuple-element.105), channel_id=1, source_target_pairs={{0,6},{2,4},{4,2},{6,0},{8,14},{10,12},{12,10},{14,8},{16,22},{18,... | collective-permute-start | bytes 786440 | tf_op jit(solution)/shard_map/ppermute | solution.py:400
  (8 other events, 104.9 us)

commit v6 on v5

--- a/solution.py
+++ b/solution.py
@@ -354,7 +354,7 @@
     )(query, key, value, dout)
     row_other = send(row_home, perm=NEXT)
     a, b = send(key_home, perm=NEAR), send(key_home, perm=REST)
-    row_other, a = lax.optimization_barrier((row_other, a))
+    row_other, a, b = lax.optimization_barrier((row_other, a, b))
     both = jnp.concatenate([row_home, row_other], axis=0)
     near, last = send(both, perm=Y[1]), send(both, perm=Y[3])
     held = jnp.concatenate([key_home, a, b, send(a, perm=REST)], axis=0)
@@ -402,11 +402,12 @@
     _, mixed = lax.optimization_barrier((grad, mixed))
     grad = grad.reshape(4, CHUNK, 2 * width)
     grad = [grad[0]] + [send(grad[n], perm=X[n]) for n in range(1, 4)]
-    mixed = add(*mixed)
+    mixed = [add(*[part[t] for part in mixed]) for t in range(TILES)]
     mixed = [mixed[0], send(mixed[1], perm=NEXT)]
     grad, dq = lax.optimization_barrier((grad, dq))
-    grad, dq = add(*grad), add(*dq)
+    dq = [add(*[part[t] for part in dq]) for t in range(TILES)]
     dq = [dq[0], send(dq[1], perm=NEXT)]
+    grad = add(*grad)
     out_shape = jax.ShapeDtypeStruct((CHUNK, group * width), BF16)
     attended, grad_query = pl.pallas_call(
         functools.partial(combine, group, width),

time: 112 us -> 115 us (1.027)
  the two profiles are of different devices: /device:TPU:32 before, /device:TPU:2 now
where the time goes in v6:
time: 115 us; the launch traced here: 114 us
  starting transfers between devices  54.2 us (47%)
  waiting for transfers between devices  37.9 us (33%)
  Pallas kernels  17.1 us (15%)
  local copies, waits for them, and re-layouts  3.38 us (3%)
    ppermute x2, starting transfers between devices, local(): one, two = (send(far[0], perm=NEAR), send(far[1], perm=REST))  8.54 us
    pallas_call x3, Pallas kernels, run_backward(): pl.pallas_call(functools.partial(backward, group, width, span, begins, en...  8.06 us
    ppermute x2, starting transfers between devices, local(): a, b = (send(key_home, perm=NEAR), send(key_home, perm=REST))  6.85 us
    ppermute x2, waiting for transfers between devices, local(): a, b = (send(key_home, perm=NEAR), send(key_home, perm=REST))  6.62 us
    pallas_call x1, Pallas kernels, run_forward(): pl.pallas_call(functools.partial(forward, group, width), out_shape=[jax.S...  6.41 us
    ppermute x2, waiting for transfers between devices, local(): ga, gb = (send(ga, perm=NEAR), send(gb, perm=REST))  5.35 us
    ppermute x3, waiting for transfers between devices, local(): keys = [held] + [send(held, perm=X[n]) for n in range(1, 4)]  5.29 us
    ppermute x1, waiting for transfers between devices, local(): held = jnp.concatenate([key_home, a, b, send(a, perm=REST)], axis=0)  4.91 us
  transfers between devices with their start and end apart: 30, of which 14 were waited for; matrix products, arithmetic and copies ran while one was open for 4% of the time, Pallas kernels for 5%

profile of v6, /device:TPU:2, one launch (start us, length us, event | category | flops | bytes accessed | tf_op | source)
XLA Modules:
  0.0 114.4 jit_solution(5866452482013889306)
XLA Ops:
  2.4 1.9 %collective-permute-start = (bf16[128,1024]{1,0:T(8,128)(2,1)}, bf16[128,1024]{1,0:T(8,128)(2,1)S(1)}, u32[]{:S(2)}, u32[]{:S(2)}) collective-permute-start(bf16[128,1024]{1,0:T(8,128)(2,1)} %get-tuple-element.61.refs_0_), channel_id=1, source_target_pairs={{0,32},{2,34},{4,36},{6,38},{8,40},{10,42},{12,44},{14,46},{16,48}... | collective-permute-start | bytes 786440 | tf_op jit(solution)/shard_map/ppermute | solution.py:355
  4.3 5.4 %collective-permute-start.2 = (bf16[128,256]{1,0:T(8,128)(2,1)}, bf16[128,256]{1,0:T(8,128)(2,1)S(1)}, u32[]{:S(2)}, u32[]{:S(2)}) collective-permute-start(bf16[128,256]{1,0:T(8,128)(2,1)} %get-tuple-element.62), channel_id=1, source_target_pairs={{0,192},{2,194},{4,196},{6,198},{8,200},{10,202},{12,204},{14,206}... | collective-permute-start | bytes 196616 | tf_op jit(solution)/shard_map/ppermute | solution.py:356
  12.2 6.6 %collective-permute-done.2 = bf16[128,256]{1,0:T(8,128)(2,1)S(1)} collective-permute-done((bf16[128,256]{1,0:T(8,128)(2,1)}, bf16[128,256]{1,0:T(8,128)(2,1)S(1)}, u32[]{:S(2)}, u32[]{:S(2)}) %collective-permute-start.2) | collective-permute-done | bytes 65568 | tf_op jit(solution)/shard_map/ppermute | solution.py:356
  18.8 3.1 %collective-permute-start.4 = (bf16[256,1024]{1,0:T(8,128)(2,1)S(1)}, bf16[256,1024]{1,0:T(8,128)(2,1)S(1)}, u32[]{:S(2)}, u32[]{:S(2)}) collective-permute-start(bf16[256,1024]{1,0:T(8,128)(2,1)S(1)} %constant_dynamic-update-slice_fusion), channel_id=1, source_target_pairs={{0,6},{2,4},{4,2},{6,0},{8,14},{10,12},{12,10},{14,8},{16,22},{18,... | collective-permute-start | bytes 1572872 | tf_op jit(solution)/shard_map/ppermute | solution.py:359
  24.4 4.9 %collective-permute-done.7 = bf16[128,256]{1,0:T(8,128)(2,1)S(1)} collective-permute-done((bf16[128,256]{1,0:T(8,128)(2,1)S(1)}, bf16[128,256]{1,0:T(8,128)(2,1)S(1)}, u32[]{:S(2)}, u32[]{:S(2)}) %collective-permute-start.7) | collective-permute-done | bytes 65568 | tf_op jit(solution)/shard_map/ppermute | solution.py:360
  33.4 2.0 %collective-permute-start.5 = (bf16[128,1024]{1,0:T(8,128)(2,1)S(1)}, bf16[128,1024]{1,0:T(8,128)(2,1)S(1)}, u32[]{:S(2)}, u32[]{:S(2)}) collective-permute-start(bf16[128,1024]{1,0:T(8,128)(2,1)S(1)} %slice.162), channel_id=1, source_target_pairs={{0,2},{2,0},{4,6},{6,4},{8,10},{10,8},{12,14},{14,12},{16,18},{18,... | collective-permute-start | bytes 786440 | tf_op jit(solution)/shard_map/ppermute | solution.py:362
  36.9 2.4 %collective-permute-done.10.refs_9_ = bf16[512,256]{1,0:T(8,128)(2,1)S(1)} collective-permute-done((bf16[512,256]{1,0:T(8,128)(2,1)S(1)}, bf16[512,256]{1,0:T(8,128)(2,1)S(1)}, u32[]{:S(2)}, u32[]{:S(2)}) %collective-permute-start.10) | collective-permute-done | bytes 262176 | tf_op jit(solution)/shard_map/ppermute | solution.py:361
  40.3 1.9 %collective-permute-done.8.refs_7_ = bf16[512,256]{1,0:T(8,128)(2,1)S(1)} collective-permute-done((bf16[512,256]{1,0:T(8,128)(2,1)S(1)}, bf16[512,256]{1,0:T(8,128)(2,1)S(1)}, u32[]{:S(2)}, u32[]{:S(2)}) %collective-permute-start.8) | collective-permute-done | bytes 262176 | tf_op jit(solution)/shard_map/ppermute | solution.py:361
  43.9 6.4 %forward.1 = (bf16[2,4,128,512]{3,2,1,0:T(8,128)(2,1)S(1)}, f32[2,12,512]{2,1,0:T(8,128)S(1)}, bf16[2,4,512,128]{3,2,1,0:T(8,128)(2,1)S(1)}, bf16[2,4,512,128]{3...) custom-call(s32[16]{0:T(128)S(1)} %concatenate.18.sc, ...), custom_call_target="tpu_custom_call" | custom-call | flops 12884901888 | bytes 8388608 | tf_op jit(solution)/shard_map/forward/pallas_call | solution.py:300
  50.4 4.3 %collective-permute-done.11 = f32[2,12,512]{2,1,0:T(8,128)S(1)} collective-permute-done((f32[2,12,512]{2,1,0:T(8,128)S(1)}, f32[2,12,512]{2,1,0:T(8,128)S(1)}, u32[]{:S(2)}, u32[]{:S(2)}) %collective-permute-start.11) | collective-permute-done | bytes 49184 | tf_op jit(solution)/shard_map/ppermute | solution.py:373
  56.2 2.9 %collective-permute-start.12 = (f32[2,12,512]{2,1,0:T(8,128)S(1)}, f32[2,12,512]{2,1,0:T(8,128)S(1)}, u32[]{:S(2)}, u32[]{:S(2)}) collective-permute-start(f32[2,12,512]{2,1,0:T(8,128)S(1)} %pad_maximum_fusion.2.refs_0_), channel_id=1, source_target_pairs={{0,2},{2,0},{4,6},{6,4},{8,10},{10,8},{12,14},{14,12},{16,18},{18,... | collective-permute-start | bytes 147464 | tf_op jit(solution)/shard_map/ppermute | solution.py:385
  59.1 2.1 %collective-permute-done.14.refs_3_ = f32[2,12,512]{2,1,0:T(8,128)S(1)} collective-permute-done((f32[2,12,512]{2,1,0:T(8,128)S(1)}, f32[2,12,512]{2,1,0:T(8,128)S(1)}, u32[]{:S(2)}, u32[]{:S(2)}) %collective-permute-start.14) | collective-permute-done | bytes 49184 | tf_op jit(solution)/shard_map/ppermute | solution.py:385
  62.0 2.8 %backward_begin.1 = (bf16[2,256,256]{2,1,0:T(8,128)(2,1)S(1)}, bf16[2,512,128]{2,1,0:T(8,128)(2,1)S(1)}, bf16[2,512,128]{2,1,0:T(8,128)(2,1)S(1)}, bf16[2,512,12...) custom-call(s32[16]{0:T(128)S(1)} %concatenate.18.sc, ...), custom_call_target="tpu_custom_call" | custom-call | flops 5368709120 | bytes 8388608 | tf_op jit(solution)/shard_map/backward_begin/pallas_call | solution.py:324
  66.1 7.4 %collective-permute-start.15 = (bf16[256,256]{1,0:T(8,128)(2,1)S(1)}, bf16[256,256]{1,0:T(8,128)(2,1)S(1)}, u32[]{:S(2)}, u32[]{:S(2)}) collective-permute-start(bf16[256,256]{1,0:T(8,128)(2,1)S(1)} %get-tuple-element.131), channel_id=1, source_target_pairs={{0,192},{2,194},{4,196},{6,198},{8,200},{10,202},{12,204},{14,206}... | collective-permute-start | bytes 393224 | tf_op jit(solution)/shard_map/ppermute | solution.py:391
  73.4 3.4 %collective-permute-start.18 = (bf16[2,512,128]{2,1,0:T(8,128)(2,1)S(1)}, bf16[2,512,128]{2,1,0:T(8,128)(2,1)S(1)}, u32[]{:S(2)}, u32[]{:S(2)}) collective-permute-start(bf16[2,512,128]{2,1,0:T(8,128)(2,1)S(1)} %get-tuple-element.91), channel_id=1, source_target_pairs={{0,4},{2,6},{4,0},{6,2},{8,12},{10,14},{12,8},{14,10},{16,20},{18,... | collective-permute-start | bytes 786440 | tf_op jit(solution)/shard_map/ppermute | solution.py:392
  78.1 2.7 %backward_middle.1 = (bf16[4,256,256]{2,1,0:T(8,128)(2,1)S(1)}, f32[2,4,128,512]{3,2,1,0:T(8,128)S(1)}, f32[2,4,1,512]{3,2,1,0:T(1,128)S(1)}, f32[2,4,1,512]{3,2,1,0:T(1,128)S(1)}) custom-call(s32[16]{0:T(128)S(1)} %concatenate.18.sc, bf16[2,4,512,128]{3,2,1,0:T(8,128)(2,1)S(1)} %get-tuple-element.66.q_s, ...), custom_call_target="tpu_custom_call" | custom-call | flops 10737418240 | bytes 8388608 | tf_op jit(solution)/shard_map/backward_middle/pallas_call | solution.py:324
  81.1 3.4 %collective-permute-start.21 = (bf16[512,256]{1,0:T(8,128)(2,1)S(1)}, bf16[512,256]{1,0:T(8,128)(2,1)S(1)}, u32[]{:S(2)}, u32[]{:S(2)}) collective-permute-start(bf16[512,256]{1,0:T(8,128)(2,1)S(1)} %get-tuple-element.95), channel_id=1, source_target_pairs={{0,192},{2,194},{4,196},{6,198},{8,200},{10,202},{12,204},{14,206}... | collective-permute-start | bytes 786440 | tf_op jit(solution)/shard_map/ppermute | solution.py:397
  84.5 2.6 %backward_end.1 = (bf16[2,256,256]{2,1,0:T(8,128)(2,1)S(1)}, bf16[2,512,128]{2,1,0:T(8,128)(2,1)S(1)}, bf16[2,512,128]{2,1,0:T(8,128)(2,1)S(1)}, bf16[2,512,128]...) custom-call(s32[16]{0:T(128)S(1)} %concatenate.18.sc, bf16[2,4,512,128]{3,2,1,0:T(8,128)(2,1)S(1)} %get-tuple-element.66.q_s, ...), custom_call_target="tpu_custom_call" | custom-call | flops 5368709120 | bytes 8388608 | tf_op jit(solution)/shard_map/backward_end/pallas_call | solution.py:324
  87.1 3.6 %collective-permute-done.20 = bf16[512,256]{1,0:T(8,128)(2,1)S(1)} collective-permute-done((bf16[512,256]{1,0:T(8,128)(2,1)S(1)}, bf16[512,256]{1,0:T(8,128)(2,1)S(1)}, u32[]{:S(2)}, u32[]{:S(2)}) %collective-permute-start.20) | collective-permute-done | bytes 262176 | tf_op jit(solution)/shard_map/ppermute | solution.py:397
  92.6 2.4 %collective-permute-start.24 = (bf16[128,256]{1,0:T(8,128)(2,1)S(1)}, bf16[128,256]{1,0:T(8,128)(2,1)S(1)}, u32[]{:S(2)}, u32[]{:S(2)}) collective-permute-start(bf16[128,256]{1,0:T(8,128)(2,1)S(1)} %get-tuple-element.126), channel_id=1, source_target_pairs={{0,24},{2,26},{4,28},{6,30},{8,16},{10,18},{12,20},{14,22},{16,8},... | collective-permute-start | bytes 196616 | tf_op jit(solution)/shard_map/ppermute | solution.py:404
  99.1 2.3 %collective-permute-start.22 = (bf16[128,256]{1,0:T(8,128)(2,1)S(1)}, bf16[128,256]{1,0:T(8,128)(2,1)S(1)}, u32[]{:S(2)}, u32[]{:S(2)}) collective-permute-start(bf16[128,256]{1,0:T(8,128)(2,1)S(1)} %get-tuple-element.128), channel_id=1, source_target_pairs={{0,16},{2,18},{4,20},{6,22},{8,24},{10,26},{12,28},{14,30},{16,0},... | collective-permute-start | bytes 196616 | tf_op jit(solution)/shard_map/ppermute | solution.py:404
  101.6 3.3 %collective-permute-done.23 = bf16[128,256]{1,0:T(8,128)(2,1)S(1)} collective-permute-done((bf16[128,256]{1,0:T(8,128)(2,1)S(1)}, bf16[128,256]{1,0:T(8,128)(2,1)S(1)}, u32[]{:S(2)}, u32[]{:S(2)}) %collective-permute-start.23) | collective-permute-done | bytes 65568 | tf_op jit(solution)/shard_map/ppermute | solution.py:404
  104.9 3.5 %collective-permute-start.28 = (bf16[512,128]{1,0:T(8,128)(2,1)S(1)}, bf16[512,128]{1,0:T(8,128)(2,1)S(1)}, u32[]{:S(2)}, u32[]{:S(2)}) collective-permute-start(bf16[512,128]{1,0:T(8,128)(2,1)S(1)} %get-tuple-element.120), channel_id=1, source_target_pairs={{0,32},{2,34},{4,36},{6,38},{8,40},{10,42},{12,44},{14,46},{16,48}... | collective-permute-start | bytes 393224 | tf_op jit(solution)/shard_map/ppermute | solution.py:406
  111.3 2.3 %collective-permute-done.29.refs_3_ = bf16[512,128]{1,0:T(8,128)(2,1)S(1)} collective-permute-done((bf16[512,128]{1,0:T(8,128)(2,1)S(1)}, bf16[512,128]{1,0:T(8,128)(2,1)S(1)}, u32[]{:S(2)}, u32[]{:S(2)}) %collective-permute-start.29) | collective-permute-done | bytes 131104 | tf_op jit(solution)/shard_map/ppermute | solution.py:409
  (70 shorter events, 30.0 us)
Async XLA Ops:
  2.4 16.4 %collective-permute-start = (bf16[128,1024]{1,0:T(8,128)(2,1)}, bf16[128,1024]{1,0:T(8,128)(2,1)S(1)}, u32[]{:S(2)}, u32[]{:S(2)}) collective-permute-start(bf16[128,1024]{1,0:T(8,128)(2,1)} %get-tuple-element.61.refs_0_), channel_id=1, source_target_pairs={{0,32},{2,34},{4,36},{6,38},{8,40},{10,42},{12,44},{14,46},{16,48}... | collective-permute-start | bytes 786440 | tf_op jit(solution)/shard_map/ppermute | solution.py:355
  4.3 14.4 %collective-permute-start.2 = (bf16[128,256]{1,0:T(8,128)(2,1)}, bf16[128,256]{1,0:T(8,128)(2,1)S(1)}, u32[]{:S(2)}, u32[]{:S(2)}) collective-permute-start(bf16[128,256]{1,0:T(8,128)(2,1)} %get-tuple-element.62), channel_id=1, source_target_pairs={{0,192},{2,194},{4,196},{6,198},{8,200},{10,202},{12,204},{14,206}... | collective-permute-start | bytes 196616 | tf_op jit(solution)/shard_map/ppermute | solution.py:356
  9.7 9.0 %collective-permute-start.1 = (bf16[128,256]{1,0:T(8,128)(2,1)}, bf16[128,256]{1,0:T(8,128)(2,1)S(1)}, u32[]{:S(2)}, u32[]{:S(2)}) collective-permute-start(bf16[128,256]{1,0:T(8,128)(2,1)} %get-tuple-element.62), channel_id=1, source_target_pairs={{0,64},{2,66},{4,68},{6,70},{8,72},{10,74},{12,76},{14,78},{16,80}... | collective-permute-start | bytes 196616 | tf_op jit(solution)/shard_map/ppermute | solution.py:356
  18.8 14.6 %collective-permute-start.4 = (bf16[256,1024]{1,0:T(8,128)(2,1)S(1)}, bf16[256,1024]{1,0:T(8,128)(2,1)S(1)}, u32[]{:S(2)}, u32[]{:S(2)}) collective-permute-start(bf16[256,1024]{1,0:T(8,128)(2,1)S(1)} %constant_dynamic-update-slice_fusion), channel_id=1, source_target_pairs={{0,6},{2,4},{4,2},{6,0},{8,14},{10,12},{12,10},{14,8},{16,22},{18,... | collective-permute-start | bytes 1572872 | tf_op jit(solution)/shard_map/ppermute | solution.py:359
  21.9 13.5 %collective-permute-start.3 = (bf16[256,1024]{1,0:T(8,128)(2,1)S(1)}, bf16[256,1024]{1,0:T(8,128)(2,1)S(1)}, u32[]{:S(2)}, u32[]{:S(2)}) collective-permute-start(bf16[256,1024]{1,0:T(8,128)(2,1)S(1)} %constant_dynamic-update-slice_fusion), channel_id=1, source_target_pairs={{0,2},{2,0},{4,6},{6,4},{8,10},{10,8},{12,14},{14,12},{16,18},{18,... | collective-permute-start | bytes 1572872 | tf_op jit(solution)/shard_map/ppermute | solution.py:359
  29.3 10.0 %collective-permute-start.10 = (bf16[512,256]{1,0:T(8,128)(2,1)S(1)}, bf16[512,256]{1,0:T(8,128)(2,1)S(1)}, u32[]{:S(2)}, u32[]{:S(2)}) collective-permute-start(bf16[512,256]{1,0:T(8,128)(2,1)S(1)} %constant_dynamic-update-slice_fusion.2.refs_6_), channel_id=1, source_target_pairs={{0,24},{2,26},{4,28},{6,30},{8,16},{10,18},{12,20},{14,22},{16,8},... | collective-permute-start | bytes 786440 | tf_op jit(solution)/shard_map/ppermute | solution.py:361
  30.8 9.5 %collective-permute-start.9 = (bf16[512,256]{1,0:T(8,128)(2,1)S(1)}, bf16[512,256]{1,0:T(8,128)(2,1)S(1)}, u32[]{:S(2)}, u32[]{:S(2)}) collective-permute-start(bf16[512,256]{1,0:T(8,128)(2,1)S(1)} %constant_dynamic-update-slice_fusion.2.refs_6_), channel_id=1, source_target_pairs={{0,8},{2,10},{4,12},{6,14},{8,0},{10,2},{12,4},{14,6},{16,24},{18,... | collective-permute-start | bytes 786440 | tf_op jit(solution)/shard_map/ppermute | solution.py:361
  31.9 10.3 %collective-permute-start.8 = (bf16[512,256]{1,0:T(8,128)(2,1)S(1)}, bf16[512,256]{1,0:T(8,128)(2,1)S(1)}, u32[]{:S(2)}, u32[]{:S(2)}) collective-permute-start(bf16[512,256]{1,0:T(8,128)(2,1)S(1)} %constant_dynamic-update-slice_fusion.2.refs_6_), channel_id=1, source_target_pairs={{0,16},{2,18},{4,20},{6,22},{8,24},{10,26},{12,28},{14,30},{16,0},... | collective-permute-start | bytes 786440 | tf_op jit(solution)/shard_map/ppermute | solution.py:361
  33.4 8.8 %collective-permute-start.5 = (bf16[128,1024]{1,0:T(8,128)(2,1)S(1)}, bf16[128,1024]{1,0:T(8,128)(2,1)S(1)}, u32[]{:S(2)}, u32[]{:S(2)}) collective-permute-start(bf16[128,1024]{1,0:T(8,128)(2,1)S(1)} %slice.162), channel_id=1, source_target_pairs={{0,2},{2,0},{4,6},{6,4},{8,10},{10,8},{12,14},{14,12},{16,18},{18,... | collective-permute-start | bytes 786440 | tf_op jit(solution)/shard_map/ppermute | solution.py:362
  36.1 7.8 %collective-permute-start.6 = (bf16[128,1024]{1,0:T(8,128)(2,1)}, bf16[128,1024]{1,0:T(8,128)(2,1)S(1)}, u32[]{:S(2)}, u32[]{:S(2)}) collective-permute-start(bf16[128,1024]{1,0:T(8,128)(2,1)} %slice.163), channel_id=1, source_target_pairs={{0,6},{2,4},{4,2},{6,0},{8,14},{10,12},{12,10},{14,8},{16,22},{18,... | collective-permute-start | bytes 786440 | tf_op jit(solution)/shard_map/ppermute | solution.py:362
  54.7 6.4 %collective-permute-start.14 = (f32[2,12,512]{2,1,0:T(8,128)S(1)}, f32[2,12,512]{2,1,0:T(8,128)S(1)}, u32[]{:S(2)}, u32[]{:S(2)}) collective-permute-start(f32[2,12,512]{2,1,0:T(8,128)S(1)} %pad_maximum_fusion.2.refs_0_), channel_id=1, source_target_pairs={{0,6},{2,4},{4,2},{6,0},{8,14},{10,12},{12,10},{14,8},{16,22},{18,... | collective-permute-start | bytes 147464 | tf_op jit(solution)/shard_map/ppermute | solution.py:385
  64.9 15.9 %collective-permute-start.16 = (bf16[256,256]{1,0:T(8,128)(2,1)S(1)}, bf16[256,256]{1,0:T(8,128)(2,1)S(1)}, u32[]{:S(2)}, u32[]{:S(2)}) collective-permute-start(bf16[256,256]{1,0:T(8,128)(2,1)S(1)} %get-tuple-element.130), channel_id=1, source_target_pairs={{0,64},{2,66},{4,68},{6,70},{8,72},{10,74},{12,76},{14,78},{16,80}... | collective-permute-start | bytes 393224 | tf_op jit(solution)/shard_map/ppermute | solution.py:391
  66.1 14.8 %collective-permute-start.15 = (bf16[256,256]{1,0:T(8,128)(2,1)S(1)}, bf16[256,256]{1,0:T(8,128)(2,1)S(1)}, u32[]{:S(2)}, u32[]{:S(2)}) collective-permute-start(bf16[256,256]{1,0:T(8,128)(2,1)S(1)} %get-tuple-element.131), channel_id=1, source_target_pairs={{0,192},{2,194},{4,196},{6,198},{8,200},{10,202},{12,204},{14,206}... | collective-permute-start | bytes 393224 | tf_op jit(solution)/shard_map/ppermute | solution.py:391
  73.4 13.6 %collective-permute-start.17 = (bf16[2,512,128]{2,1,0:T(8,128)(2,1)S(1)}, bf16[2,512,128]{2,1,0:T(8,128)(2,1)S(1)}, u32[]{:S(2)}, u32[]{:S(2)}) collective-permute-start(bf16[2,512,128]{2,1,0:T(8,128)(2,1)S(1)} %get-tuple-element.90), channel_id=1, source_target_pairs={{0,2},{2,0},{4,6},{6,4},{8,10},{10,8},{12,14},{14,12},{16,18},{18,... | collective-permute-start | bytes 786440 | tf_op jit(solution)/shard_map/ppermute | solution.py:392
  73.4 13.6 %collective-permute-start.18 = (bf16[2,512,128]{2,1,0:T(8,128)(2,1)S(1)}, bf16[2,512,128]{2,1,0:T(8,128)(2,1)S(1)}, u32[]{:S(2)}, u32[]{:S(2)}) collective-permute-start(bf16[2,512,128]{2,1,0:T(8,128)(2,1)S(1)} %get-tuple-element.91), channel_id=1, source_target_pairs={{0,4},{2,6},{4,0},{6,2},{8,12},{10,14},{12,8},{14,10},{16,20},{18,... | collective-permute-start | bytes 786440 | tf_op jit(solution)/shard_map/ppermute | solution.py:392
  76.9 10.2 %collective-permute-start.19 = (bf16[2,512,128]{2,1,0:T(8,128)(2,1)S(1)}, bf16[2,512,128]{2,1,0:T(8,128)(2,1)S(1)}, u32[]{:S(2)}, u32[]{:S(2)}) collective-permute-start(bf16[2,512,128]{2,1,0:T(8,128)(2,1)S(1)} %get-tuple-element.92), channel_id=1, source_target_pairs={{0,6},{2,4},{4,2},{6,0},{8,14},{10,12},{12,10},{14,8},{16,22},{18,... | collective-permute-start | bytes 786440 | tf_op jit(solution)/shard_map/ppermute | solution.py:392
  81.0 9.6 %collective-permute-start.20 = (bf16[512,256]{1,0:T(8,128)(2,1)S(1)}, bf16[512,256]{1,0:T(8,128)(2,1)S(1)}, u32[]{:S(2)}, u32[]{:S(2)}) collective-permute-start(bf16[512,256]{1,0:T(8,128)(2,1)S(1)} %get-tuple-element.94), channel_id=1, source_target_pairs={{0,64},{2,66},{4,68},{6,70},{8,72},{10,74},{12,76},{14,78},{16,80}... | collective-permute-start | bytes 786440 | tf_op jit(solution)/shard_map/ppermute | solution.py:397
  81.1 11.3 %collective-permute-start.21 = (bf16[512,256]{1,0:T(8,128)(2,1)S(1)}, bf16[512,256]{1,0:T(8,128)(2,1)S(1)}, u32[]{:S(2)}, u32[]{:S(2)}) collective-permute-start(bf16[512,256]{1,0:T(8,128)(2,1)S(1)} %get-tuple-element.95), channel_id=1, source_target_pairs={{0,192},{2,194},{4,196},{6,198},{8,200},{10,202},{12,204},{14,206}... | collective-permute-start | bytes 786440 | tf_op jit(solution)/shard_map/ppermute | solution.py:397
  92.6 6.5 %collective-permute-start.24 = (bf16[128,256]{1,0:T(8,128)(2,1)S(1)}, bf16[128,256]{1,0:T(8,128)(2,1)S(1)}, u32[]{:S(2)}, u32[]{:S(2)}) collective-permute-start(bf16[128,256]{1,0:T(8,128)(2,1)S(1)} %get-tuple-element.126), channel_id=1, source_target_pairs={{0,24},{2,26},{4,28},{6,30},{8,16},{10,18},{12,20},{14,22},{16,8},... | collective-permute-start | bytes 196616 | tf_op jit(solution)/shard_map/ppermute | solution.py:404
  95.0 13.3 %collective-permute-start.25 = (bf16[2,512,128]{2,1,0:T(8,128)(2,1)S(1)}, bf16[2,512,128]{2,1,0:T(8,128)(2,1)S(1)}, u32[]{:S(2)}, u32[]{:S(2)}) collective-permute-start(bf16[2,512,128]{2,1,0:T(8,128)(2,1)S(1)} %get-tuple-element.105), channel_id=1, source_target_pairs={{0,4},{2,6},{4,0},{6,2},{8,12},{10,14},{12,8},{14,10},{16,20},{18,... | collective-permute-start | bytes 786440 | tf_op jit(solution)/shard_map/ppermute | solution.py:400
  96.9 11.5 %collective-permute-start.26 = (bf16[2,512,128]{2,1,0:T(8,128)(2,1)S(1)}, bf16[2,512,128]{2,1,0:T(8,128)(2,1)S(1)}, u32[]{:S(2)}, u32[]{:S(2)}) collective-permute-start(bf16[2,512,128]{2,1,0:T(8,128)(2,1)S(1)} %get-tuple-element.106), channel_id=1, source_target_pairs={{0,2},{2,0},{4,6},{6,4},{8,10},{10,8},{12,14},{14,12},{16,18},{18,... | collective-permute-start | bytes 786440 | tf_op jit(solution)/shard_map/ppermute | solution.py:400
  97.4 10.9 %collective-permute-start.27 = (bf16[2,512,128]{2,1,0:T(8,128)(2,1)S(1)}, bf16[2,512,128]{2,1,0:T(8,128)(2,1)S(1)}, u32[]{:S(2)}, u32[]{:S(2)}) collective-permute-start(bf16[2,512,128]{2,1,0:T(8,128)(2,1)S(1)} %get-tuple-element.107), channel_id=1, source_target_pairs={{0,6},{2,4},{4,2},{6,0},{8,14},{10,12},{12,10},{14,8},{16,22},{18,... | collective-permute-start | bytes 786440 | tf_op jit(solution)/shard_map/ppermute | solution.py:400
  99.1 9.2 %collective-permute-start.22 = (bf16[128,256]{1,0:T(8,128)(2,1)S(1)}, bf16[128,256]{1,0:T(8,128)(2,1)S(1)}, u32[]{:S(2)}, u32[]{:S(2)}) collective-permute-start(bf16[128,256]{1,0:T(8,128)(2,1)S(1)} %get-tuple-element.128), channel_id=1, source_target_pairs={{0,16},{2,18},{4,20},{6,22},{8,24},{10,26},{12,28},{14,30},{16,0},... | collective-permute-start | bytes 196616 | tf_op jit(solution)/shard_map/ppermute | solution.py:404
  104.9 6.4 %collective-permute-start.28 = (bf16[512,128]{1,0:T(8,128)(2,1)S(1)}, bf16[512,128]{1,0:T(8,128)(2,1)S(1)}, u32[]{:S(2)}, u32[]{:S(2)}) collective-permute-start(bf16[512,128]{1,0:T(8,128)(2,1)S(1)} %get-tuple-element.120), channel_id=1, source_target_pairs={{0,32},{2,34},{4,36},{6,38},{8,40},{10,42},{12,44},{14,46},{16,48}... | collective-permute-start | bytes 393224 | tf_op jit(solution)/shard_map/ppermute | solution.py:406
  (8 other events, 111.0 us)

commit v7 on v6

--- a/solution.py
+++ b/solution.py
@@ -402,7 +402,7 @@
     _, mixed = lax.optimization_barrier((grad, mixed))
     grad = grad.reshape(4, CHUNK, 2 * width)
     grad = [grad[0]] + [send(grad[n], perm=X[n]) for n in range(1, 4)]
-    mixed = [add(*[part[t] for part in mixed]) for t in range(TILES)]
+    mixed = add(*mixed)
     mixed = [mixed[0], send(mixed[1], perm=NEXT)]
     grad, dq = lax.optimization_barrier((grad, dq))
     dq = [add(*[part[t] for part in dq]) for t in range(TILES)]

time: 115 us -> 113 us (0.983)
  the two profiles are of different devices: /device:TPU:2 before, /device:TPU:32 now
where the time goes in v7:
time: 113 us; the launch traced here: 112 us
  starting transfers between devices  58.4 us (52%)
  waiting for transfers between devices  33.8 us (30%)
  Pallas kernels  14.7 us (13%)
  local copies, waits for them, and re-layouts  3.4 us (3%)
    ppermute x2, starting transfers between devices, local(): one, two = (send(far[0], perm=NEAR), send(far[1], perm=REST))  13.6 us
    pallas_call x3, Pallas kernels, run_backward(): pl.pallas_call(functools.partial(backward, group, width, span, begins, en...  6.69 us
    ppermute x2, starting transfers between devices, local(): a, b = (send(key_home, perm=NEAR), send(key_home, perm=REST))  6.02 us
    ppermute x3, waiting for transfers between devices, local(): grad = [grad[0]] + [send(grad[n], perm=X[n]) for n in range(1, 4)]  5.72 us
    pallas_call x1, Pallas kernels, run_forward(): pl.pallas_call(functools.partial(forward, group, width), out_shape=[jax.S...  5.44 us
    ppermute x3, waiting for transfers between devices, local(): keys = [held] + [send(held, perm=X[n]) for n in range(1, 4)]  4.92 us
    ppermute x3, starting transfers between devices, local(): grad = [grad[0]] + [send(grad[n], perm=X[n]) for n in range(1, 4)]  4.71 us
    ppermute x3, starting transfers between devices, local(): mixed = [mixed[0]] + [send(mixed[s], perm=Y[s]) for s in range(1, SLOTS)]  4.7 us
  transfers between devices with their start and end apart: 30, of which 16 were waited for; matrix products, arithmetic and copies ran while one was open for 4% of the time, Pallas kernels for 5%

profile of v7, /device:TPU:32, one launch (start us, length us, event | category | flops | bytes accessed | tf_op | source)
XLA Modules:
  0.0 112.1 jit_solution(16908054421655842106)
XLA Ops:
  4.3 4.6 %collective-permute-start.2 = (bf16[128,256]{1,0:T(8,128)(2,1)}, bf16[128,256]{1,0:T(8,128)(2,1)S(1)}, u32[]{:S(2)}, u32[]{:S(2)}) collective-permute-start(bf16[128,256]{1,0:T(8,128)(2,1)} %get-tuple-element.62), channel_id=1, source_target_pairs={{0,192},{2,194},{4,196},{6,198},{8,200},{10,202},{12,204},{14,206}... | collective-permute-start | bytes 196616 | tf_op jit(solution)/shard_map/ppermute | solution.py:356
  11.7 3.4 %collective-permute-done.1 = bf16[128,256]{1,0:T(8,128)(2,1)S(1)} collective-permute-done((bf16[128,256]{1,0:T(8,128)(2,1)}, bf16[128,256]{1,0:T(8,128)(2,1)S(1)}, u32[]{:S(2)}, u32[]{:S(2)}) %collective-permute-start.1) | collective-permute-done | bytes 65568 | tf_op jit(solution)/shard_map/ppermute | solution.py:356
  15.1 3.1 %collective-permute-start.4 = (bf16[256,1024]{1,0:T(8,128)(2,1)S(1)}, bf16[256,1024]{1,0:T(8,128)(2,1)S(1)}, u32[]{:S(2)}, u32[]{:S(2)}) collective-permute-start(bf16[256,1024]{1,0:T(8,128)(2,1)S(1)} %constant_dynamic-update-slice_fusion), channel_id=1, source_target_pairs={{0,6},{2,4},{4,2},{6,0},{8,14},{10,12},{12,10},{14,8},{16,22},{18,... | collective-permute-start | bytes 1572872 | tf_op jit(solution)/shard_map/ppermute | solution.py:359
  19.2 3.1 %collective-permute-start.7 = (bf16[128,256]{1,0:T(8,128)(2,1)S(1)}, bf16[128,256]{1,0:T(8,128)(2,1)S(1)}, u32[]{:S(2)}, u32[]{:S(2)}) collective-permute-start(bf16[128,256]{1,0:T(8,128)(2,1)S(1)} %collective-permute-done.1), channel_id=1, source_target_pairs={{0,192},{2,194},{4,196},{6,198},{8,200},{10,202},{12,204},{14,206}... | collective-permute-start | bytes 196616 | tf_op jit(solution)/shard_map/ppermute | solution.py:360
  22.3 4.0 %collective-permute-done.7 = bf16[128,256]{1,0:T(8,128)(2,1)S(1)} collective-permute-done((bf16[128,256]{1,0:T(8,128)(2,1)S(1)}, bf16[128,256]{1,0:T(8,128)(2,1)S(1)}, u32[]{:S(2)}, u32[]{:S(2)}) %collective-permute-start.7) | collective-permute-done | bytes 65568 | tf_op jit(solution)/shard_map/ppermute | solution.py:360
  26.3 2.8 %collective-permute-start.10 = (bf16[512,256]{1,0:T(8,128)(2,1)S(1)}, bf16[512,256]{1,0:T(8,128)(2,1)S(1)}, u32[]{:S(2)}, u32[]{:S(2)}) collective-permute-start(bf16[512,256]{1,0:T(8,128)(2,1)S(1)} %constant_dynamic-update-slice_fusion.2.refs_6_), channel_id=1, source_target_pairs={{0,24},{2,26},{4,28},{6,30},{8,16},{10,18},{12,20},{14,22},{16,8},... | collective-permute-start | bytes 786440 | tf_op jit(solution)/shard_map/ppermute | solution.py:361
  33.8 3.3 %collective-permute-done.10.refs_9_ = bf16[512,256]{1,0:T(8,128)(2,1)S(1)} collective-permute-done((bf16[512,256]{1,0:T(8,128)(2,1)S(1)}, bf16[512,256]{1,0:T(8,128)(2,1)S(1)}, u32[]{:S(2)}, u32[]{:S(2)}) %collective-permute-start.10) | collective-permute-done | bytes 262176 | tf_op jit(solution)/shard_map/ppermute | solution.py:361
  38.7 2.2 %collective-permute-done.6.refs_5_ = bf16[128,1024]{1,0:T(8,128)(2,1)S(1)} collective-permute-done((bf16[128,1024]{1,0:T(8,128)(2,1)}, bf16[128,1024]{1,0:T(8,128)(2,1)S(1)}, u32[]{:S(2)}, u32[]{:S(2)}) %collective-permute-start.6) | collective-permute-done | bytes 262176 | tf_op jit(solution)/shard_map/ppermute | solution.py:362
  40.9 5.4 %forward.1 = (bf16[2,4,128,512]{3,2,1,0:T(8,128)(2,1)S(1)}, f32[2,12,512]{2,1,0:T(8,128)S(1)}, bf16[2,4,512,128]{3,2,1,0:T(8,128)(2,1)S(1)}, bf16[2,4,512,128]{3...) custom-call(s32[16]{0:T(128)S(1)} %concatenate.18.sc, ...), custom_call_target="tpu_custom_call" | custom-call | flops 12884901888 | bytes 8388608 | tf_op jit(solution)/shard_map/forward/pallas_call | solution.py:300
  48.3 2.4 %collective-permute-done.11 = f32[2,12,512]{2,1,0:T(8,128)S(1)} collective-permute-done((f32[2,12,512]{2,1,0:T(8,128)S(1)}, f32[2,12,512]{2,1,0:T(8,128)S(1)}, u32[]{:S(2)}, u32[]{:S(2)}) %collective-permute-start.11) | collective-permute-done | bytes 49184 | tf_op jit(solution)/shard_map/ppermute | solution.py:373
  53.0 2.1 %collective-permute-start.12 = (f32[2,12,512]{2,1,0:T(8,128)S(1)}, f32[2,12,512]{2,1,0:T(8,128)S(1)}, u32[]{:S(2)}, u32[]{:S(2)}) collective-permute-start(f32[2,12,512]{2,1,0:T(8,128)S(1)} %pad_maximum_fusion.2.refs_0_), channel_id=1, source_target_pairs={{0,2},{2,0},{4,6},{6,4},{8,10},{10,8},{12,14},{14,12},{16,18},{18,... | collective-permute-start | bytes 147464 | tf_op jit(solution)/shard_map/ppermute | solution.py:385
  55.1 2.1 %collective-permute-done.14.refs_3_ = f32[2,12,512]{2,1,0:T(8,128)S(1)} collective-permute-done((f32[2,12,512]{2,1,0:T(8,128)S(1)}, f32[2,12,512]{2,1,0:T(8,128)S(1)}, u32[]{:S(2)}, u32[]{:S(2)}) %collective-permute-start.14) | collective-permute-done | bytes 49184 | tf_op jit(solution)/shard_map/ppermute | solution.py:385
  59.3 4.7 %collective-permute-start.16 = (bf16[256,256]{1,0:T(8,128)(2,1)S(1)}, bf16[256,256]{1,0:T(8,128)(2,1)S(1)}, u32[]{:S(2)}, u32[]{:S(2)}) collective-permute-start(bf16[256,256]{1,0:T(8,128)(2,1)S(1)} %get-tuple-element.130), channel_id=1, source_target_pairs={{0,64},{2,66},{4,68},{6,70},{8,72},{10,74},{12,76},{14,78},{16,80}... | collective-permute-start | bytes 393224 | tf_op jit(solution)/shard_map/ppermute | solution.py:391
  64.0 9.0 %collective-permute-start.15 = (bf16[256,256]{1,0:T(8,128)(2,1)S(1)}, bf16[256,256]{1,0:T(8,128)(2,1)S(1)}, u32[]{:S(2)}, u32[]{:S(2)}) collective-permute-start(bf16[256,256]{1,0:T(8,128)(2,1)S(1)} %get-tuple-element.131), channel_id=1, source_target_pairs={{0,192},{2,194},{4,196},{6,198},{8,200},{10,202},{12,204},{14,206}... | collective-permute-start | bytes 393224 | tf_op jit(solution)/shard_map/ppermute | solution.py:391
  73.0 2.6 %collective-permute-start.18 = (bf16[2,512,128]{2,1,0:T(8,128)(2,1)S(1)}, bf16[2,512,128]{2,1,0:T(8,128)(2,1)S(1)}, u32[]{:S(2)}, u32[]{:S(2)}) collective-permute-start(bf16[2,512,128]{2,1,0:T(8,128)(2,1)S(1)} %get-tuple-element.91), channel_id=1, source_target_pairs={{0,4},{2,6},{4,0},{6,2},{8,12},{10,14},{12,8},{14,10},{16,20},{18,... | collective-permute-start | bytes 786440 | tf_op jit(solution)/shard_map/ppermute | solution.py:392
  75.6 2.1 %collective-permute-start.19 = (bf16[2,512,128]{2,1,0:T(8,128)(2,1)S(1)}, bf16[2,512,128]{2,1,0:T(8,128)(2,1)S(1)}, u32[]{:S(2)}, u32[]{:S(2)}) collective-permute-start(bf16[2,512,128]{2,1,0:T(8,128)(2,1)S(1)} %get-tuple-element.92), channel_id=1, source_target_pairs={{0,6},{2,4},{4,2},{6,0},{8,14},{10,12},{12,10},{14,8},{16,22},{18,... | collective-permute-start | bytes 786440 | tf_op jit(solution)/shard_map/ppermute | solution.py:392
  77.7 2.8 %backward_middle.1 = (bf16[4,256,256]{2,1,0:T(8,128)(2,1)S(1)}, f32[2,4,128,512]{3,2,1,0:T(8,128)S(1)}, f32[2,4,1,512]{3,2,1,0:T(1,128)S(1)}, f32[2,4,1,512]{3,2,1,0:T(1,128)S(1)}) custom-call(s32[16]{0:T(128)S(1)} %concatenate.18.sc, bf16[2,4,512,128]{3,2,1,0:T(8,128)(2,1)S(1)} %get-tuple-element.66.q_s, ...), custom_call_target="tpu_custom_call" | custom-call | flops 10737418240 | bytes 8388608 | tf_op jit(solution)/shard_map/backward_middle/pallas_call | solution.py:324
  80.7 3.2 %collective-permute-start.21 = (bf16[512,256]{1,0:T(8,128)(2,1)S(1)}, bf16[512,256]{1,0:T(8,128)(2,1)S(1)}, u32[]{:S(2)}, u32[]{:S(2)}) collective-permute-start(bf16[512,256]{1,0:T(8,128)(2,1)S(1)} %get-tuple-element.95), channel_id=1, source_target_pairs={{0,192},{2,194},{4,196},{6,198},{8,200},{10,202},{12,204},{14,206}... | collective-permute-start | bytes 786440 | tf_op jit(solution)/shard_map/ppermute | solution.py:397
  84.0 2.7 %backward_end.1 = (bf16[2,256,256]{2,1,0:T(8,128)(2,1)S(1)}, bf16[2,512,128]{2,1,0:T(8,128)(2,1)S(1)}, bf16[2,512,128]{2,1,0:T(8,128)(2,1)S(1)}, bf16[2,512,128]...) custom-call(s32[16]{0:T(128)S(1)} %concatenate.18.sc, bf16[2,4,512,128]{3,2,1,0:T(8,128)(2,1)S(1)} %get-tuple-element.66.q_s, ...), custom_call_target="tpu_custom_call" | custom-call | flops 5368709120 | bytes 8388608 | tf_op jit(solution)/shard_map/backward_end/pallas_call | solution.py:324
  86.7 4.3 %collective-permute-done.19 = bf16[2,512,128]{2,1,0:T(8,128)(2,1)S(1)} collective-permute-done((bf16[2,512,128]{2,1,0:T(8,128)(2,1)S(1)}, bf16[2,512,128]{2,1,0:T(8,128)(2,1)S(1)}, u32[]{:S(2)}, u32[]{:S(2)}) %collective-permute-start.19) | collective-permute-done | bytes 262176 | tf_op jit(solution)/shard_map/ppermute | solution.py:392
  91.0 3.0 %collective-permute-start.26 = (bf16[2,512,128]{2,1,0:T(8,128)(2,1)S(1)}, bf16[2,512,128]{2,1,0:T(8,128)(2,1)S(1)}, u32[]{:S(2)}, u32[]{:S(2)}) collective-permute-start(bf16[2,512,128]{2,1,0:T(8,128)(2,1)S(1)} %get-tuple-element.106), channel_id=1, source_target_pairs={{0,2},{2,0},{4,6},{6,4},{8,10},{10,8},{12,14},{14,12},{16,18},{18,... | collective-permute-start | bytes 786440 | tf_op jit(solution)/shard_map/ppermute | solution.py:400
  95.3 3.8 %collective-permute-start.24 = (bf16[128,256]{1,0:T(8,128)(2,1)S(1)}, bf16[128,256]{1,0:T(8,128)(2,1)S(1)}, u32[]{:S(2)}, u32[]{:S(2)}) collective-permute-start(bf16[128,256]{1,0:T(8,128)(2,1)S(1)} %get-tuple-element.126), channel_id=1, source_target_pairs={{0,24},{2,26},{4,28},{6,30},{8,16},{10,18},{12,20},{14,22},{16,8},... | collective-permute-start | bytes 196616 | tf_op jit(solution)/shard_map/ppermute | solution.py:404
  102.0 2.9 %collective-permute-done.23 = bf16[128,256]{1,0:T(8,128)(2,1)S(1)} collective-permute-done((bf16[128,256]{1,0:T(8,128)(2,1)S(1)}, bf16[128,256]{1,0:T(8,128)(2,1)S(1)}, u32[]{:S(2)}, u32[]{:S(2)}) %collective-permute-start.23) | collective-permute-done | bytes 65568 | tf_op jit(solution)/shard_map/ppermute | solution.py:404
  107.9 2.0 %collective-permute-done.28.refs_2_ = bf16[512,128]{1,0:T(8,128)(2,1)S(1)} collective-permute-done((bf16[512,128]{1,0:T(8,128)(2,1)S(1)}, bf16[512,128]{1,0:T(8,128)(2,1)S(1)}, u32[]{:S(2)}, u32[]{:S(2)}) %collective-permute-start.28) | collective-permute-done | bytes 131104 | tf_op jit(solution)/shard_map/ppermute | solution.py:406
  (71 shorter events, 29.7 us)
Async XLA Ops:
  2.4 12.7 %collective-permute-start = (bf16[128,1024]{1,0:T(8,128)(2,1)}, bf16[128,1024]{1,0:T(8,128)(2,1)S(1)}, u32[]{:S(2)}, u32[]{:S(2)}) collective-permute-start(bf16[128,1024]{1,0:T(8,128)(2,1)} %get-tuple-element.61.refs_0_), channel_id=1, source_target_pairs={{0,32},{2,34},{4,36},{6,38},{8,40},{10,42},{12,44},{14,46},{16,48}... | collective-permute-start | bytes 786440 | tf_op jit(solution)/shard_map/ppermute | solution.py:355
  4.3 7.4 %collective-permute-start.2 = (bf16[128,256]{1,0:T(8,128)(2,1)}, bf16[128,256]{1,0:T(8,128)(2,1)S(1)}, u32[]{:S(2)}, u32[]{:S(2)}) collective-permute-start(bf16[128,256]{1,0:T(8,128)(2,1)} %get-tuple-element.62), channel_id=1, source_target_pairs={{0,192},{2,194},{4,196},{6,198},{8,200},{10,202},{12,204},{14,206}... | collective-permute-start | bytes 196616 | tf_op jit(solution)/shard_map/ppermute | solution.py:356
  8.8 6.3 %collective-permute-start.1 = (bf16[128,256]{1,0:T(8,128)(2,1)}, bf16[128,256]{1,0:T(8,128)(2,1)S(1)}, u32[]{:S(2)}, u32[]{:S(2)}) collective-permute-start(bf16[128,256]{1,0:T(8,128)(2,1)} %get-tuple-element.62), channel_id=1, source_target_pairs={{0,64},{2,66},{4,68},{6,70},{8,72},{10,74},{12,76},{14,78},{16,80}... | collective-permute-start | bytes 196616 | tf_op jit(solution)/shard_map/ppermute | solution.py:356
  15.1 15.3 %collective-permute-start.4 = (bf16[256,1024]{1,0:T(8,128)(2,1)S(1)}, bf16[256,1024]{1,0:T(8,128)(2,1)S(1)}, u32[]{:S(2)}, u32[]{:S(2)}) collective-permute-start(bf16[256,1024]{1,0:T(8,128)(2,1)S(1)} %constant_dynamic-update-slice_fusion), channel_id=1, source_target_pairs={{0,6},{2,4},{4,2},{6,0},{8,14},{10,12},{12,10},{14,8},{16,22},{18,... | collective-permute-start | bytes 1572872 | tf_op jit(solution)/shard_map/ppermute | solution.py:359
  18.2 14.2 %collective-permute-start.3 = (bf16[256,1024]{1,0:T(8,128)(2,1)S(1)}, bf16[256,1024]{1,0:T(8,128)(2,1)S(1)}, u32[]{:S(2)}, u32[]{:S(2)}) collective-permute-start(bf16[256,1024]{1,0:T(8,128)(2,1)S(1)} %constant_dynamic-update-slice_fusion), channel_id=1, source_target_pairs={{0,2},{2,0},{4,6},{6,4},{8,10},{10,8},{12,14},{14,12},{16,18},{18,... | collective-permute-start | bytes 1572872 | tf_op jit(solution)/shard_map/ppermute | solution.py:359
  19.2 7.1 %collective-permute-start.7 = (bf16[128,256]{1,0:T(8,128)(2,1)S(1)}, bf16[128,256]{1,0:T(8,128)(2,1)S(1)}, u32[]{:S(2)}, u32[]{:S(2)}) collective-permute-start(bf16[128,256]{1,0:T(8,128)(2,1)S(1)} %collective-permute-done.1), channel_id=1, source_target_pairs={{0,192},{2,194},{4,196},{6,198},{8,200},{10,202},{12,204},{14,206}... | collective-permute-start | bytes 196616 | tf_op jit(solution)/shard_map/ppermute | solution.py:360
  26.3 10.8 %collective-permute-start.10 = (bf16[512,256]{1,0:T(8,128)(2,1)S(1)}, bf16[512,256]{1,0:T(8,128)(2,1)S(1)}, u32[]{:S(2)}, u32[]{:S(2)}) collective-permute-start(bf16[512,256]{1,0:T(8,128)(2,1)S(1)} %constant_dynamic-update-slice_fusion.2.refs_6_), channel_id=1, source_target_pairs={{0,24},{2,26},{4,28},{6,30},{8,16},{10,18},{12,20},{14,22},{16,8},... | collective-permute-start | bytes 786440 | tf_op jit(solution)/shard_map/ppermute | solution.py:361
  29.0 9.0 %collective-permute-start.9 = (bf16[512,256]{1,0:T(8,128)(2,1)S(1)}, bf16[512,256]{1,0:T(8,128)(2,1)S(1)}, u32[]{:S(2)}, u32[]{:S(2)}) collective-permute-start(bf16[512,256]{1,0:T(8,128)(2,1)S(1)} %constant_dynamic-update-slice_fusion.2.refs_6_), channel_id=1, source_target_pairs={{0,8},{2,10},{4,12},{6,14},{8,0},{10,2},{12,4},{14,6},{16,24},{18,... | collective-permute-start | bytes 786440 | tf_op jit(solution)/shard_map/ppermute | solution.py:361
  29.8 8.8 %collective-permute-start.8 = (bf16[512,256]{1,0:T(8,128)(2,1)S(1)}, bf16[512,256]{1,0:T(8,128)(2,1)S(1)}, u32[]{:S(2)}, u32[]{:S(2)}) collective-permute-start(bf16[512,256]{1,0:T(8,128)(2,1)S(1)} %constant_dynamic-update-slice_fusion.2.refs_6_), channel_id=1, source_target_pairs={{0,16},{2,18},{4,20},{6,22},{8,24},{10,26},{12,28},{14,30},{16,0},... | collective-permute-start | bytes 786440 | tf_op jit(solution)/shard_map/ppermute | solution.py:361
  30.4 8.3 %collective-permute-start.5 = (bf16[128,1024]{1,0:T(8,128)(2,1)S(1)}, bf16[128,1024]{1,0:T(8,128)(2,1)S(1)}, u32[]{:S(2)}, u32[]{:S(2)}) collective-permute-start(bf16[128,1024]{1,0:T(8,128)(2,1)S(1)} %slice.138), channel_id=1, source_target_pairs={{0,2},{2,0},{4,6},{6,4},{8,10},{10,8},{12,14},{14,12},{16,18},{18,... | collective-permute-start | bytes 786440 | tf_op jit(solution)/shard_map/ppermute | solution.py:362
  33.1 7.8 %collective-permute-start.6 = (bf16[128,1024]{1,0:T(8,128)(2,1)}, bf16[128,1024]{1,0:T(8,128)(2,1)S(1)}, u32[]{:S(2)}, u32[]{:S(2)}) collective-permute-start(bf16[128,1024]{1,0:T(8,128)(2,1)} %slice.139), channel_id=1, source_target_pairs={{0,6},{2,4},{4,2},{6,0},{8,14},{10,12},{12,10},{14,8},{16,22},{18,... | collective-permute-start | bytes 786440 | tf_op jit(solution)/shard_map/ppermute | solution.py:362
  50.8 6.4 %collective-permute-start.14 = (f32[2,12,512]{2,1,0:T(8,128)S(1)}, f32[2,12,512]{2,1,0:T(8,128)S(1)}, u32[]{:S(2)}, u32[]{:S(2)}) collective-permute-start(f32[2,12,512]{2,1,0:T(8,128)S(1)} %pad_maximum_fusion.2.refs_0_), channel_id=1, source_target_pairs={{0,6},{2,4},{4,2},{6,0},{8,14},{10,12},{12,10},{14,8},{16,22},{18,... | collective-permute-start | bytes 147464 | tf_op jit(solution)/shard_map/ppermute | solution.py:385
  51.1 6.2 %collective-permute-start.13 = (f32[2,12,512]{2,1,0:T(8,128)S(1)}, f32[2,12,512]{2,1,0:T(8,128)S(1)}, u32[]{:S(2)}, u32[]{:S(2)}) collective-permute-start(f32[2,12,512]{2,1,0:T(8,128)S(1)} %pad_maximum_fusion.2.refs_0_), channel_id=1, source_target_pairs={{0,4},{2,6},{4,0},{6,2},{8,12},{10,14},{12,8},{14,10},{16,20},{18,... | collective-permute-start | bytes 147464 | tf_op jit(solution)/shard_map/ppermute | solution.py:385
  59.3 21.2 %collective-permute-start.16 = (bf16[256,256]{1,0:T(8,128)(2,1)S(1)}, bf16[256,256]{1,0:T(8,128)(2,1)S(1)}, u32[]{:S(2)}, u32[]{:S(2)}) collective-permute-start(bf16[256,256]{1,0:T(8,128)(2,1)S(1)} %get-tuple-element.130), channel_id=1, source_target_pairs={{0,64},{2,66},{4,68},{6,70},{8,72},{10,74},{12,76},{14,78},{16,80}... | collective-permute-start | bytes 393224 | tf_op jit(solution)/shard_map/ppermute | solution.py:391
  64.0 16.5 %collective-permute-start.15 = (bf16[256,256]{1,0:T(8,128)(2,1)S(1)}, bf16[256,256]{1,0:T(8,128)(2,1)S(1)}, u32[]{:S(2)}, u32[]{:S(2)}) collective-permute-start(bf16[256,256]{1,0:T(8,128)(2,1)S(1)} %get-tuple-element.131), channel_id=1, source_target_pairs={{0,192},{2,194},{4,196},{6,198},{8,200},{10,202},{12,204},{14,206}... | collective-permute-start | bytes 393224 | tf_op jit(solution)/shard_map/ppermute | solution.py:391
  73.0 13.7 %collective-permute-start.17 = (bf16[2,512,128]{2,1,0:T(8,128)(2,1)S(1)}, bf16[2,512,128]{2,1,0:T(8,128)(2,1)S(1)}, u32[]{:S(2)}, u32[]{:S(2)}) collective-permute-start(bf16[2,512,128]{2,1,0:T(8,128)(2,1)S(1)} %get-tuple-element.90), channel_id=1, source_target_pairs={{0,2},{2,0},{4,6},{6,4},{8,10},{10,8},{12,14},{14,12},{16,18},{18,... | collective-permute-start | bytes 786440 | tf_op jit(solution)/shard_map/ppermute | solution.py:392
  73.0 13.7 %collective-permute-start.18 = (bf16[2,512,128]{2,1,0:T(8,128)(2,1)S(1)}, bf16[2,512,128]{2,1,0:T(8,128)(2,1)S(1)}, u32[]{:S(2)}, u32[]{:S(2)}) collective-permute-start(bf16[2,512,128]{2,1,0:T(8,128)(2,1)S(1)} %get-tuple-element.91), channel_id=1, source_target_pairs={{0,4},{2,6},{4,0},{6,2},{8,12},{10,14},{12,8},{14,10},{16,20},{18,... | collective-permute-start | bytes 786440 | tf_op jit(solution)/shard_map/ppermute | solution.py:392
  75.6 15.5 %collective-permute-start.19 = (bf16[2,512,128]{2,1,0:T(8,128)(2,1)S(1)}, bf16[2,512,128]{2,1,0:T(8,128)(2,1)S(1)}, u32[]{:S(2)}, u32[]{:S(2)}) collective-permute-start(bf16[2,512,128]{2,1,0:T(8,128)(2,1)S(1)} %get-tuple-element.92), channel_id=1, source_target_pairs={{0,6},{2,4},{4,2},{6,0},{8,14},{10,12},{12,10},{14,8},{16,22},{18,... | collective-permute-start | bytes 786440 | tf_op jit(solution)/shard_map/ppermute | solution.py:392
  80.6 14.5 %collective-permute-start.20 = (bf16[512,256]{1,0:T(8,128)(2,1)S(1)}, bf16[512,256]{1,0:T(8,128)(2,1)S(1)}, u32[]{:S(2)}, u32[]{:S(2)}) collective-permute-start(bf16[512,256]{1,0:T(8,128)(2,1)S(1)} %get-tuple-element.94), channel_id=1, source_target_pairs={{0,64},{2,66},{4,68},{6,70},{8,72},{10,74},{12,76},{14,78},{16,80}... | collective-permute-start | bytes 786440 | tf_op jit(solution)/shard_map/ppermute | solution.py:397
  80.7 14.4 %collective-permute-start.21 = (bf16[512,256]{1,0:T(8,128)(2,1)S(1)}, bf16[512,256]{1,0:T(8,128)(2,1)S(1)}, u32[]{:S(2)}, u32[]{:S(2)}) collective-permute-start(bf16[512,256]{1,0:T(8,128)(2,1)S(1)} %get-tuple-element.95), channel_id=1, source_target_pairs={{0,192},{2,194},{4,196},{6,198},{8,200},{10,202},{12,204},{14,206}... | collective-permute-start | bytes 786440 | tf_op jit(solution)/shard_map/ppermute | solution.py:397
  91.0 14.9 %collective-permute-start.25 = (bf16[2,512,128]{2,1,0:T(8,128)(2,1)S(1)}, bf16[2,512,128]{2,1,0:T(8,128)(2,1)S(1)}, u32[]{:S(2)}, u32[]{:S(2)}) collective-permute-start(bf16[2,512,128]{2,1,0:T(8,128)(2,1)S(1)} %get-tuple-element.105), channel_id=1, source_target_pairs={{0,4},{2,6},{4,0},{6,2},{8,12},{10,14},{12,8},{14,10},{16,20},{18,... | collective-permute-start | bytes 786440 | tf_op jit(solution)/shard_map/ppermute | solution.py:400
  91.0 14.9 %collective-permute-start.26 = (bf16[2,512,128]{2,1,0:T(8,128)(2,1)S(1)}, bf16[2,512,128]{2,1,0:T(8,128)(2,1)S(1)}, u32[]{:S(2)}, u32[]{:S(2)}) collective-permute-start(bf16[2,512,128]{2,1,0:T(8,128)(2,1)S(1)} %get-tuple-element.106), channel_id=1, source_target_pairs={{0,2},{2,0},{4,6},{6,4},{8,10},{10,8},{12,14},{14,12},{16,18},{18,... | collective-permute-start | bytes 786440 | tf_op jit(solution)/shard_map/ppermute | solution.py:400
  94.0 11.9 %collective-permute-start.27 = (bf16[2,512,128]{2,1,0:T(8,128)(2,1)S(1)}, bf16[2,512,128]{2,1,0:T(8,128)(2,1)S(1)}, u32[]{:S(2)}, u32[]{:S(2)}) collective-permute-start(bf16[2,512,128]{2,1,0:T(8,128)(2,1)S(1)} %get-tuple-element.107), channel_id=1, source_target_pairs={{0,6},{2,4},{4,2},{6,0},{8,14},{10,12},{12,10},{14,8},{16,22},{18,... | collective-permute-start | bytes 786440 | tf_op jit(solution)/shard_map/ppermute | solution.py:400
  95.3 6.3 %collective-permute-start.24 = (bf16[128,256]{1,0:T(8,128)(2,1)S(1)}, bf16[128,256]{1,0:T(8,128)(2,1)S(1)}, u32[]{:S(2)}, u32[]{:S(2)}) collective-permute-start(bf16[128,256]{1,0:T(8,128)(2,1)S(1)} %get-tuple-element.126), channel_id=1, source_target_pairs={{0,24},{2,26},{4,28},{6,30},{8,16},{10,18},{12,20},{14,22},{16,8},... | collective-permute-start | bytes 196616 | tf_op jit(solution)/shard_map/ppermute | solution.py:404
  (8 other events, 100.9 us)

commit v8 on v7

--- a/solution.py
+++ b/solution.py
@@ -358,7 +358,8 @@
     both = jnp.concatenate([row_home, row_other], axis=0)
     near, last = send(both, perm=Y[1]), send(both, perm=Y[3])
     held = jnp.concatenate([key_home, a, b, send(a, perm=REST)], axis=0)
-    keys = [held] + [send(held, perm=X[n]) for n in range(1, 4)]
+    one, three, two = (send(held, perm=X[n]) for n in (1, 3, 2))
+    keys = [held, one, two, three]
     far_own, far_other = send(last[:CHUNK], perm=Y[1]), send(near[CHUNK:], perm=Y[3])
     rows = [row_home, row_other, near, last, far_own, far_other]
 
@@ -382,7 +383,8 @@
         ],
         axis=1,
     )
-    stats = [merged] + [send(merged, perm=Y[s]) for s in range(1, SLOTS)]
+    one, three, two = (send(merged, perm=Y[s]) for s in (1, 3, 2))
+    stats = [merged, one, two, three]
 
     back = functools.partial(run_backward, group, width)
     out = back((3, 4), True, False, sc, held, *stats, stat, values)

time: 113 us -> 113 us (level)
  waiting for transfers between devices: 33.8 us -> 30.9 us
  starting transfers between devices: 58.4 us -> 60.3 us
    ppermute x3, waiting for transfers between devices: 4.35 us -> 0.67 us  [local(): mixed = [mixed[0]] + [send(mixed[s], perm=Y[s]) for s in range(1, SLOTS)]]
    ppermute x2, starting transfers between devices: 13.6 us -> 10.8 us  [local(): one, two = (send(far[0], perm=NEAR), send(far[1], perm=REST))]
    ppermute x2, starting transfers between devices: 3.33 us -> 4.83 us  [local(): ga, gb = (send(ga, perm=NEAR), send(gb, perm=REST))]
    ppermute x3, starting transfers between devices: 4.71 us -> 6.18 us  [local(): grad = [grad[0]] + [send(grad[n], perm=X[n]) for n in range(1, 4)]]
    ppermute x1, starting transfers between devices: 1.99 us -> 3.2 us  [local(): other = send(stat, perm=NEXT)[::-1]]
where the time goes in v8:
time: 113 us; the launch traced here: 111 us
  starting transfers between devices  60.3 us (53%)
  waiting for transfers between devices  30.9 us (27%)
  Pallas kernels  14.7 us (13%)
  local copies, waits for them, and re-layouts  3.4 us (3%)
    ppermute x2, starting transfers between devices, local(): one, two = (send(far[0], perm=NEAR), send(far[1], perm=REST))  10.8 us
    pallas_call x3, Pallas kernels, run_backward(): pl.pallas_call(functools.partial(backward, group, width, span, begins, en...  6.69 us
    ppermute x3, waiting for transfers between devices, local(): grad = [grad[0]] + [send(grad[n], perm=X[n]) for n in range(1, 4)]  6.6 us
    ppermute x3, starting transfers between devices, local(): grad = [grad[0]] + [send(grad[n], perm=X[n]) for n in range(1, 4)]  6.18 us
    ppermute x2, starting transfers between devices, local(): a, b = (send(key_home, perm=NEAR), send(key_home, perm=REST))  6.02 us
    pallas_call x1, Pallas kernels, run_forward(): pl.pallas_call(functools.partial(forward, group, width), out_shape=[jax.S...  5.44 us
    ppermute x3, waiting for transfers between devices, local(): one, three, two = (send(held, perm=X[n]) for n in (1, 3, 2))  4.92 us
    ppermute x2, starting transfers between devices, local(): ga, gb = (send(ga, perm=NEAR), send(gb, perm=REST))  4.83 us
  transfers between devices with their start and end apart: 30, of which 16 were waited for; matrix products, arithmetic and copies ran while one was open for 4% of the time, Pallas kernels for 5%

profile of v8, /device:TPU:32, one launch (start us, length us, event | category | flops | bytes accessed | tf_op | source)
XLA Modules:
  0.0 111.0 jit_solution(16908054421655842106)
XLA Ops:
  4.3 4.6 %collective-permute-start.2 = (bf16[128,256]{1,0:T(8,128)(2,1)}, bf16[128,256]{1,0:T(8,128)(2,1)S(1)}, u32[]{:S(2)}, u32[]{:S(2)}) collective-permute-start(bf16[128,256]{1,0:T(8,128)(2,1)} %get-tuple-element.62), channel_id=1, source_target_pairs={{0,192},{2,194},{4,196},{6,198},{8,200},{10,202},{12,204},{14,206}... | collective-permute-start | bytes 196616 | tf_op jit(solution)/shard_map/ppermute | solution.py:356
  11.7 3.4 %collective-permute-done.1 = bf16[128,256]{1,0:T(8,128)(2,1)S(1)} collective-permute-done((bf16[128,256]{1,0:T(8,128)(2,1)}, bf16[128,256]{1,0:T(8,128)(2,1)S(1)}, u32[]{:S(2)}, u32[]{:S(2)}) %collective-permute-start.1) | collective-permute-done | bytes 65568 | tf_op jit(solution)/shard_map/ppermute | solution.py:356
  15.1 3.1 %collective-permute-start.4 = (bf16[256,1024]{1,0:T(8,128)(2,1)S(1)}, bf16[256,1024]{1,0:T(8,128)(2,1)S(1)}, u32[]{:S(2)}, u32[]{:S(2)}) collective-permute-start(bf16[256,1024]{1,0:T(8,128)(2,1)S(1)} %constant_dynamic-update-slice_fusion), channel_id=1, source_target_pairs={{0,6},{2,4},{4,2},{6,0},{8,14},{10,12},{12,10},{14,8},{16,22},{18,... | collective-permute-start | bytes 1572872 | tf_op jit(solution)/shard_map/ppermute | solution.py:359
  19.2 3.1 %collective-permute-start.7 = (bf16[128,256]{1,0:T(8,128)(2,1)S(1)}, bf16[128,256]{1,0:T(8,128)(2,1)S(1)}, u32[]{:S(2)}, u32[]{:S(2)}) collective-permute-start(bf16[128,256]{1,0:T(8,128)(2,1)S(1)} %collective-permute-done.1), channel_id=1, source_target_pairs={{0,192},{2,194},{4,196},{6,198},{8,200},{10,202},{12,204},{14,206}... | collective-permute-start | bytes 196616 | tf_op jit(solution)/shard_map/ppermute | solution.py:360
  22.3 4.0 %collective-permute-done.7 = bf16[128,256]{1,0:T(8,128)(2,1)S(1)} collective-permute-done((bf16[128,256]{1,0:T(8,128)(2,1)S(1)}, bf16[128,256]{1,0:T(8,128)(2,1)S(1)}, u32[]{:S(2)}, u32[]{:S(2)}) %collective-permute-start.7) | collective-permute-done | bytes 65568 | tf_op jit(solution)/shard_map/ppermute | solution.py:360
  26.3 2.8 %collective-permute-start.10 = (bf16[512,256]{1,0:T(8,128)(2,1)S(1)}, bf16[512,256]{1,0:T(8,128)(2,1)S(1)}, u32[]{:S(2)}, u32[]{:S(2)}) collective-permute-start(bf16[512,256]{1,0:T(8,128)(2,1)S(1)} %constant_dynamic-update-slice_fusion.2.refs_6_), channel_id=1, source_target_pairs={{0,24},{2,26},{4,28},{6,30},{8,16},{10,18},{12,20},{14,22},{16,8},... | collective-permute-start | bytes 786440 | tf_op jit(solution)/shard_map/ppermute | solution.py:361
  33.8 3.3 %collective-permute-done.10.refs_9_ = bf16[512,256]{1,0:T(8,128)(2,1)S(1)} collective-permute-done((bf16[512,256]{1,0:T(8,128)(2,1)S(1)}, bf16[512,256]{1,0:T(8,128)(2,1)S(1)}, u32[]{:S(2)}, u32[]{:S(2)}) %collective-permute-start.10) | collective-permute-done | bytes 262176 | tf_op jit(solution)/shard_map/ppermute | solution.py:361
  38.7 2.2 %collective-permute-done.6.refs_5_ = bf16[128,1024]{1,0:T(8,128)(2,1)S(1)} collective-permute-done((bf16[128,1024]{1,0:T(8,128)(2,1)}, bf16[128,1024]{1,0:T(8,128)(2,1)S(1)}, u32[]{:S(2)}, u32[]{:S(2)}) %collective-permute-start.6) | collective-permute-done | bytes 262176 | tf_op jit(solution)/shard_map/ppermute | solution.py:363
  40.9 5.4 %forward.1 = (bf16[2,4,128,512]{3,2,1,0:T(8,128)(2,1)S(1)}, f32[2,12,512]{2,1,0:T(8,128)S(1)}, bf16[2,4,512,128]{3,2,1,0:T(8,128)(2,1)S(1)}, bf16[2,4,512,128]{3...) custom-call(s32[16]{0:T(128)S(1)} %concatenate.18.sc, ...), custom_call_target="tpu_custom_call" | custom-call | flops 12884901888 | bytes 8388608 | tf_op jit(solution)/shard_map/forward/pallas_call | solution.py:300
  46.4 3.2 %collective-permute-start.11 = (f32[2,12,512]{2,1,0:T(8,128)S(1)}, f32[2,12,512]{2,1,0:T(8,128)S(1)}, u32[]{:S(2)}, u32[]{:S(2)}) collective-permute-start(f32[2,12,512]{2,1,0:T(8,128)S(1)} %get-tuple-element.71.refs_4_), channel_id=1, source_target_pairs={{0,32},{2,34},{4,36},{6,38},{8,40},{10,42},{12,44},{14,46},{16,48}... | collective-permute-start | bytes 147464 | tf_op jit(solution)/shard_map/ppermute | solution.py:374
  49.6 2.2 %collective-permute-done.11 = f32[2,12,512]{2,1,0:T(8,128)S(1)} collective-permute-done((f32[2,12,512]{2,1,0:T(8,128)S(1)}, f32[2,12,512]{2,1,0:T(8,128)S(1)}, u32[]{:S(2)}, u32[]{:S(2)}) %collective-permute-start.11) | collective-permute-done | bytes 49184 | tf_op jit(solution)/shard_map/ppermute | solution.py:374
  53.0 3.2 %collective-permute-start.12 = (f32[2,12,512]{2,1,0:T(8,128)S(1)}, f32[2,12,512]{2,1,0:T(8,128)S(1)}, u32[]{:S(2)}, u32[]{:S(2)}) collective-permute-start(f32[2,12,512]{2,1,0:T(8,128)S(1)} %pad_maximum_fusion.2.refs_0_), channel_id=1, source_target_pairs={{0,2},{2,0},{4,6},{6,4},{8,10},{10,8},{12,14},{14,12},{16,18},{18,... | collective-permute-start | bytes 147464 | tf_op jit(solution)/shard_map/ppermute | solution.py:386
  56.2 2.1 %collective-permute-done.14.refs_3_ = f32[2,12,512]{2,1,0:T(8,128)S(1)} collective-permute-done((f32[2,12,512]{2,1,0:T(8,128)S(1)}, f32[2,12,512]{2,1,0:T(8,128)S(1)}, u32[]{:S(2)}, u32[]{:S(2)}) %collective-permute-start.14) | collective-permute-done | bytes 49184 | tf_op jit(solution)/shard_map/ppermute | solution.py:386
  60.4 3.8 %collective-permute-start.16 = (bf16[256,256]{1,0:T(8,128)(2,1)S(1)}, bf16[256,256]{1,0:T(8,128)(2,1)S(1)}, u32[]{:S(2)}, u32[]{:S(2)}) collective-permute-start(bf16[256,256]{1,0:T(8,128)(2,1)S(1)} %get-tuple-element.130), channel_id=1, source_target_pairs={{0,64},{2,66},{4,68},{6,70},{8,72},{10,74},{12,76},{14,78},{16,80}... | collective-permute-start | bytes 393224 | tf_op jit(solution)/shard_map/ppermute | solution.py:393
  64.2 7.0 %collective-permute-start.15 = (bf16[256,256]{1,0:T(8,128)(2,1)S(1)}, bf16[256,256]{1,0:T(8,128)(2,1)S(1)}, u32[]{:S(2)}, u32[]{:S(2)}) collective-permute-start(bf16[256,256]{1,0:T(8,128)(2,1)S(1)} %get-tuple-element.131), channel_id=1, source_target_pairs={{0,192},{2,194},{4,196},{6,198},{8,200},{10,202},{12,204},{14,206}... | collective-permute-start | bytes 393224 | tf_op jit(solution)/shard_map/ppermute | solution.py:393
  72.6 3.4 %collective-permute-start.19 = (bf16[2,512,128]{2,1,0:T(8,128)(2,1)S(1)}, bf16[2,512,128]{2,1,0:T(8,128)(2,1)S(1)}, u32[]{:S(2)}, u32[]{:S(2)}) collective-permute-start(bf16[2,512,128]{2,1,0:T(8,128)(2,1)S(1)} %get-tuple-element.92), channel_id=1, source_target_pairs={{0,6},{2,4},{4,2},{6,0},{8,14},{10,12},{12,10},{14,8},{16,22},{18,... | collective-permute-start | bytes 786440 | tf_op jit(solution)/shard_map/ppermute | solution.py:394
  76.0 2.8 %backward_middle.1 = (bf16[4,256,256]{2,1,0:T(8,128)(2,1)S(1)}, f32[2,4,128,512]{3,2,1,0:T(8,128)S(1)}, f32[2,4,1,512]{3,2,1,0:T(1,128)S(1)}, f32[2,4,1,512]{3,2,1,0:T(1,128)S(1)}) custom-call(s32[16]{0:T(128)S(1)} %concatenate.18.sc, bf16[2,4,512,128]{3,2,1,0:T(8,128)(2,1)S(1)} %get-tuple-element.66.q_s, ...), custom_call_target="tpu_custom_call" | custom-call | flops 10737418240 | bytes 8388608 | tf_op jit(solution)/shard_map/backward_middle/pallas_call | solution.py:324
  80.2 3.5 %collective-permute-start.21 = (bf16[512,256]{1,0:T(8,128)(2,1)S(1)}, bf16[512,256]{1,0:T(8,128)(2,1)S(1)}, u32[]{:S(2)}, u32[]{:S(2)}) collective-permute-start(bf16[512,256]{1,0:T(8,128)(2,1)S(1)} %get-tuple-element.95), channel_id=1, source_target_pairs={{0,192},{2,194},{4,196},{6,198},{8,200},{10,202},{12,204},{14,206}... | collective-permute-start | bytes 786440 | tf_op jit(solution)/shard_map/ppermute | solution.py:399
  83.8 2.7 %backward_end.1 = (bf16[2,256,256]{2,1,0:T(8,128)(2,1)S(1)}, bf16[2,512,128]{2,1,0:T(8,128)(2,1)S(1)}, bf16[2,512,128]{2,1,0:T(8,128)(2,1)S(1)}, bf16[2,512,128]...) custom-call(s32[16]{0:T(128)S(1)} %concatenate.18.sc, bf16[2,4,512,128]{3,2,1,0:T(8,128)(2,1)S(1)} %get-tuple-element.66.q_s, ...), custom_call_target="tpu_custom_call" | custom-call | flops 5368709120 | bytes 8388608 | tf_op jit(solution)/shard_map/backward_end/pallas_call | solution.py:324
  87.1 2.5 %collective-permute-start.25 = (bf16[2,512,128]{2,1,0:T(8,128)(2,1)S(1)}, bf16[2,512,128]{2,1,0:T(8,128)(2,1)S(1)}, u32[]{:S(2)}, u32[]{:S(2)}) collective-permute-start(bf16[2,512,128]{2,1,0:T(8,128)(2,1)S(1)} %get-tuple-element.105), channel_id=1, source_target_pairs={{0,4},{2,6},{4,0},{6,2},{8,12},{10,14},{12,8},{14,10},{16,20},{18,... | collective-permute-start | bytes 786440 | tf_op jit(solution)/shard_map/ppermute | solution.py:402
  89.7 2.0 %collective-permute-start.26 = (bf16[2,512,128]{2,1,0:T(8,128)(2,1)S(1)}, bf16[2,512,128]{2,1,0:T(8,128)(2,1)S(1)}, u32[]{:S(2)}, u32[]{:S(2)}) collective-permute-start(bf16[2,512,128]{2,1,0:T(8,128)(2,1)S(1)} %get-tuple-element.106), channel_id=1, source_target_pairs={{0,2},{2,0},{4,6},{6,4},{8,10},{10,8},{12,14},{14,12},{16,18},{18,... | collective-permute-start | bytes 786440 | tf_op jit(solution)/shard_map/ppermute | solution.py:402
  91.9 6.2 %collective-permute-start.24 = (bf16[128,256]{1,0:T(8,128)(2,1)S(1)}, bf16[128,256]{1,0:T(8,128)(2,1)S(1)}, u32[]{:S(2)}, u32[]{:S(2)}) collective-permute-start(bf16[128,256]{1,0:T(8,128)(2,1)S(1)} %get-tuple-element.126), channel_id=1, source_target_pairs={{0,24},{2,26},{4,28},{6,30},{8,16},{10,18},{12,20},{14,22},{16,8},... | collective-permute-start | bytes 196616 | tf_op jit(solution)/shard_map/ppermute | solution.py:406
  98.2 2.4 %collective-permute-done.24 = bf16[128,256]{1,0:T(8,128)(2,1)S(1)} collective-permute-done((bf16[128,256]{1,0:T(8,128)(2,1)S(1)}, bf16[128,256]{1,0:T(8,128)(2,1)S(1)}, u32[]{:S(2)}, u32[]{:S(2)}) %collective-permute-start.24) | collective-permute-done | bytes 65568 | tf_op jit(solution)/shard_map/ppermute | solution.py:406
  100.6 3.2 %collective-permute-done.23 = bf16[128,256]{1,0:T(8,128)(2,1)S(1)} collective-permute-done((bf16[128,256]{1,0:T(8,128)(2,1)S(1)}, bf16[128,256]{1,0:T(8,128)(2,1)S(1)}, u32[]{:S(2)}, u32[]{:S(2)}) %collective-permute-start.23) | collective-permute-done | bytes 65568 | tf_op jit(solution)/shard_map/ppermute | solution.py:406
  (71 shorter events, 28.0 us)
Async XLA Ops:
  2.4 12.7 %collective-permute-start = (bf16[128,1024]{1,0:T(8,128)(2,1)}, bf16[128,1024]{1,0:T(8,128)(2,1)S(1)}, u32[]{:S(2)}, u32[]{:S(2)}) collective-permute-start(bf16[128,1024]{1,0:T(8,128)(2,1)} %get-tuple-element.61.refs_0_), channel_id=1, source_target_pairs={{0,32},{2,34},{4,36},{6,38},{8,40},{10,42},{12,44},{14,46},{16,48}... | collective-permute-start | bytes 786440 | tf_op jit(solution)/shard_map/ppermute | solution.py:355
  4.3 7.4 %collective-permute-start.2 = (bf16[128,256]{1,0:T(8,128)(2,1)}, bf16[128,256]{1,0:T(8,128)(2,1)S(1)}, u32[]{:S(2)}, u32[]{:S(2)}) collective-permute-start(bf16[128,256]{1,0:T(8,128)(2,1)} %get-tuple-element.62), channel_id=1, source_target_pairs={{0,192},{2,194},{4,196},{6,198},{8,200},{10,202},{12,204},{14,206}... | collective-permute-start | bytes 196616 | tf_op jit(solution)/shard_map/ppermute | solution.py:356
  8.8 6.3 %collective-permute-start.1 = (bf16[128,256]{1,0:T(8,128)(2,1)}, bf16[128,256]{1,0:T(8,128)(2,1)S(1)}, u32[]{:S(2)}, u32[]{:S(2)}) collective-permute-start(bf16[128,256]{1,0:T(8,128)(2,1)} %get-tuple-element.62), channel_id=1, source_target_pairs={{0,64},{2,66},{4,68},{6,70},{8,72},{10,74},{12,76},{14,78},{16,80}... | collective-permute-start | bytes 196616 | tf_op jit(solution)/shard_map/ppermute | solution.py:356
  15.1 15.3 %collective-permute-start.4 = (bf16[256,1024]{1,0:T(8,128)(2,1)S(1)}, bf16[256,1024]{1,0:T(8,128)(2,1)S(1)}, u32[]{:S(2)}, u32[]{:S(2)}) collective-permute-start(bf16[256,1024]{1,0:T(8,128)(2,1)S(1)} %constant_dynamic-update-slice_fusion), channel_id=1, source_target_pairs={{0,6},{2,4},{4,2},{6,0},{8,14},{10,12},{12,10},{14,8},{16,22},{18,... | collective-permute-start | bytes 1572872 | tf_op jit(solution)/shard_map/ppermute | solution.py:359
  18.2 14.2 %collective-permute-start.3 = (bf16[256,1024]{1,0:T(8,128)(2,1)S(1)}, bf16[256,1024]{1,0:T(8,128)(2,1)S(1)}, u32[]{:S(2)}, u32[]{:S(2)}) collective-permute-start(bf16[256,1024]{1,0:T(8,128)(2,1)S(1)} %constant_dynamic-update-slice_fusion), channel_id=1, source_target_pairs={{0,2},{2,0},{4,6},{6,4},{8,10},{10,8},{12,14},{14,12},{16,18},{18,... | collective-permute-start | bytes 1572872 | tf_op jit(solution)/shard_map/ppermute | solution.py:359
  19.2 7.1 %collective-permute-start.7 = (bf16[128,256]{1,0:T(8,128)(2,1)S(1)}, bf16[128,256]{1,0:T(8,128)(2,1)S(1)}, u32[]{:S(2)}, u32[]{:S(2)}) collective-permute-start(bf16[128,256]{1,0:T(8,128)(2,1)S(1)} %collective-permute-done.1), channel_id=1, source_target_pairs={{0,192},{2,194},{4,196},{6,198},{8,200},{10,202},{12,204},{14,206}... | collective-permute-start | bytes 196616 | tf_op jit(solution)/shard_map/ppermute | solution.py:360
  26.3 10.8 %collective-permute-start.10 = (bf16[512,256]{1,0:T(8,128)(2,1)S(1)}, bf16[512,256]{1,0:T(8,128)(2,1)S(1)}, u32[]{:S(2)}, u32[]{:S(2)}) collective-permute-start(bf16[512,256]{1,0:T(8,128)(2,1)S(1)} %constant_dynamic-update-slice_fusion.2.refs_6_), channel_id=1, source_target_pairs={{0,24},{2,26},{4,28},{6,30},{8,16},{10,18},{12,20},{14,22},{16,8},... | collective-permute-start | bytes 786440 | tf_op jit(solution)/shard_map/ppermute | solution.py:361
  29.0 9.0 %collective-permute-start.9 = (bf16[512,256]{1,0:T(8,128)(2,1)S(1)}, bf16[512,256]{1,0:T(8,128)(2,1)S(1)}, u32[]{:S(2)}, u32[]{:S(2)}) collective-permute-start(bf16[512,256]{1,0:T(8,128)(2,1)S(1)} %constant_dynamic-update-slice_fusion.2.refs_6_), channel_id=1, source_target_pairs={{0,8},{2,10},{4,12},{6,14},{8,0},{10,2},{12,4},{14,6},{16,24},{18,... | collective-permute-start | bytes 786440 | tf_op jit(solution)/shard_map/ppermute | solution.py:361
  29.8 8.8 %collective-permute-start.8 = (bf16[512,256]{1,0:T(8,128)(2,1)S(1)}, bf16[512,256]{1,0:T(8,128)(2,1)S(1)}, u32[]{:S(2)}, u32[]{:S(2)}) collective-permute-start(bf16[512,256]{1,0:T(8,128)(2,1)S(1)} %constant_dynamic-update-slice_fusion.2.refs_6_), channel_id=1, source_target_pairs={{0,16},{2,18},{4,20},{6,22},{8,24},{10,26},{12,28},{14,30},{16,0},... | collective-permute-start | bytes 786440 | tf_op jit(solution)/shard_map/ppermute | solution.py:361
  30.4 8.3 %collective-permute-start.5 = (bf16[128,1024]{1,0:T(8,128)(2,1)S(1)}, bf16[128,1024]{1,0:T(8,128)(2,1)S(1)}, u32[]{:S(2)}, u32[]{:S(2)}) collective-permute-start(bf16[128,1024]{1,0:T(8,128)(2,1)S(1)} %slice.138), channel_id=1, source_target_pairs={{0,2},{2,0},{4,6},{6,4},{8,10},{10,8},{12,14},{14,12},{16,18},{18,... | collective-permute-start | bytes 786440 | tf_op jit(solution)/shard_map/ppermute | solution.py:363
  33.1 7.8 %collective-permute-start.6 = (bf16[128,1024]{1,0:T(8,128)(2,1)}, bf16[128,1024]{1,0:T(8,128)(2,1)S(1)}, u32[]{:S(2)}, u32[]{:S(2)}) collective-permute-start(bf16[128,1024]{1,0:T(8,128)(2,1)} %slice.139), channel_id=1, source_target_pairs={{0,6},{2,4},{4,2},{6,0},{8,14},{10,12},{12,10},{14,8},{16,22},{18,... | collective-permute-start | bytes 786440 | tf_op jit(solution)/shard_map/ppermute | solution.py:363
  51.9 6.4 %collective-permute-start.14 = (f32[2,12,512]{2,1,0:T(8,128)S(1)}, f32[2,12,512]{2,1,0:T(8,128)S(1)}, u32[]{:S(2)}, u32[]{:S(2)}) collective-permute-start(f32[2,12,512]{2,1,0:T(8,128)S(1)} %pad_maximum_fusion.2.refs_0_), channel_id=1, source_target_pairs={{0,6},{2,4},{4,2},{6,0},{8,14},{10,12},{12,10},{14,8},{16,22},{18,... | collective-permute-start | bytes 147464 | tf_op jit(solution)/shard_map/ppermute | solution.py:386
  52.2 6.2 %collective-permute-start.13 = (f32[2,12,512]{2,1,0:T(8,128)S(1)}, f32[2,12,512]{2,1,0:T(8,128)S(1)}, u32[]{:S(2)}, u32[]{:S(2)}) collective-permute-start(f32[2,12,512]{2,1,0:T(8,128)S(1)} %pad_maximum_fusion.2.refs_0_), channel_id=1, source_target_pairs={{0,4},{2,6},{4,0},{6,2},{8,12},{10,14},{12,8},{14,10},{16,20},{18,... | collective-permute-start | bytes 147464 | tf_op jit(solution)/shard_map/ppermute | solution.py:386
  60.4 18.4 %collective-permute-start.16 = (bf16[256,256]{1,0:T(8,128)(2,1)S(1)}, bf16[256,256]{1,0:T(8,128)(2,1)S(1)}, u32[]{:S(2)}, u32[]{:S(2)}) collective-permute-start(bf16[256,256]{1,0:T(8,128)(2,1)S(1)} %get-tuple-element.130), channel_id=1, source_target_pairs={{0,64},{2,66},{4,68},{6,70},{8,72},{10,74},{12,76},{14,78},{16,80}... | collective-permute-start | bytes 393224 | tf_op jit(solution)/shard_map/ppermute | solution.py:393
  64.2 14.6 %collective-permute-start.15 = (bf16[256,256]{1,0:T(8,128)(2,1)S(1)}, bf16[256,256]{1,0:T(8,128)(2,1)S(1)}, u32[]{:S(2)}, u32[]{:S(2)}) collective-permute-start(bf16[256,256]{1,0:T(8,128)(2,1)S(1)} %get-tuple-element.131), channel_id=1, source_target_pairs={{0,192},{2,194},{4,196},{6,198},{8,200},{10,202},{12,204},{14,206}... | collective-permute-start | bytes 393224 | tf_op jit(solution)/shard_map/ppermute | solution.py:393
  71.3 15.2 %collective-permute-start.17 = (bf16[2,512,128]{2,1,0:T(8,128)(2,1)S(1)}, bf16[2,512,128]{2,1,0:T(8,128)(2,1)S(1)}, u32[]{:S(2)}, u32[]{:S(2)}) collective-permute-start(bf16[2,512,128]{2,1,0:T(8,128)(2,1)S(1)} %get-tuple-element.90), channel_id=1, source_target_pairs={{0,2},{2,0},{4,6},{6,4},{8,10},{10,8},{12,14},{14,12},{16,18},{18,... | collective-permute-start | bytes 786440 | tf_op jit(solution)/shard_map/ppermute | solution.py:394
  72.6 13.9 %collective-permute-start.18 = (bf16[2,512,128]{2,1,0:T(8,128)(2,1)S(1)}, bf16[2,512,128]{2,1,0:T(8,128)(2,1)S(1)}, u32[]{:S(2)}, u32[]{:S(2)}) collective-permute-start(bf16[2,512,128]{2,1,0:T(8,128)(2,1)S(1)} %get-tuple-element.91), channel_id=1, source_target_pairs={{0,4},{2,6},{4,0},{6,2},{8,12},{10,14},{12,8},{14,10},{16,20},{18,... | collective-permute-start | bytes 786440 | tf_op jit(solution)/shard_map/ppermute | solution.py:394
  72.6 14.6 %collective-permute-start.19 = (bf16[2,512,128]{2,1,0:T(8,128)(2,1)S(1)}, bf16[2,512,128]{2,1,0:T(8,128)(2,1)S(1)}, u32[]{:S(2)}, u32[]{:S(2)}) collective-permute-start(bf16[2,512,128]{2,1,0:T(8,128)(2,1)S(1)} %get-tuple-element.92), channel_id=1, source_target_pairs={{0,6},{2,4},{4,2},{6,0},{8,14},{10,12},{12,10},{14,8},{16,22},{18,... | collective-permute-start | bytes 786440 | tf_op jit(solution)/shard_map/ppermute | solution.py:394
  78.9 12.8 %collective-permute-start.20 = (bf16[512,256]{1,0:T(8,128)(2,1)S(1)}, bf16[512,256]{1,0:T(8,128)(2,1)S(1)}, u32[]{:S(2)}, u32[]{:S(2)}) collective-permute-start(bf16[512,256]{1,0:T(8,128)(2,1)S(1)} %get-tuple-element.94), channel_id=1, source_target_pairs={{0,64},{2,66},{4,68},{6,70},{8,72},{10,74},{12,76},{14,78},{16,80}... | collective-permute-start | bytes 786440 | tf_op jit(solution)/shard_map/ppermute | solution.py:399
  80.2 11.5 %collective-permute-start.21 = (bf16[512,256]{1,0:T(8,128)(2,1)S(1)}, bf16[512,256]{1,0:T(8,128)(2,1)S(1)}, u32[]{:S(2)}, u32[]{:S(2)}) collective-permute-start(bf16[512,256]{1,0:T(8,128)(2,1)S(1)} %get-tuple-element.95), channel_id=1, source_target_pairs={{0,192},{2,194},{4,196},{6,198},{8,200},{10,202},{12,204},{14,206}... | collective-permute-start | bytes 786440 | tf_op jit(solution)/shard_map/ppermute | solution.py:399
  87.1 17.7 %collective-permute-start.25 = (bf16[2,512,128]{2,1,0:T(8,128)(2,1)S(1)}, bf16[2,512,128]{2,1,0:T(8,128)(2,1)S(1)}, u32[]{:S(2)}, u32[]{:S(2)}) collective-permute-start(bf16[2,512,128]{2,1,0:T(8,128)(2,1)S(1)} %get-tuple-element.105), channel_id=1, source_target_pairs={{0,4},{2,6},{4,0},{6,2},{8,12},{10,14},{12,8},{14,10},{16,20},{18,... | collective-permute-start | bytes 786440 | tf_op jit(solution)/shard_map/ppermute | solution.py:402
  89.7 15.2 %collective-permute-start.26 = (bf16[2,512,128]{2,1,0:T(8,128)(2,1)S(1)}, bf16[2,512,128]{2,1,0:T(8,128)(2,1)S(1)}, u32[]{:S(2)}, u32[]{:S(2)}) collective-permute-start(bf16[2,512,128]{2,1,0:T(8,128)(2,1)S(1)} %get-tuple-element.106), channel_id=1, source_target_pairs={{0,2},{2,0},{4,6},{6,4},{8,10},{10,8},{12,14},{14,12},{16,18},{18,... | collective-permute-start | bytes 786440 | tf_op jit(solution)/shard_map/ppermute | solution.py:402
  91.7 13.1 %collective-permute-start.27 = (bf16[2,512,128]{2,1,0:T(8,128)(2,1)S(1)}, bf16[2,512,128]{2,1,0:T(8,128)(2,1)S(1)}, u32[]{:S(2)}, u32[]{:S(2)}) collective-permute-start(bf16[2,512,128]{2,1,0:T(8,128)(2,1)S(1)} %get-tuple-element.107), channel_id=1, source_target_pairs={{0,6},{2,4},{4,2},{6,0},{8,14},{10,12},{12,10},{14,8},{16,22},{18,... | collective-permute-start | bytes 786440 | tf_op jit(solution)/shard_map/ppermute | solution.py:402
  91.9 8.7 %collective-permute-start.24 = (bf16[128,256]{1,0:T(8,128)(2,1)S(1)}, bf16[128,256]{1,0:T(8,128)(2,1)S(1)}, u32[]{:S(2)}, u32[]{:S(2)}) collective-permute-start(bf16[128,256]{1,0:T(8,128)(2,1)S(1)} %get-tuple-element.126), channel_id=1, source_target_pairs={{0,24},{2,26},{4,28},{6,30},{8,16},{10,18},{12,20},{14,22},{16,8},... | collective-permute-start | bytes 196616 | tf_op jit(solution)/shard_map/ppermute | solution.py:406
  (8 other events, 103.0 us)
